TPU v7x, 32 devices: a whole 2x2x4 slice. The times are simulated.
32 devices in a mesh: img: 8 (over z, x), rep: 4 (over y, core).
Axes of the slice: x: 2, y: 2, z: 4, core: 2. Of those that a mesh axis runs over, the one named last changes fastest.
Arguments:
- pair_images: int32 [96, 2], P('img'), may hold values from 0 to 63, as said below
- depths: float32 [64, 147456], P('img', 'rep'), may hold values from 0.5 to 4
- depth_moment: float32 [64, 147456], P('img', 'rep'), may hold values from -8 to 8
- depth_second: float32 [64, 147456], P('img', 'rep'), may hold values from 1 to 100
- cameras: float32 [64, 7], P('img'), may hold values from -0.5 to 0.5
- camera_moment: float32 [64, 7], P('img'), may hold values from -8 to 8
- camera_second: float32 [64, 7], P('img'), may hold values from 1 to 100
- pair_poses: float32 [96, 7], P('img'), may hold values from -0.5 to 0.5
- pair_moment: float32 [96, 7], P('img'), may hold values from -8 to 8
- pair_second: float32 [96, 7], P('img'), may hold values from 1 to 100
- pointmaps: bfloat16 [96, 2, 3, 147456], P('img', None, None, 'rep'), may hold values from -6 to 6
- confidence: bfloat16 [96, 2, 147456], P('img', None, 'rep'), may hold values from 1 to 10
Outputs:
- new_depths: float32 [64, 147456], P('img', 'rep')
- new_depth_moment: float32 [64, 147456], P('img', 'rep')
- new_depth_second: float32 [64, 147456], P('img', 'rep')
- new_cameras: float32 [64, 7], P('img')
- new_camera_moment: float32 [64, 7], P('img')
- new_camera_second: float32 [64, 7], P('img')
- new_pair_poses: float32 [96, 7], P('img')
- new_pair_moment: float32 [96, 7], P('img')
- new_pair_second: float32 [96, 7], P('img')
Inputs may be any that keep to these rules, and one draw needn't show every extreme that they name: `pair_images`: the two images of a pair differ. Counting both views, the pairs stored on one index of img name the images of any one index of img (images k * 8 to k * 8 + 7) at most 4 times; one index of img, the same for all, is named exactly 4 times by the pairs of every index.
All inputs are finite; a program needn't handle non-finite values.
Results may differ from a plain program's by a relative error of at most 0.0003.
Values may be sent and summed in bfloat16 or wider, within the bound.
No kernel may reach another device: no remote copies, remote signals or barrier semaphores. Data moves between devices by JAX's collectives and lax.ppermute only.
A program may use at most 128 MiB of HBM per device.

v0:
```python
import jax
import jax.numpy as jnp
from jax import lax
from jax.sharding import PartitionSpec as P

HEIGHT = 288
WIDTH = 512
START = 50
NPIX = 147456


beta_one = 0.9
beta_two = 0.999
adam_eps = 1e-08
depth_rate = 0.05
camera_rate = 0.01
pose_rate = 0.01


def rotation(first, middle, last):
    inverse = 1.0 / (1.0 + first * first + middle * middle + last * last)
    return (
        (1.0 + first * first - middle * middle - last * last) * inverse,
        2.0 * (first * middle - last) * inverse,
        2.0 * (first * last + middle) * inverse,
        2.0 * (first * middle + last) * inverse,
        (1.0 - first * first + middle * middle - last * last) * inverse,
        2.0 * (middle * last - first) * inverse,
        2.0 * (first * last - middle) * inverse,
        2.0 * (middle * last + first) * inverse,
        (1.0 - first * first - middle * middle + last * last) * inverse,
    )


def view_loss(depth_rows, camera_rows, pose_rows, points, weights, pixel_rows, pixel_cols):
    focals = WIDTH * jnp.exp(camera_rows[:, 0:1])
    ray_x = (pixel_cols[None, :] - 0.5 * WIDTH) / focals
    ray_y = (pixel_rows[None, :] - 0.5 * HEIGHT) / focals
    cam_rot = rotation(camera_rows[:, 1:2], camera_rows[:, 2:3], camera_rows[:, 3:4])
    pose_rot = rotation(pose_rows[:, 0:1], pose_rows[:, 1:2], pose_rows[:, 2:3])
    scales = jnp.exp(pose_rows[:, 6:7])
    point_x = points[:, 0].astype(jnp.float32)
    point_y = points[:, 1].astype(jnp.float32)
    point_z = points[:, 2].astype(jnp.float32)
    squared = jnp.zeros_like(depth_rows)
    for k in range(3):
        world_pts = (
            depth_rows * (cam_rot[3 * k] * ray_x + cam_rot[3 * k + 1] * ray_y + cam_rot[3 * k + 2])
            + camera_rows[:, 4 + k : 5 + k]
        )
        target = (
            scales
            * (
                pose_rot[3 * k] * point_x
                + pose_rot[3 * k + 1] * point_y
                + pose_rot[3 * k + 2] * point_z
            )
            + pose_rows[:, 3 + k : 4 + k]
        )
        offset = world_pts - target
        squared = squared + offset * offset
    return 0.5 * jnp.sum(weights.astype(jnp.float32) * squared)


def adam_step(values, moment, second, gradient, step_rate, step_count):
    moment = beta_one * moment + (1.0 - beta_one) * gradient
    second = beta_two * second + (1.0 - beta_two) * gradient * gradient
    fix_one = 1.0 - beta_one**step_count
    fix_two = 1.0 - beta_two**step_count
    values = values - step_rate * (moment / fix_one) / (jnp.sqrt(second / fix_two) + adam_eps)
    return (values, moment, second)


def body(
    pair_images,
    depths,
    depth_moment,
    depth_second,
    cameras,
    camera_moment,
    camera_second,
    pair_poses,
    pair_moment,
    pair_second,
    pointmaps,
    confidence,
):
    shards = lax.axis_size("img")
    own_index = lax.axis_index("img")
    local_images = depths.shape[0]
    row_len = depths.shape[1]
    local_pairs = pair_images.shape[0]
    requests = 2 * local_pairs
    capacity = max(2, 3 * local_pairs // shards)
    slot_total = shards * capacity
    pixel = lax.axis_index("rep") * row_len + jnp.arange(row_len, dtype=jnp.int32)
    pixel_rows = (pixel // WIDTH).astype(jnp.float32) + 0.5
    pixel_cols = (pixel % WIDTH).astype(jnp.float32) + 0.5
    listing = lax.all_gather(pair_images, "img", axis=0, tiled=True).reshape(shards, requests)
    owners = listing // local_images
    request_ids = jnp.arange(requests, dtype=jnp.int32)
    earlier = request_ids[None, :] < request_ids[:, None]
    same_owner = owners[:, :, None] == owners[:, None, :]
    ranks = jnp.sum(same_owner & earlier[None, :, :], axis=2)
    slot_ids = jnp.arange(capacity, dtype=jnp.int32)
    hits = (owners[:, :, None] == own_index) & (ranks[:, :, None] == slot_ids[None, None, :])
    slot_image = jnp.sum(jnp.where(hits, (listing % local_images)[:, :, None], 0), axis=1).reshape(
        slot_total
    )
    slot_live = jnp.any(hits, axis=1).reshape(slot_total)
    my_owner = lax.dynamic_index_in_dim(owners, own_index, 0, keepdims=False)
    my_ranks = lax.dynamic_index_in_dim(ranks, own_index, 0, keepdims=False)
    my_slots = my_owner * capacity + my_ranks
    sent_hits = my_slots[:, None] == jnp.arange(slot_total, dtype=jnp.int32)[None, :]
    slot_request = jnp.sum(jnp.where(sent_hits, request_ids[:, None], 0), axis=0)
    slot_sent = jnp.any(sent_hits, axis=0)
    folding = (
        (slot_image[None, :] == jnp.arange(local_images, dtype=jnp.int32)[:, None])
        & slot_live[None, :]
    ).astype(jnp.float32)
    points = pointmaps.reshape(requests, 3, row_len)
    weights = confidence.reshape(requests, row_len)

    def gradients(depth_rows, camera_rows, pose_rows, point_rows, weight_rows):
        loss, pullback = jax.vjp(
            lambda a, b, c: view_loss(a, b, c, point_rows, weight_rows, pixel_rows, pixel_cols),
            depth_rows,
            camera_rows,
            pose_rows,
        )
        return pullback(jnp.ones_like(loss))

    pose_rows = jnp.repeat(pair_poses, 2, axis=0)
    out_depth = jnp.where(slot_live[:, None], jnp.take(depths, slot_image, axis=0), 0.0).reshape(
        shards, capacity, row_len
    )
    out_camera = jnp.where(slot_live[:, None], jnp.take(cameras, slot_image, axis=0), 0.0).reshape(
        shards, capacity, 7
    )
    in_depth = lax.all_to_all(out_depth, "img", split_axis=0, concat_axis=0, tiled=True)
    in_camera = lax.all_to_all(out_camera, "img", split_axis=0, concat_axis=0, tiled=True)
    req_depth = jnp.take(in_depth.reshape(slot_total, row_len), my_slots, axis=0)
    req_camera = jnp.take(in_camera.reshape(slot_total, 7), my_slots, axis=0)
    grad_depth, grad_camera, grad_pose = gradients(
        req_depth, req_camera, pose_rows, points, weights
    )
    back_depth = jnp.where(
        slot_sent[:, None], jnp.take(grad_depth, slot_request, axis=0), 0.0
    ).reshape(shards, capacity, row_len)
    back_camera = jnp.where(
        slot_sent[:, None], jnp.take(grad_camera, slot_request, axis=0), 0.0
    ).reshape(shards, capacity, 7)
    ret_depth = lax.all_to_all(back_depth, "img", split_axis=0, concat_axis=0, tiled=True)
    ret_camera = lax.all_to_all(back_camera, "img", split_axis=0, concat_axis=0, tiled=True)
    depth_grad = jnp.dot(
        folding,
        ret_depth.reshape(slot_total, row_len),
        precision=lax.Precision.HIGHEST,
        preferred_element_type=jnp.float32,
    )
    camera_grad = jnp.dot(
        folding,
        ret_camera.reshape(slot_total, 7),
        precision=lax.Precision.HIGHEST,
        preferred_element_type=jnp.float32,
    )
    pose_grad = jnp.sum(grad_pose.reshape(local_pairs, 2, 7), axis=1)
    camera_grad, pose_grad = lax.psum((camera_grad, pose_grad), "rep")
    camera_grad = camera_grad / NPIX
    pose_grad = pose_grad / NPIX
    step_count = START + 1
    depths, depth_moment, depth_second = adam_step(
        depths, depth_moment, depth_second, depth_grad, depth_rate, step_count
    )
    cameras, camera_moment, camera_second = adam_step(
        cameras, camera_moment, camera_second, camera_grad, camera_rate, step_count
    )
    pair_poses, pair_moment, pair_second = adam_step(
        pair_poses, pair_moment, pair_second, pose_grad, pose_rate, step_count
    )
    return (
        depths,
        depth_moment,
        depth_second,
        cameras,
        camera_moment,
        camera_second,
        pair_poses,
        pair_moment,
        pair_second,
    )


def solution(mesh):
    return jax.shard_map(
        body,
        mesh=mesh,
        in_specs=(
            P("img", None),
            P("img", "rep"),
            P("img", "rep"),
            P("img", "rep"),
            P("img", None),
            P("img", None),
            P("img", None),
            P("img", None),
            P("img", None),
            P("img", None),
            P("img", None, None, "rep"),
            P("img", None, "rep"),
        ),
        out_specs=(
            P("img", "rep"),
            P("img", "rep"),
            P("img", "rep"),
            P("img", None),
            P("img", None),
            P("img", None),
            P("img", None),
            P("img", None),
            P("img", None),
        ),
        check_vma=False,
    )
```

profile of v0, /device:TPU:0, one launch (start us, length us, event | category | flops | bytes accessed | tf_op | source)
XLA Modules:
  0.0 361.8 jit_solution(2671256720334237982)
XLA Ops:
  0.7 22.5 %all-gather = s32[8,12,2]{1,2,0:T(2,128)S(1)} all-gather(s32[1,12,2]{1,2,0:T(2,128)} %bitcast.492), channel_id=1, replica_groups=mesh['img'=8,'rep'=4] {'img'}, dimensions={0}, use_global_device_ids=true | all-gather | bytes 864 | tf_op jit(solution)/shard_map/all_gather | solution.py:99
  25.9 1.3 gather_fusion.2
  27.9 3.3 all-to-all-start.1
  31.2 7.2 %gather_fusion = f32[32,36864]{1,0:T(8,128)} fusion(f32[8,36864]{1,0:T(8,128)} %param.13, s32[1024]{0:T(1024)S(1)} %pad_clamp_fusion.2), kind=kCustom, calls=%fused_computation | custom fusion | bytes 9437312 | tf_op jit(solution)/shard_map/jit(_take)/gather | solution.py:134
  38.4 5.6 %gather.33 = f32[8,4,36864]{2,1,0:T(4,128)} reshape(f32[32,36864]{1,0:T(8,128)} %gather_fusion) | data formatting | bytes 9437184 | tf_op jit(solution)/shard_map/jit(_take)/gather | solution.py:134
  44.0 5.9 %select_select_fusion.1 = f32[8,4,36864]{2,1,0:T(4,128)} fusion(f32[8,4,36864]{2,1,0:T(4,128)} %gather.33, pred[8,4]{1,0:T(8,128)(4,1)S(1)} %copy.332, pred[8,4]{1,0:T(8,128)(4,1)S(1)} %copy.326), kind=kLoop, calls=%fused_computation.25 | loop fusion | flops 2359296 | bytes 9437248 | tf_op jit(solution)/shard_map/jit(_where)/select_n | solution.py:134
  53.9 6.0 %copy.342 = bf16[12,2,3,36864]{3,1,0,2:T(2,128)(2,1)} copy(bf16[12,2,3,36864]{3,1,2,0:T(2,128)(2,1)} %param.22) | data formatting | bytes 10616832 | tf_op args[10]
  59.9 8.5 %reshape.491 = bf16[24,3,36864]{2,0,1:T(8,128)(2,1)} reshape(bf16[12,2,3,36864]{3,1,0,2:T(2,128)(2,1)} %copy.342) | data formatting | bytes 10616832 | tf_op jit(solution)/shard_map/reshape | solution.py:121
  68.4 5.9 %all-to-all-start = ((f32[8,4,36864]{2,1,0:T(4,128)}), f32[8,4,36864]{2,1,0:T(4,128)}, u32[]{:S(2)}, u32[]{:S(2)}) async-start(f32[8,4,36864]{2,1,0:T(4,128)} %select_select_fusion.1), calls=%async_computation | async-start | bytes 9437184 | tf_op jit(solution)/shard_map/all_to_all | solution.py:140
  74.3 3.3 convert_multiply_fusion.18
  77.6 3.8 %mul.1018 = f32[24,36864]{1,0:T(8,128)} reshape(f32[12,2,36864]{2,1,0:T(2,128)S(1)} %convert_multiply_fusion.18) | data formatting | bytes 7077888 | tf_op jit(solution)/shard_map/transpose(jvp())/mul | solution.py:62
  84.9 1.3 pad_clamp_fusion
  88.6 1.3 multiply_bitcast_fusion.13
  93.8 81.0 %all-to-all-done = f32[8,4,36864]{2,1,0:T(4,128)} async-done(((f32[8,4,36864]{2,1,0:T(4,128)}), f32[8,4,36864]{2,1,0:T(4,128)}, u32[]{:S(2)}, u32[]{:S(2)}) %all-to-all-start) | async-done | bytes 4718624 | tf_op jit(solution)/shard_map/all_to_all | solution.py:140
  174.8 5.7 %reshape.488 = f32[32,36864]{1,0:T(8,128)} reshape(f32[8,4,36864]{2,1,0:T(4,128)} %all-to-all-done) | data formatting | bytes 9437184 | tf_op jit(solution)/shard_map/reshape | solution.py:142
  180.6 5.7 %gather_fusion.1 = f32[24,36864]{1,0:T(8,128)S(1)} fusion(f32[32,36864]{1,0:T(8,128)} %reshape.488, s32[1024]{0:T(1024)} %copy-done.24), kind=kCustom, calls=%fused_computation.1 | custom fusion | bytes 7077984 | tf_op jit(solution)/shard_map/jit(_take)/gather | solution.py:142
  186.4 9.8 %fusion.14 = (f32[24]{0:T(128)}, f32[24]{0:T(128)}, f32[24]{0:T(128)}, f32[24]{0:T(128)}, f32[24]{0:T(128)S(1)}, /*index=5*/f32[24,36864]{1,0:T(8,128)S(1)}) fusion(f32[24]{0:T(128)} %exponential_bitcast_fusion, bf16[24,3,36864]{2,0,1:T(8,128)(2,1)} %reshape.491, f32[24]{0:T(128)} %get-tuple-element.116, f32[24]{0:T(128)} %get-tuple-element.117, ...), kind=kLoop, calls=%fused_computation.40 | loop fusion | flops 29196168 | bytes 16221624 | tf_op jit(solution)/shard_map/transpose(jvp())/reduce_sum | solution.py:56
  196.4 5.6 %fusion.13 = (f32[24]{0:T(128)}, f32[24]{0:T(128)}, f32[24]{0:T(128)}, f32[24]{0:T(128)}, f32[24]{0:T(128)S(1)}, /*index=5*/f32[24,36864]{1,0:T(8,128)S(1)}) fusion(f32[24]{0:T(128)S(1)} %copy-done.25, bf16[24,3,36864]{2,0,1:T(8,128)(2,1)S(1)} %bitcast.481, f32[24]{0:T(128)S(1)} %copy-done.62, f32[24]{0:T(128)S(1)} %copy-done.63, f32[24]{0:T(128)S(1)} %copy-done.64, ...), kind=kLoop, calls=%fused_computation.39 | loop fusion | flops 29196168 | bytes 16221624 | tf_op jit(solution)/shard_map/transpose(jvp())/reduce_sum | solution.py:56
  202.1 5.8 %fusion.12 = (f32[24]{0:T(128)}, f32[24]{0:T(128)}, f32[24]{0:T(128)}, f32[24]{0:T(128)}, f32[24]{0:T(128)S(1)}, /*index=5*/f32[24,36864]{1,0:T(8,128)S(1)}) fusion(f32[24]{0:T(128)S(1)} %copy-done.25, bf16[24,3,36864]{2,0,1:T(8,128)(2,1)S(1)} %bitcast.481, f32[24]{0:T(128)S(1)} %copy-done.61, f32[24]{0:T(128)S(1)} %copy-done.60, f32[24]{0:T(128)S(1)} %copy-done.53, ...), kind=kLoop, calls=%fused_computation.38 | loop fusion | flops 29196168 | bytes 16221624 | tf_op jit(solution)/shard_map/transpose(jvp())/reduce_sum | solution.py:56
  207.9 4.5 %select_multiply_fusion.2 = (f32[24,36864]{1,0:T(8,128)S(1)}, f32[24,36864]{1,0:T(8,128)S(1)}, f32[24,36864]{1,0:T(8,128)S(1)}, f32[24,36864]{1,0:T(8,128)S(1)}) fusion(f32[24,36864]{1,0:T(8,128)S(1)} %get-tuple-element.66, f32[24,36864]{1,0:T(8,128)} %copy-done.1, pred[24]{0:T(512)(128)(4,1)S(1)} %copy-done.10, f32[24,36864]{1,0:T(8,128)S(1)} %get-tuple-element.67, ...), kind=kLoop, calls=%fused_computation.65 | loop fusion | flops 20348928 | bytes 28607448 | tf_op jit(solution)/shard_map/transpose(jvp())/mul | solution.py:48
  212.5 4.6 %multiply_reduce_fusion.4 = (f32[24]{0:T(128)S(1)}, f32[24]{0:T(128)S(1)}, f32[24]{0:T(128)S(1)}, f32[24]{0:T(128)S(1)}, f32[24]{0:T(128)S(1)}, /*index=5*/f32[2...) fusion(f32[24,36864]{1,0:T(8,128)S(1)} %get-tuple-element.92, ...), kind=kLoop, calls=%fused_computation.48 | loop fusion | flops 29196024 | bytes 10913568 | tf_op jit(solution)/shard_map/transpose(jvp())/reduce_sum | solution.py:38
  217.3 1.3 gather_fusion.5
  218.5 1.4 select_select_fusion.2
  220.0 3.6 %all-to-all-start.3 = ((f32[8,4,7]{2,1,0:T(4,128)}), f32[8,4,7]{2,1,0:T(4,128)S(1)}, u32[]{:S(2)}, u32[]{:S(2)}) async-start(f32[8,4,7]{2,1,0:T(4,128)} %select_select_fusion.2), calls=%async_computation.3 | async-start | bytes 32768 | tf_op jit(solution)/shard_map/all_to_all | solution.py:154
  223.6 4.2 %gather_fusion.4 = f32[32,36864]{1,0:T(8,128)} fusion(f32[24,36864]{1,0:T(8,128)S(1)} %get-tuple-element.91, s32[1024]{0:T(1024)} %pad_clamp_fusion), kind=kCustom, calls=%fused_computation.4 | custom fusion | bytes 9437312 | tf_op jit(solution)/shard_map/jit(_take)/gather | solution.py:148
  227.8 5.5 %gather.39 = f32[8,4,36864]{2,1,0:T(4,128)} reshape(f32[32,36864]{1,0:T(8,128)} %gather_fusion.4) | data formatting | bytes 9437184 | tf_op jit(solution)/shard_map/jit(_take)/gather | solution.py:148
  233.3 5.8 %select_select_fusion = f32[8,4,36864]{2,1,0:T(4,128)} fusion(f32[8,4,36864]{2,1,0:T(4,128)} %gather.39, pred[8,4]{1,0:T(8,128)(4,1)S(1)} %copy-done.42, pred[8,4]{1,0:T(8,128)(4,1)S(1)} %copy-done.43), kind=kLoop, calls=%fused_computation.24 | loop fusion | flops 2359296 | bytes 9437248 | tf_op jit(solution)/shard_map/jit(_where)/select_n | solution.py:147
  239.4 6.1 %all-to-all-start.2 = ((f32[8,4,36864]{2,1,0:T(4,128)}), f32[8,4,36864]{2,1,0:T(4,128)}, u32[]{:S(2)}, u32[]{:S(2)}) async-start(f32[8,4,36864]{2,1,0:T(4,128)} %select_select_fusion), calls=%async_computation.2 | async-start | bytes 9437184 | tf_op jit(solution)/shard_map/all_to_all | solution.py:153
  246.4 6.5 %all-reduce.14 = (f32[8,7]{1,0:T(8,128)S(1)}, f32[12,7]{0,1:T(8,128)S(1)}) all-reduce(f32[8,7]{1,0:T(8,128)S(1)} %fusion.30, f32[12,7]{0,1:T(8,128)S(1)} %copy.346), channel_id=1, replica_groups=mesh['img'=8,'rep'=4] {'rep'}, use_global_device_ids=true, to_apply=%region_19.20 | all-reduce | flops 140 | bytes 1120 | tf_op jit(solution)/shard_map/psum | solution.py:168
  254.2 95.5 %all-to-all-done.2 = f32[8,4,36864]{2,1,0:T(4,128)} async-done(((f32[8,4,36864]{2,1,0:T(4,128)}), f32[8,4,36864]{2,1,0:T(4,128)}, u32[]{:S(2)}, u32[]{:S(2)}) %all-to-all-start.2) | async-done | bytes 4718624 | tf_op jit(solution)/shard_map/all_to_all | solution.py:153
  349.7 5.6 %reshape.492 = f32[32,36864]{1,0:T(8,128)} reshape(f32[8,4,36864]{2,1,0:T(4,128)} %all-to-all-done.2) | data formatting | bytes 9437184 | tf_op jit(solution)/shard_map/reshape | solution.py:157
  355.4 6.5 %divide_subtract_fusion = (f32[8,36864]{1,0:T(8,128)}, f32[8,36864]{1,0:T(8,128)}, f32[8,36864]{1,0:T(8,128)}) fusion(f32[8,36864]{1,0:T(8,128)S(1)} %copy-done, f32[8,36864]{1,0:T(8,128)S(1)} %copy-done.6, f32[8,36864]{1,0:T(8,128)S(1)} %copy-done.7, f32[32,36864]{1,0:T(8,128)} %reshape.492, s32[32]{0:T(128)S(1)} %copy-done.39, pred[32]{0:T(512)(128)(4,1)S(1)} %copy-done.68), kind=kOutput, calls=%fused_computation.71 | convolution fusion | flops 116785664 | bytes 11796640 | tf_op jit(solution)/shard_map/dot_general | solution.py:155
  (220 shorter events, 19.5 us)
Async XLA Ops:
  25.9 18.1 %copy-start.40 = (pred[8,4]{1,0:T(8,128)(4,1)}, pred[8,4]{1,0:T(8,128)(4,1)S(1)}, u32[]{:S(2)}) copy-start(pred[8,4]{1,0:T(8,128)(4,1)S(1)} %copy.326) | copy-start | bytes 100
  27.9 40.6 %all-to-all-start.1 = ((f32[8,4,7]{2,1,0:T(4,128)}), f32[8,4,7]{2,1,0:T(4,128)S(1)}, u32[]{:S(2)}, u32[]{:S(2)}) async-start(f32[8,4,7]{2,1,0:T(4,128)} %select_select_fusion.3), calls=%async_computation.1 | async-start | bytes 32768 | tf_op jit(solution)/shard_map/all_to_all | solution.py:141
  68.4 106.4 %all-to-all-start = ((f32[8,4,36864]{2,1,0:T(4,128)}), f32[8,4,36864]{2,1,0:T(4,128)}, u32[]{:S(2)}, u32[]{:S(2)}) async-start(f32[8,4,36864]{2,1,0:T(4,128)} %select_select_fusion.1), calls=%async_computation | async-start | bytes 9437184 | tf_op jit(solution)/shard_map/all_to_all | solution.py:140
  186.3 15.8 %copy-start.1 = (f32[24,36864]{1,0:T(8,128)}, f32[24,36864]{1,0:T(8,128)S(1)}, u32[]{:S(2)}) copy-start(f32[24,36864]{1,0:T(8,128)S(1)} %gather_fusion.1) | copy-start | bytes 10616836
  186.3 10.0 %slice-start = ((s8[5308416]{0:T(1024)(128)(4,1)}), s8[4194304]{0:T(1024)(128)(4,1)S(1)}, s32[]{:S(2)}) async-start(s8[5308416]{0:T(1024)(128)(4,1)} %bitcast.480), calls=%async_computation.4 | async-start | bytes 8388608
  186.3 9.9 %slice-start.1 = ((s8[5308416]{0:T(1024)(128)(4,1)}), s8[1114112]{0:T(1024)(128)(4,1)S(1)}, s32[]{:S(2)}) async-start(s8[5308416]{0:T(1024)(128)(4,1)} %bitcast.480), calls=%async_computation.5 | async-start | bytes 2228224
  186.3 9.9 %copy-start.2 = (f32[24,36864]{1,0:T(8,128)S(1)}, f32[24,36864]{1,0:T(8,128)}, u32[]{:S(2)}) copy-start(f32[24,36864]{1,0:T(8,128)} %mul.1018) | copy-start | bytes 10616836
  186.3 9.9 %copy-start.3 = (f32[36864]{0:T(1024)S(1)}, f32[36864]{0:T(1024)}, u32[]{:S(2)}) copy-start(f32[36864]{0:T(1024)} %get-tuple-element.128) | copy-start | bytes 442372
  186.3 9.9 %copy-start.4 = (f32[36864]{0:T(1024)S(1)}, f32[36864]{0:T(1024)}, u32[]{:S(2)}) copy-start(f32[36864]{0:T(1024)} %get-tuple-element.129) | copy-start | bytes 442372
  186.3 9.9 %copy-start.20 = (f32[24]{0:T(128)S(1)}, f32[24]{0:T(128)}, u32[]{:S(2)}) copy-start(f32[24]{0:T(128)} %get-tuple-element.106) | copy-start | bytes 292
  186.3 9.9 %copy-start.21 = (f32[24]{0:T(128)S(1)}, f32[24]{0:T(128)}, u32[]{:S(2)}) copy-start(f32[24]{0:T(128)} %get-tuple-element.108) | copy-start | bytes 292
  186.4 9.9 %copy-start.25 = (f32[24]{0:T(128)S(1)}, f32[24]{0:T(128)}, u32[]{:S(2)}) copy-start(f32[24]{0:T(128)} %exponential_bitcast_fusion) | copy-start | bytes 292
  186.4 9.9 %copy-start.27 = (f32[24]{0:T(128)S(1)}, f32[24]{0:T(128)}, u32[]{:S(2)}) copy-start(f32[24]{0:T(128)} %get-tuple-element.105) | copy-start | bytes 292
  186.4 9.9 %copy-start.49 = (f32[24]{0:T(128)S(1)}, f32[24]{0:T(128)}, u32[]{:S(2)}) copy-start(f32[24]{0:T(128)} %get-tuple-element.54) | copy-start | bytes 292
  186.4 9.9 %copy-start.62 = (f32[24]{0:T(128)S(1)}, f32[24]{0:T(128)}, u32[]{:S(2)}) copy-start(f32[24]{0:T(128)} %get-tuple-element.120) | copy-start | bytes 292
  186.4 9.9 %copy-start.63 = (f32[24]{0:T(128)S(1)}, f32[24]{0:T(128)}, u32[]{:S(2)}) copy-start(f32[24]{0:T(128)} %get-tuple-element.121) | copy-start | bytes 292
  186.4 9.9 %copy-start.64 = (f32[24]{0:T(128)S(1)}, f32[24]{0:T(128)}, u32[]{:S(2)}) copy-start(f32[24]{0:T(128)} %get-tuple-element.123) | copy-start | bytes 292
  196.2 20.9 %copy-start.54 = (f32[24]{0:T(128)}, f32[24]{0:T(128)S(1)}, u32[]{:S(2)}) copy-start(f32[24]{0:T(128)S(1)} %get-tuple-element.49) | copy-start | bytes 292
  202.0 15.1 %copy-start.56 = (f32[24]{0:T(128)}, f32[24]{0:T(128)S(1)}, u32[]{:S(2)}) copy-start(f32[24]{0:T(128)S(1)} %get-tuple-element.48) | copy-start | bytes 292
  220.0 19.4 %all-to-all-start.3 = ((f32[8,4,7]{2,1,0:T(4,128)}), f32[8,4,7]{2,1,0:T(4,128)S(1)}, u32[]{:S(2)}, u32[]{:S(2)}) async-start(f32[8,4,7]{2,1,0:T(4,128)} %select_select_fusion.2), calls=%async_computation.3 | async-start | bytes 32768 | tf_op jit(solution)/shard_map/all_to_all | solution.py:154
  239.3 13.6 %copy-start.12 = (f32[12,7]{0,1:T(8,128)S(1)}, f32[12,7]{0,1:T(8,128)}, u32[]{:S(2)}) copy-start(f32[12,7]{0,1:T(8,128)} %param.19) | copy-start | bytes 1012
  239.3 13.6 %copy-start.44 = (f32[12,7]{0,1:T(8,128)S(1)}, f32[12,7]{0,1:T(8,128)}, u32[]{:S(2)}) copy-start(f32[12,7]{0,1:T(8,128)} %param.20) | copy-start | bytes 1012
  239.3 13.6 %copy-start.45 = (f32[12,7]{0,1:T(8,128)S(1)}, f32[12,7]{0,1:T(8,128)}, u32[]{:S(2)}) copy-start(f32[12,7]{0,1:T(8,128)} %param.21) | copy-start | bytes 1012
  239.4 14.2 %copy-start.5 = (f32[8,7]{1,0:T(8,128)S(1)}, f32[8,7]{1,0:T(8,128)}, u32[]{:S(2)}) copy-start(f32[8,7]{1,0:T(8,128)} %param.16) | copy-start | bytes 676
  239.4 14.2 %copy-start.46 = (f32[8,7]{1,0:T(8,128)S(1)}, f32[8,7]{1,0:T(8,128)}, u32[]{:S(2)}) copy-start(f32[8,7]{1,0:T(8,128)} %param.17) | copy-start | bytes 676
  239.4 14.2 %copy-start.47 = (f32[8,7]{1,0:T(8,128)S(1)}, f32[8,7]{1,0:T(8,128)}, u32[]{:S(2)}) copy-start(f32[8,7]{1,0:T(8,128)} %param.18) | copy-start | bytes 676
  239.4 110.3 %all-to-all-start.2 = ((f32[8,4,36864]{2,1,0:T(4,128)}), f32[8,4,36864]{2,1,0:T(4,128)}, u32[]{:S(2)}, u32[]{:S(2)}) async-start(f32[8,4,36864]{2,1,0:T(4,128)} %select_select_fusion), calls=%async_computation.2 | async-start | bytes 9437184 | tf_op jit(solution)/shard_map/all_to_all | solution.py:153
  254.2 101.2 %copy-start = (f32[8,36864]{1,0:T(8,128)S(1)}, f32[8,36864]{1,0:T(8,128)}, u32[]{:S(2)}) copy-start(f32[8,36864]{1,0:T(8,128)} %param.13) | copy-start | bytes 3538948
  254.2 101.2 %copy-start.6 = (f32[8,36864]{1,0:T(8,128)S(1)}, f32[8,36864]{1,0:T(8,128)}, u32[]{:S(2)}) copy-start(f32[8,36864]{1,0:T(8,128)} %param.14) | copy-start | bytes 3538948
  254.2 101.2 %copy-start.7 = (f32[8,36864]{1,0:T(8,128)S(1)}, f32[8,36864]{1,0:T(8,128)}, u32[]{:S(2)}) copy-start(f32[8,36864]{1,0:T(8,128)} %param.15) | copy-start | bytes 3538948
  254.2 101.2 %copy-start.39 = (s32[32]{0:T(128)S(1)}, s32[32]{0:T(128)}, u32[]{:S(2)}) copy-start(s32[32]{0:T(128)} %copy-done.38) | copy-start | bytes 388
  254.2 101.2 %copy-start.68 = (pred[32]{0:T(512)(128)(4,1)S(1)}, pred[32]{0:T(512)(128)(4,1)}, u32[]{:S(2)}) copy-start(pred[32]{0:T(512)(128)(4,1)} %copy-done.67) | copy-start | bytes 100
  (50 other events, 308.9 us)
where the time goes:
time: 363 us; the launch traced here: 362 us
  waiting for transfers between devices  177 us (49%)
  local copies, waits for them, and re-layouts  70 us (19%)
  other arithmetic  59 us (16%)
  blocking collectives  28.9 us (8%)
  starting transfers between devices  19 us (5%)
  matrix products  6.57 us (2%)
    all_to_all x1, waiting for transfers between devices, body(): lax.all_to_all(back_depth, 'img', split_axis=0, concat_axis=0, tiled=True)  95.5 us
    all_to_all x1, waiting for transfers between devices, body(): lax.all_to_all(out_depth, 'img', split_axis=0, concat_axis=0, tiled=True)  81 us
    all_gather x1, blocking collectives, body(): lax.all_gather(pair_images, 'img', axis=0, tiled=True)  22.5 us
    reduce_sum x3, other arithmetic, view_loss(): pose_rot[3 * k + 2] * point_z  21.2 us
    gather x2, local copies, waits for them, and re-layouts, body(): jnp.take(depths, slot_image, axis=0)  12.8 us
    gather x2, local copies, waits for them, and re-layouts, body(): jnp.take(grad_depth, slot_request, axis=0)  9.71 us
    unnamed x162, local copies, waits for them, and re-layouts  9.25 us
    reshape x1, local copies, waits for them, and re-layouts, body(): points = pointmaps.reshape(requests, 3, row_len)  8.5 us
  transfers between devices with their start and end apart: 4, of which 2 were waited for; matrix products, arithmetic and copies ran while one was open for 20% of the time, Pallas kernels for 0%

commit v1 on v0

v1 whole, which is shorter than its diff:
```python
import functools
import math

import jax
import jax.numpy as jnp
from jax import lax
from jax.experimental import pallas as pl
from jax.experimental.pallas import tpu as pltpu
from jax.sharding import PartitionSpec as P

HEIGHT = 288
WIDTH = 512
START = 50
NPIX = 147456
LANES = 128
CHUNKS = 1

beta_one = 0.9
beta_two = 0.999
adam_eps = 1e-08
depth_rate = 0.05
camera_rate = 0.01
pose_rate = 0.01

DEPTH_MID = 2.25
DEPTH_STEP = 1.75 / 32766.0
VIEW_BOUND = 340.0
CODE_UNIT = 8.0
INTS = jnp.int16
SUMS = 11
COEFS = 16

SMEM = pl.BlockSpec(memory_space=pltpu.SMEM)
VMEM = pl.BlockSpec(memory_space=pltpu.VMEM)
PARAMS = pltpu.CompilerParams(vmem_limit_bytes=40 * 1024 * 1024)


def code_scale(bound):
    return 32766.0 / math.log2(1.0 + bound / CODE_UNIT)


def encode(magnitude, negative, bound):
    steps = (jnp.log2(1.0 + magnitude) * code_scale(bound) + 0.5).astype(jnp.int32)
    steps = jnp.minimum(steps, 32767)
    return jnp.where(negative, -steps, steps).astype(INTS)


def decode(code, bound):
    steps = code.astype(jnp.int32)
    size = jnp.abs(steps).astype(jnp.float32) * (1.0 / code_scale(bound))
    value = CODE_UNIT * jnp.exp2(size) - CODE_UNIT
    return jnp.where(steps < 0, -value, value)


def table_kernel(half, cap, images, me_ref, list_ref, tab_ref, count_ref):
    me = me_ref[0]
    shards = 2 * half
    requests = list_ref.shape[1]
    asked = shards * cap

    @pl.loop(0, 2 * asked)
    def _(i):
        tab_ref[i] = -1

    @pl.loop(0, 2 * shards)
    def _(i):
        count_ref[i] = 0

    def put(cell, base, value):
        rank = count_ref[cell]
        tab_ref[base + jnp.minimum(rank, cap - 1)] = value
        count_ref[cell] = rank + 1

    @pl.loop(0, half)
    def _(k):
        @pl.loop(0, requests)
        def _(r):
            image = list_ref[k, r]
            owner = lax.div(image, images)

            @pl.when(owner == me)
            def _():
                put(k, k * cap, image - owner * images)

            @pl.when(owner == (me ^ half))
            def _():
                put(half + k, (half + k) * cap, image - owner * images)

    @pl.loop(0, requests)
    def _(r):
        relative = lax.div(list_ref[0, r], images) ^ me
        put(shards + relative, asked + relative * cap, r)


def slot_tables(me, listing, half, cap, images):
    return pl.pallas_call(
        functools.partial(table_kernel, half, cap, images),
        out_shape=jax.ShapeDtypeStruct((4 * half * cap,), jnp.int32),
        in_specs=[SMEM, SMEM],
        out_specs=SMEM,
        scratch_shapes=[pltpu.SMEM((4 * half,), jnp.int32)],
        name="slot_tables",
    )(me, listing)


def pack_kernel(first, cap, tab_ref, src_ref, *out_refs):
    for k, out_ref in enumerate(out_refs):

        @pl.loop(0, cap)
        def _(c):
            image = jnp.maximum(tab_ref[first + k * cap + c], 0)
            out_ref[c] = src_ref[image]


def pack_slots(table, maps, first, half, cap):
    rows = maps.shape[1]
    return pl.pallas_call(
        functools.partial(pack_kernel, first, cap),
        out_shape=[jax.ShapeDtypeStruct((cap, rows, LANES), INTS)] * half,
        in_specs=[SMEM, VMEM],
        out_specs=[VMEM] * half,
        compiler_params=PARAMS,
        name="pack_slots",
    )(table, maps)


def part_kernel(point_ref, weight_ref, out_ref, wide):
    rows = point_ref.shape[2]
    for q in range(4):
        source = point_ref.at[0, q] if q < 3 else weight_ref.at[0]
        wide[q] = source[...].astype(jnp.float32)
    for q in range(4):
        for v in range(2):
            for t in range(0, rows // 2, 16):
                out_ref[v, q, t : t + 16] = wide[q, pl.ds(2 * t + v, 16, stride=2), :].astype(
                    jnp.bfloat16
                )


def part_views(points, weights):
    pairs, _, _, pixels = points.shape
    rows = pixels // LANES
    points = (
        points.transpose(0, 2, 1, 3)
        .reshape(pairs, 3, 2, rows, LANES)
        .transpose(0, 1, 3, 2, 4)
        .reshape(pairs, 3, 2 * rows, LANES)
    )
    weights = (
        weights.reshape(pairs, 2, rows, LANES).transpose(0, 2, 1, 3).reshape(pairs, 2 * rows, LANES)
    )
    return pl.pallas_call(
        part_kernel,
        grid=(pairs,),
        out_shape=jax.ShapeDtypeStruct((2 * pairs, 4, rows, LANES), jnp.bfloat16),
        in_specs=[
            pl.BlockSpec((1, 3, 2 * rows, LANES), lambda e: (e, 0, 0, 0)),
            pl.BlockSpec((1, 2 * rows, LANES), lambda e: (e, 0, 0)),
        ],
        out_specs=pl.BlockSpec((2, 4, rows, LANES), lambda e: (e, 0, 0, 0)),
        scratch_shapes=[pltpu.VMEM((4, 2 * rows, LANES), jnp.float32)],
        compiler_params=PARAMS,
        name="part_views",
    )(points, weights)


def view_kernel(first, half, cap, start, tab_ref, coef_ref, row_ref, view_ref, *refs):
    depth_refs, grad_refs = refs[:half], refs[half : 2 * half]
    sum_ref, depth_all, grad_all = refs[2 * half :]
    rows = depth_all.shape[1]
    for k in range(half):
        depth_all[k * cap : (k + 1) * cap] = depth_refs[k][...]
    sum_ref[...] = jnp.zeros_like(sum_ref)
    across = WIDTH // LANES
    line = lax.broadcasted_iota(jnp.int32, (16, LANES), 0)
    lane = lax.broadcasted_iota(jnp.int32, (16, LANES), 1)
    columns = ((line % across) * LANES + lane).astype(jnp.float32) + (0.5 - 0.5 * WIDTH)
    lines = (line // across).astype(jnp.float32) + row_ref[0]

    @pl.loop(0, half * cap)
    def _(s):
        view = tab_ref[first + s]

        @pl.when(view >= 0)
        def _():
            def coef(i):
                return coef_ref[view, i]

            step = [coef(3 + j) * (16.0 / across) for j in range(3)]
            ray = [columns * coef(j) + (lines * coef(3 + j) + coef(6 + j)) for j in range(3)]
            shift = [coef(9 + j) for j in range(3)]
            gain = coef(12)
            totals = [None] * SUMS

            def add(i, value):
                value = value[:8] + value[8:]
                totals[i] = value if totals[i] is None else totals[i] + value

            for t in range(0, rows, 16):
                here = slice(start + t, start + t + 16)
                point = [view_ref[view, j, here].astype(jnp.float32) for j in range(3)]
                weight = view_ref[view, 3, here].astype(jnp.float32)
                depth = (
                    depth_all[s, t : t + 16].astype(jnp.int32).astype(jnp.float32) * DEPTH_STEP
                    + DEPTH_MID
                )
                pull = [weight * (depth * ray[j] + (shift[j] - point[j])) for j in range(3)]
                along = pull[0] * ray[0] + pull[1] * ray[1] + pull[2] * ray[2]
                grad_all[s, t : t + 16] = encode(
                    jnp.abs(along) * gain, along < 0.0, VIEW_BOUND
                )
                for j in range(3):
                    add(j, pull[j])
                    add(8 + j, depth * pull[j])
                    a, b = (j + 1) % 3, (j + 2) % 3
                    add(3 + j, point[a] * pull[b] - point[b] * pull[a])
                add(6, point[0] * pull[0] + point[1] * pull[1] + point[2] * pull[2])
                add(7, depth * along)
                ray = [ray[j] + step[j] for j in range(3)]
            for i in range(SUMS):
                sum_ref[view, i : i + 1] = jnp.sum(totals[i], axis=0, keepdims=True)

    for k in range(half):
        grad_refs[k][...] = grad_all[k * cap : (k + 1) * cap]


def view_terms(table, coefs, row, views, depths, first, start, half, cap):
    rows = depths[0].shape[1]
    out = pl.pallas_call(
        functools.partial(view_kernel, first, half, cap, start),
        out_shape=[jax.ShapeDtypeStruct((cap, rows, LANES), INTS)] * half
        + [jax.ShapeDtypeStruct((views.shape[0], COEFS, LANES), jnp.float32)],
        in_specs=[SMEM, SMEM, SMEM] + [VMEM] * (half + 1),
        out_specs=[VMEM] * (half + 1),
        scratch_shapes=[
            pltpu.VMEM((half * cap, rows, LANES), INTS),
            pltpu.VMEM((half * cap, rows, LANES), INTS),
        ],
        compiler_params=PARAMS,
        name="view_terms",
    )(table, coefs, row, views, *depths)
    return out[:half], out[half]


def fold(first, cap, tab_ref, slot_refs, total_ref):
    total_ref[...] = jnp.zeros_like(total_ref)
    for k, slot_ref in enumerate(slot_refs):

        @pl.loop(0, cap)
        def _(c):
            image = tab_ref[first + k * cap + c]

            @pl.when(image >= 0)
            def _():
                total_ref[image] += decode(slot_ref[c], VIEW_BOUND)


def fold_kernel(first, cap, bound, tab_ref, *refs):
    slot_refs, out_ref, total = refs[:-2], refs[-2], refs[-1]
    fold(first, cap, tab_ref, slot_refs, total)

    @pl.loop(0, total.shape[0])
    def _(i):
        value = total[i]
        out_ref[i] = encode(jnp.abs(value) * (1.0 / CODE_UNIT), value < 0.0, bound)


def fold_slots(table, slots, first, images, cap, bound):
    rows = slots[0].shape[1]
    return pl.pallas_call(
        functools.partial(fold_kernel, first, cap, bound),
        out_shape=jax.ShapeDtypeStruct((images, rows, LANES), INTS),
        in_specs=[SMEM] + [VMEM] * len(slots),
        out_specs=VMEM,
        scratch_shapes=[pltpu.VMEM((images, rows, LANES), jnp.float32)],
        compiler_params=PARAMS,
        name="fold_slots",
    )(table, *slots)


def local_kernel(first, cap, tab_ref, *refs):
    fold(first, cap, tab_ref, refs[:-1], refs[-1])


def fold_local(table, slots, first, images, cap):
    rows = slots[0].shape[1]
    return pl.pallas_call(
        functools.partial(local_kernel, first, cap),
        out_shape=jax.ShapeDtypeStruct((images, rows, LANES), jnp.float32),
        in_specs=[SMEM] + [VMEM] * len(slots),
        out_specs=VMEM,
        compiler_params=PARAMS,
        name="fold_local",
    )(table, *slots)


def adam_step(values, moment, second, gradient, step_rate):
    step_count = START + 1
    moment = beta_one * moment + (1.0 - beta_one) * gradient
    second = beta_two * second + (1.0 - beta_two) * gradient * gradient
    fix_one = 1.0 - beta_one**step_count
    fix_two = 1.0 - beta_two**step_count
    values = values - step_rate * (moment / fix_one) / (jnp.sqrt(second / fix_two) + adam_eps)
    return (values, moment, second)


def depth_kernel(bound, local_ref, far_ref, x_ref, m_ref, s_ref, nx_ref, nm_ref, ns_ref, grad):
    images, rows, _ = local_ref.shape
    for i in range(images):
        grad[i * rows : (i + 1) * rows] = local_ref[i] + decode(far_ref[i], bound)
    for t in range(rows):
        here = slice(t * LANES, (t + 1) * LANES)
        gradient = grad[pl.ds(t, images, stride=rows), :]
        nx_ref[:, here], nm_ref[:, here], ns_ref[:, here] = adam_step(
            x_ref[:, here], m_ref[:, here], s_ref[:, here], gradient, depth_rate
        )


def update_depths(local, far, values, moment, second, bound):
    images, rows, _ = local.shape
    block = 48
    wide = pl.BlockSpec((images, block * LANES), lambda t: (0, t))
    tall = pl.BlockSpec((images, block, LANES), lambda t: (0, t, 0))
    return pl.pallas_call(
        functools.partial(depth_kernel, bound),
        grid=(rows // block,),
        out_shape=[jax.ShapeDtypeStruct(values.shape, jnp.float32)] * 3,
        in_specs=[tall, tall, wide, wide, wide],
        out_specs=[wide, wide, wide],
        scratch_shapes=[pltpu.VMEM((images * block, LANES), jnp.float32)],
        compiler_params=PARAMS,
        name="update_depths",
    )(local, far, values, moment, second)


def rotation(first, middle, last):
    inverse = 1.0 / (1.0 + first * first + middle * middle + last * last)
    return (
        (1.0 + first * first - middle * middle - last * last) * inverse,
        2.0 * (first * middle - last) * inverse,
        2.0 * (first * last + middle) * inverse,
        2.0 * (first * middle + last) * inverse,
        (1.0 - first * first + middle * middle - last * last) * inverse,
        2.0 * (middle * last - first) * inverse,
        2.0 * (first * last - middle) * inverse,
        2.0 * (middle * last + first) * inverse,
        (1.0 - first * first - middle * middle + last * last) * inverse,
    )


def cross(a, b):
    return [a[(j + 1) % 3] * b[(j + 2) % 3] - a[(j + 2) % 3] * b[(j + 1) % 3] for j in range(3)]


def turn_gradient(spin, torque):
    factor = 2.0 / (1.0 + spin[0] * spin[0] + spin[1] * spin[1] + spin[2] * spin[2])
    swing = cross(spin, torque)
    return [factor * (torque[j] + swing[j]) for j in range(3)]


def view_coefs(cams, poses):
    inverse_focal = jnp.exp(-cams[0]) * (1.0 / WIDTH)
    cam = rotation(cams[1], cams[2], cams[3])
    pose = rotation(poses[0], poses[1], poses[2])
    scale = jnp.exp(poses[6])
    back = jnp.exp(-poses[6])
    gap = [cams[4 + k] - poses[3 + k] for k in range(3)]
    both = [
        [sum(pose[3 * k + j] * cam[3 * k + i] for k in range(3)) for i in range(3)] for j in range(3)
    ]
    matrix = [[both[j][i] * back for i in range(3)] for j in range(3)]
    shift = [sum(pose[3 * k + j] * gap[k] for k in range(3)) * back for j in range(3)]
    rows = [matrix[j][0] * inverse_focal for j in range(3)]
    rows += [matrix[j][1] * inverse_focal for j in range(3)]
    rows += [matrix[j][2] for j in range(3)]
    rows += shift
    rows += [scale * scale * (1.0 / CODE_UNIT)]
    rows += [jnp.zeros_like(scale)] * (COEFS - len(rows))
    return jnp.stack(rows, axis=1), (both, pose, scale, matrix, shift)


def view_gradients(sums, cams, poses, parts):
    both, pose, scale, matrix, shift = parts
    square = scale * scale
    force, torque, stretch, drawn, lever = sums[0:3], sums[3:6], sums[6], sums[7], sums[8:11]
    push = [scale * sum(pose[3 * k + j] * force[j] for j in range(3)) for k in range(3)]
    swing = cross(shift, force)
    arm = [torque[j] - swing[j] for j in range(3)]
    camera_torque = [square * sum(both[j][i] * arm[j] for j in range(3)) for i in range(3)]
    pose_torque = [-square * torque[j] for j in range(3)]
    focal = -square * (drawn - sum(matrix[j][2] * lever[j] for j in range(3)))
    camera = [focal] + turn_gradient([cams[1], cams[2], cams[3]], camera_torque) + push
    posed = (
        turn_gradient([poses[0], poses[1], poses[2]], pose_torque)
        + [-value for value in push]
        + [-square * stretch]
    )
    return jnp.stack(camera, axis=1), jnp.stack(posed, axis=1)


def body(
    pair_images,
    depths,
    depth_moment,
    depth_second,
    cameras,
    camera_moment,
    camera_second,
    pair_poses,
    pair_moment,
    pair_second,
    pointmaps,
    confidence,
):
    shards = lax.axis_size("img")
    half = shards // 2
    me = lax.axis_index("img")
    rep = lax.axis_index("rep")
    images, row_len = depths.shape
    pairs = pair_images.shape[0]
    requests = 2 * pairs
    cap = max(2, 3 * pairs // shards)
    rows = row_len // LANES
    size = rows // CHUNKS
    far_bound = VIEW_BOUND * half * cap

    def swap(value, k):
        return lax.ppermute(value, "img", [(i, i ^ k) for i in range(shards)])

    listing = pair_images.reshape(1, requests)
    codes = jnp.round((depths - DEPTH_MID) * (1.0 / DEPTH_STEP)).astype(INTS)
    codes = codes.reshape(images, rows, LANES)
    near = [codes[:, c * size : (c + 1) * size] for c in range(CHUNKS)]
    far = [swap(near[c], half) for c in range(CHUNKS)]
    lists = jnp.concatenate([listing] + [swap(listing, k) for k in range(1, half)], axis=0)
    table = slot_tables(me.reshape(1), lists, half, cap, images)

    all_cameras = lax.all_gather(cameras, "img", axis=0, tiled=True)
    cams = jnp.take(all_cameras, pair_images.reshape(requests), axis=0).T
    poses = jnp.repeat(pair_poses.T, 2, axis=1)
    coefs, parts = view_coefs(cams, poses)
    views = part_views(pointmaps, confidence)

    slots = half * cap

    def exchange(values):
        return [values[0]] + [swap(values[k], k) for k in range(1, half)]

    sums = 0.0
    far_codes, near_totals = [], []
    for h in (0, 1):
        for c in range(CHUNKS):
            start = c * size
            row = rep * (row_len // WIDTH) + start // (WIDTH // LANES)
            row = (row.astype(jnp.float32) + (0.5 - 0.5 * HEIGHT)).reshape(1)
            asked = exchange(pack_slots(table, (near, far)[h][c], h * slots, half, cap))
            grads, moments = view_terms(
                table, coefs, row, views, asked, (2 + h) * slots, start, half, cap
            )
            sums = sums + jnp.sum(moments, axis=2)
            back = exchange(grads)
            if h == 1:
                folded = fold_slots(table, back, slots, images, cap, far_bound)
                far_codes.append(swap(folded, half))
            else:
                near_totals.append(fold_local(table, back, 0, images, cap))
    near_total = jnp.concatenate(near_totals, axis=1)
    far_code = jnp.concatenate(far_codes, axis=1)
    depths, depth_moment, depth_second = update_depths(
        near_total, far_code, depths, depth_moment, depth_second, far_bound
    )

    camera_terms, pose_terms = view_gradients(list(sums.T[:SUMS]), cams, poses, parts)
    chosen = (
        pair_images.reshape(1, requests) == jnp.arange(shards * images, dtype=jnp.int32)[:, None]
    )
    camera_parts = jnp.sum(jnp.where(chosen[:, :, None], camera_terms[None], 0.0), axis=1)
    camera_parts = lax.all_to_all(
        camera_parts.reshape(shards, images, 7), "img", split_axis=0, concat_axis=0, tiled=True
    )
    camera_grad = jnp.sum(camera_parts, axis=0)
    pose_grad = jnp.sum(pose_terms.reshape(pairs, 2, 7), axis=1)
    camera_grad, pose_grad = lax.psum((camera_grad, pose_grad), "rep")
    camera_grad = camera_grad / NPIX
    pose_grad = pose_grad / NPIX
    cameras, camera_moment, camera_second = adam_step(
        cameras, camera_moment, camera_second, camera_grad, camera_rate
    )
    pair_poses, pair_moment, pair_second = adam_step(
        pair_poses, pair_moment, pair_second, pose_grad, pose_rate
    )
    return (
        depths,
        depth_moment,
        depth_second,
        cameras,
        camera_moment,
        camera_second,
        pair_poses,
        pair_moment,
        pair_second,
    )


def solution(mesh):
    return jax.shard_map(
        body,
        mesh=mesh,
        in_specs=(
            P("img", None),
            P("img", "rep"),
            P("img", "rep"),
            P("img", "rep"),
            P("img", None),
            P("img", None),
            P("img", None),
            P("img", None),
            P("img", None),
            P("img", None),
            P("img", None, None, "rep"),
            P("img", None, "rep"),
        ),
        out_specs=(
            P("img", "rep"),
            P("img", "rep"),
            P("img", "rep"),
            P("img", None),
            P("img", None),
            P("img", None),
            P("img", None),
            P("img", None),
            P("img", None),
        ),
        check_vma=False,
    )
```

time: 363 us -> 195 us (0.54)
  waiting for transfers between devices: 177 us -> 20.3 us
  local copies, waits for them, and re-layouts: 70 us -> 33.1 us
  Pallas kernels: 0 us -> 31.7 us
  other arithmetic: 59 us -> 28.8 us
  blocking collectives: 28.9 us -> 52.8 us
  matrix products: 6.57 us -> 0 us
  starting transfers between devices: 19 us -> 25.1 us
    all_to_all x4 -> x1, waiting for transfers between devices: 177 us -> 0.01 us  [body(): lax.all_to_all(camera_parts.reshape(shards, images, 7), 'img', split_axis...]
    pallas_call x0 -> x9, Pallas kernels: none -> 31.7 us  [the longest x2 12.5 us: view_terms(): pl.pallas_call(functools.partial(view_kernel, first, half, cap, start), o...]
    gather x9 -> x1, local copies, waits for them, and re-layouts: 31.4 us -> 0.58 us  [body(): cams = jnp.take(all_cameras, pair_images.reshape(requests), axis=0).T]
    all_gather x1, blocking collectives: 22.5 us -> 46.1 us  [body(): all_cameras = lax.all_gather(cameras, 'img', axis=0, tiled=True)]
    reduce_sum x8 -> x5, other arithmetic: 26.3 us -> 3.1 us  [the longest x2 0.84 us: body(): sums = sums + jnp.sum(moments, axis=2)]
    ppermute x0 -> x17, starting transfers between devices: none -> 21.1 us  [swap(): return lax.ppermute(value, 'img', [(i, i ^ k) for i in range(shards)])]
    ppermute x0 -> x17, waiting for transfers between devices: none -> 20.3 us  [swap(): return lax.ppermute(value, 'img', [(i, i ^ k) for i in range(shards)])]
    reshape x5, local copies, waits for them, and re-layouts: 20 us -> 2.28 us  [the longest x2 2.04 us: body(): camera_parts.reshape(shards, images, 7)]
  transfers between devices with their start and end apart: 4 -> 18, of which waited for: 2 -> 7; matrix products, arithmetic and copies ran while one was open for 20% -> 14% of each run, Pallas kernels for 0% -> 11%
where the time goes in v1:
time: 195 us; the launch traced here: 193 us
  blocking collectives  52.8 us (27%)
  local copies, waits for them, and re-layouts  33.1 us (17%)
  Pallas kernels  31.7 us (16%)
  other arithmetic  28.8 us (15%)
  starting transfers between devices  25.1 us (13%)
  waiting for transfers between devices  20.3 us (10%)
    all_gather x1, blocking collectives, body(): all_cameras = lax.all_gather(cameras, 'img', axis=0, tiled=True)  46.1 us
    ppermute x17, starting transfers between devices, swap(): return lax.ppermute(value, 'img', [(i, i ^ k) for i in range(shards)])  21.1 us
    unnamed x104, local copies, waits for them, and re-layouts  20.6 us
    ppermute x17, waiting for transfers between devices, swap(): return lax.ppermute(value, 'img', [(i, i ^ k) for i in range(shards)])  20.3 us
    pallas_call x2, Pallas kernels, view_terms(): pl.pallas_call(functools.partial(view_kernel, first, half, cap, start), o...  12.5 us
    unnamed x7, other arithmetic  7.5 us
    psum x1, blocking collectives, body(): camera_grad, pose_grad = lax.psum((camera_grad, pose_grad), 'rep')  6.73 us
    pallas_call x1, Pallas kernels, update_depths(): pl.pallas_call(functools.partial(depth_kernel, bound), grid=(rows // bloc...  5.17 us
  transfers between devices with their start and end apart: 18, of which 7 were waited for; matrix products, arithmetic and copies ran while one was open for 14% of the time, Pallas kernels for 11%

profile of v1, /device:TPU:0, one launch (start us, length us, event | category | flops | bytes accessed | tf_op | source)
XLA Modules:
  0.0 193.1 jit_solution(2124407988551133165)
XLA Ops:
  1.5 3.0 %collective-permute-start = (s32[1,24]{1,0:T(1,128)S(1)}, s32[1,24]{1,0:T(1,128)S(1)}, u32[]{:S(2)}, u32[]{:S(2)}) collective-permute-start(s32[1,24]{1,0:T(1,128)S(1)} %reshape.4100), channel_id=1, source_target_pairs={{0,4},{4,0},{8,12},{12,8},{16,20},{20,16},{24,28},{28,24},{1,5},{5... | collective-permute-start | bytes 296 | tf_op jit(solution)/shard_map/ppermute | solution.py:428
  4.5 1.6 collective-permute-start.1
  6.1 1.5 fusion
  7.7 3.1 %collective-permute-start.9 = (s16[8,288,128]{2,1,0:T(8,128)(2,1)S(1)}, s16[8,288,128]{2,1,0:T(8,128)(2,1)S(1)}, u32[]{:S(2)}, u32[]{:S(2)}) collective-permute-start(s16[8,288,128]{2,1,0:T(8,128)(2,1)S(1)} %bitcast.374), channel_id=1, source_target_pairs={{0,16},{4,20},{8,24},{12,28},{16,0},{20,4},{24,8},{28,12},{1,17},{... | collective-permute-start | bytes 1769480 | tf_op jit(solution)/shard_map/ppermute | solution.py:428
  11.9 46.1 %all_gather.3 = f32[64,7]{1,0:T(8,128)S(1)} all-gather(f32[8,7]{1,0:T(8,128)S(1)} %copy-done.37), channel_id=1, replica_groups=mesh['img'=8,'rep'=4] {'img'}, dimensions={0}, use_global_device_ids=true | all-gather | bytes 2016 | tf_op jit(solution)/shard_map/all_gather | solution.py:438
  62.6 4.3 %slot_tables.1.tab_ref = s32[64]{0:T(128)} custom-call(s32[1]{0:T(128)} %bitcast.me_ref, s32[4,24]{1,0:T(4,128)} %pad_add_fusion.list_ref), custom_call_target="tpu_custom_call" | custom-call | tf_op jit(solution)/shard_map/slot_tables/pallas_call | solution.py:96
  67.6 1.6 pack_slots.2
  69.2 3.5 %collective-permute-start.5 = (s16[4,288,128]{2,1,0:T(8,128)(2,1)}, s16[4,288,128]{2,1,0:T(8,128)(2,1)}, u32[]{:S(2)}, u32[]{:S(2)}) collective-permute-start(s16[4,288,128]{2,1,0:T(8,128)(2,1)} %get-tuple-element.33), channel_id=1, source_target_pairs={{0,12},{4,8},{8,4},{12,0},{16,28},{20,24},{24,20},{28,16},{1,13},{... | collective-permute-start | bytes 884744 | tf_op jit(solution)/shard_map/ppermute | solution.py:428
  72.7 1.5 fusion.33
  75.6 2.5 %copy-done.3 = bf16[12,2,3,36864]{3,1,2,0:T(2,128)(2,1)S(1)} copy-done((bf16[12,2,3,36864]{3,1,2,0:T(2,128)(2,1)S(1)}, bf16[12,2,3,36864]{3,1,2,0:T(2,128)(2,1)}, u32[]{:S(2)}) %copy-start.3) | copy-done | bytes 5308440
  78.1 1.8 part_views.1.view_ref
  80.0 2.8 %copy-done = bf16[24,4,288,128]{3,2,1,0:T(8,128)(2,1)} copy-done((bf16[24,4,288,128]{3,2,1,0:T(8,128)(2,1)}, bf16[24,4,288,128]{3,2,1,0:T(8,128)(2,1)S(1)}, u32[]{:S(2)}) %copy-start) | copy-done | bytes 7077912
  83.8 3.0 %copy-done.1 = bf16[24,4,288,128]{3,2,1,0:T(8,128)(2,1)S(1)} copy-done((bf16[24,4,288,128]{3,2,1,0:T(8,128)(2,1)S(1)}, bf16[24,4,288,128]{3,2,1,0:T(8,128)(2,1)}, u32[]{:S(2)}) %copy-start.1) | copy-done | bytes 7077912
  86.9 6.8 %view_terms.2 = (s16[4,288,128]{2,1,0:T(8,128)(2,1)S(1)}, s16[4,288,128]{2,1,0:T(8,128)(2,1)S(1)}, s16[4,288,128]{2,1,0:T(8,128)(2,1)}, s16[4,288,128]{2,1,0:T(8,128)(2,1)S(1)}, f32[24,16,128]{2,1,0:T(8,128)S(1)}) custom-call(s32[64]{0:T(128)S(1)} %copy-done.11, f32[24,16]{1,0:T(8,128)S(1)} %stack.9.coef_ref, f32[1]{0:T(128)} %bitcast.19.row_ref, ...), custom_call_target="tpu_custom_call" | custom-call | tf_op jit(solution)/shard_map/view_terms/pallas_call | solution.py:229
  95.0 3.3 %collective-permute-start.8 = (s16[4,288,128]{2,1,0:T(8,128)(2,1)S(1)}, s16[4,288,128]{2,1,0:T(8,128)(2,1)S(1)}, u32[]{:S(2)}, u32[]{:S(2)}) collective-permute-start(s16[4,288,128]{2,1,0:T(8,128)(2,1)S(1)} %get-tuple-element.37), channel_id=1, source_target_pairs={{0,12},{4,8},{8,4},{12,0},{16,28},{20,24},{24,20},{28,16},{1,13},{... | collective-permute-start | bytes 884744 | tf_op jit(solution)/shard_map/ppermute | solution.py:428
  98.3 1.6 pack_slots.3
  100.5 5.7 %collective-permute-done.6.refs_1_ = s16[4,288,128]{2,1,0:T(8,128)(2,1)S(1)} collective-permute-done((s16[4,288,128]{2,1,0:T(8,128)(2,1)S(1)}, s16[4,288,128]{2,1,0:T(8,128)(2,1)S(1)}, u32[]{:S(2)}, u32[]{:S(2)}) %collective-permute-start.6) | collective-permute-done | bytes 294944 | tf_op jit(solution)/shard_map/ppermute | solution.py:428
  111.5 1.6 fold_local.1.local_ref
  114.5 3.3 %collective-permute-done.12.refs_3_ = s16[4,288,128]{2,1,0:T(8,128)(2,1)S(1)} collective-permute-done((s16[4,288,128]{2,1,0:T(8,128)(2,1)}, s16[4,288,128]{2,1,0:T(8,128)(2,1)S(1)}, u32[]{:S(2)}, u32[]{:S(2)}) %collective-permute-start.12) | collective-permute-done | bytes 294944 | tf_op jit(solution)/shard_map/ppermute | solution.py:428
  117.8 3.0 %copy-done.2 = bf16[24,4,288,128]{3,2,1,0:T(8,128)(2,1)S(1)} copy-done((bf16[24,4,288,128]{3,2,1,0:T(8,128)(2,1)S(1)}, bf16[24,4,288,128]{3,2,1,0:T(8,128)(2,1)}, u32[]{:S(2)}) %copy-start.2) | copy-done | bytes 7077912
  120.8 5.7 %view_terms.3 = (s16[4,288,128]{2,1,0:T(8,128)(2,1)S(1)}, s16[4,288,128]{2,1,0:T(8,128)(2,1)S(1)}, s16[4,288,128]{2,1,0:T(8,128)(2,1)S(1)}, s16[4,288,128]{2,1,0:T(8,128)(2,1)S(1)}, f32[24,16,128]{2,1,0:T(8,128)S(1)}) custom-call(s32[64]{0:T(128)S(1)} %copy-done.11, f32[24,16]{1,0:T(8,128)S(1)} %stack.9.coef_ref, f32[1]{0:T(128)} %bitcast.19.row_ref, ...), custom_call_target="tpu_custom_call" | custom-call | tf_op jit(solution)/shard_map/view_terms/pallas_call | solution.py:229
  138.5 1.5 add_multiply_fusion
  140.0 1.6 add_multiply_fusion.1
  146.7 3.9 %all-to-all-start = ((f32[8,8,7]{1,2,0:T(8,128)}), f32[8,8,7]{1,2,0:T(8,128)}, u32[]{:S(2)}, u32[]{:S(2)}) async-start(f32[8,8,7]{1,2,0:T(8,128)} %copy.769), calls=%async_computation | async-start | bytes 65536 | tf_op jit(solution)/shard_map/all_to_all | solution.py:478
  150.7 1.9 collective-permute-start.13
  152.5 1.5 collective-permute-start.14
  159.5 4.5 %collective-permute-done.15.refs_3_ = s16[4,288,128]{2,1,0:T(8,128)(2,1)S(1)} collective-permute-done((s16[4,288,128]{2,1,0:T(8,128)(2,1)}, s16[4,288,128]{2,1,0:T(8,128)(2,1)S(1)}, u32[]{:S(2)}, u32[]{:S(2)}) %collective-permute-start.15) | collective-permute-done | bytes 294944 | tf_op jit(solution)/shard_map/ppermute | solution.py:428
  164.9 3.1 %fold_slots.1 = s16[8,288,128]{2,1,0:T(8,128)(2,1)} custom-call(s32[64]{0:T(128)S(1)} %copy-done.11, s16[4,288,128]{2,1,0:T(8,128)(2,1)S(1)} %copy-done.9, s16[4,288,128]{2,1,0:T(8,128)(2,1)S(1)} %collective-permute-done.13.refs_1_, s16[4,288,128]{2,1,0:T(8,128)(2,1)S(1)} %collective-permute-done.14.refs_2_, ...), custom_call_target="tpu_custom_call" | custom-call | tf_op jit(solution)/shard_map/fold_slots/pallas_call | solution.py:270
  168.0 2.4 %collective-permute-start.16 = (s16[8,288,128]{2,1,0:T(8,128)(2,1)}, s16[8,288,128]{2,1,0:T(8,128)(2,1)}, u32[]{:S(2)}, u32[]{:S(2)}) collective-permute-start(s16[8,288,128]{2,1,0:T(8,128)(2,1)} %fold_slots.1), channel_id=1, source_target_pairs={{0,16},{4,20},{8,24},{12,28},{16,0},{20,4},{24,8},{28,12},{1,17},{... | collective-permute-start | bytes 1769480 | tf_op jit(solution)/shard_map/ppermute | solution.py:428
  173.1 6.7 %all-reduce = (f32[8,7]{0,1:T(8,128)}, f32[12,7]{0,1:T(8,128)S(1)}) all-reduce(f32[8,7]{0,1:T(8,128)S(1)} %reduce_sum.48, f32[12,7]{0,1:T(8,128)S(1)} %reduce_sum.49), channel_id=1, replica_groups=mesh['img'=8,'rep'=4] {'rep'}, use_global_device_ids=true, to_apply=%region_4.5 | all-reduce | flops 140 | bytes 1120 | tf_op jit(solution)/shard_map/psum | solution.py:483
  183.9 2.8 %collective-permute-done.16.far_ref = s16[8,288,128]{2,1,0:T(8,128)(2,1)} collective-permute-done((s16[8,288,128]{2,1,0:T(8,128)(2,1)}, s16[8,288,128]{2,1,0:T(8,128)(2,1)}, u32[]{:S(2)}, u32[]{:S(2)}) %collective-permute-start.16) | collective-permute-done | bytes 589856 | tf_op jit(solution)/shard_map/ppermute | solution.py:428
  187.9 5.2 %update_depths.1 = (f32[8,36864]{1,0:T(8,128)}, f32[8,36864]{1,0:T(8,128)}, f32[8,36864]{1,0:T(8,128)}) custom-call(f32[8,288,128]{2,1,0:T(8,128)S(1)} %fold_local.1.local_ref, s16[8,288,128]{2,1,0:T(8,128)(2,1)} %collective-permute-done.16.far_ref, f32[8,36864]{1,0:T(8,128)S(1)} %copy-done.4, f32[8,36864]{1,0:T(8,128)S(1)} %copy-done.6, ...), custom_call_target="tpu_custom_call" | custom-call | tf_op jit(solution)/shard_map/update_depths/pallas_call | solution.py:324
  (201 shorter events, 49.5 us)
Async XLA Ops:
  1.5 10.4 %copy-start.37 = (f32[8,7]{1,0:T(8,128)S(1)}, f32[8,7]{1,0:T(8,128)}, u32[]{:S(2)}) copy-start(f32[8,7]{1,0:T(8,128)} %param.16) | copy-start | bytes 676
  1.5 60.4 %collective-permute-start = (s32[1,24]{1,0:T(1,128)S(1)}, s32[1,24]{1,0:T(1,128)S(1)}, u32[]{:S(2)}, u32[]{:S(2)}) collective-permute-start(s32[1,24]{1,0:T(1,128)S(1)} %reshape.4100), channel_id=1, source_target_pairs={{0,4},{4,0},{8,12},{12,8},{16,20},{20,16},{24,28},{28,24},{1,5},{5... | collective-permute-start | bytes 296 | tf_op jit(solution)/shard_map/ppermute | solution.py:428
  4.5 57.4 %collective-permute-start.1 = (s32[1,24]{1,0:T(1,128)S(1)}, s32[1,24]{1,0:T(1,128)S(1)}, u32[]{:S(2)}, u32[]{:S(2)}) collective-permute-start(s32[1,24]{1,0:T(1,128)S(1)} %reshape.4100), channel_id=1, source_target_pairs={{0,8},{4,12},{8,0},{12,4},{16,24},{20,28},{24,16},{28,20},{1,9},{5... | collective-permute-start | bytes 296 | tf_op jit(solution)/shard_map/ppermute | solution.py:428
  6.1 55.9 %collective-permute-start.2 = (s32[1,24]{1,0:T(1,128)S(1)}, s32[1,24]{1,0:T(1,128)S(1)}, u32[]{:S(2)}, u32[]{:S(2)}) collective-permute-start(s32[1,24]{1,0:T(1,128)S(1)} %reshape.4100), channel_id=1, source_target_pairs={{0,12},{4,8},{8,4},{12,0},{16,28},{20,24},{24,20},{28,16},{1,13},{... | collective-permute-start | bytes 296 | tf_op jit(solution)/shard_map/ppermute | solution.py:428
  7.7 67.9 %copy-start.5 = (bf16[12,2,36864]{2,1,0:T(2,128)(2,1)S(1)}, bf16[12,2,36864]{2,1,0:T(2,128)(2,1)}, u32[]{:S(2)}) copy-start(bf16[12,2,36864]{2,1,0:T(2,128)(2,1)} %param.23) | copy-start | bytes 5308420
  7.7 90.5 %collective-permute-start.9 = (s16[8,288,128]{2,1,0:T(8,128)(2,1)S(1)}, s16[8,288,128]{2,1,0:T(8,128)(2,1)S(1)}, u32[]{:S(2)}, u32[]{:S(2)}) collective-permute-start(s16[8,288,128]{2,1,0:T(8,128)(2,1)S(1)} %bitcast.374), channel_id=1, source_target_pairs={{0,16},{4,20},{8,24},{12,28},{16,0},{20,4},{24,8},{28,12},{1,17},{... | collective-permute-start | bytes 1769480 | tf_op jit(solution)/shard_map/ppermute | solution.py:428
  10.8 64.8 %copy-start.39 = (f32[12]{0:T(128)}, f32[12]{0:T(128)S(1)}, u32[]{:S(2)}) copy-start(f32[12]{0:T(128)S(1)} %get-tuple-element.179) | copy-start | bytes 148
  69.2 14.5 %collective-permute-start.3 = (s16[4,288,128]{2,1,0:T(8,128)(2,1)}, s16[4,288,128]{2,1,0:T(8,128)(2,1)S(1)}, u32[]{:S(2)}, u32[]{:S(2)}) collective-permute-start(s16[4,288,128]{2,1,0:T(8,128)(2,1)} %get-tuple-element.31), channel_id=1, source_target_pairs={{0,4},{4,0},{8,12},{12,8},{16,20},{20,16},{24,28},{28,24},{1,5},{5... | collective-permute-start | bytes 884744 | tf_op jit(solution)/shard_map/ppermute | solution.py:428
  69.2 14.6 %collective-permute-start.4 = (s16[4,288,128]{2,1,0:T(8,128)(2,1)}, s16[4,288,128]{2,1,0:T(8,128)(2,1)}, u32[]{:S(2)}, u32[]{:S(2)}) collective-permute-start(s16[4,288,128]{2,1,0:T(8,128)(2,1)} %get-tuple-element.32), channel_id=1, source_target_pairs={{0,8},{4,12},{8,0},{12,4},{16,24},{20,28},{24,16},{28,20},{1,9},{5... | collective-permute-start | bytes 884744 | tf_op jit(solution)/shard_map/ppermute | solution.py:428
  69.2 14.6 %collective-permute-start.5 = (s16[4,288,128]{2,1,0:T(8,128)(2,1)}, s16[4,288,128]{2,1,0:T(8,128)(2,1)}, u32[]{:S(2)}, u32[]{:S(2)}) collective-permute-start(s16[4,288,128]{2,1,0:T(8,128)(2,1)} %get-tuple-element.33), channel_id=1, source_target_pairs={{0,12},{4,8},{8,4},{12,0},{16,28},{20,24},{24,20},{28,16},{1,13},{... | collective-permute-start | bytes 884744 | tf_op jit(solution)/shard_map/ppermute | solution.py:428
  86.8 19.4 %copy-start.47 = (s32[24]{0:T(128)S(1)}, s32[24]{0:T(128)}, u32[]{:S(2)}) copy-start(s32[24]{0:T(128)} %copy-done.46) | copy-start | bytes 292
  86.8 20.0 %copy-start.38 = (f32[8,7]{1,0:T(8,128)S(1)}, f32[8,7]{1,0:T(8,128)}, u32[]{:S(2)}) copy-start(f32[8,7]{1,0:T(8,128)} %param.16) | copy-start | bytes 676
  86.8 20.7 %copy-start.44 = (f32[8,7]{1,0:T(8,128)S(1)}, f32[8,7]{1,0:T(8,128)}, u32[]{:S(2)}) copy-start(f32[8,7]{1,0:T(8,128)} %param.17) | copy-start | bytes 676
  86.8 21.4 %copy-start.45 = (f32[8,7]{1,0:T(8,128)S(1)}, f32[8,7]{1,0:T(8,128)}, u32[]{:S(2)}) copy-start(f32[8,7]{1,0:T(8,128)} %param.18) | copy-start | bytes 676
  93.6 12.6 %collective-permute-start.6 = (s16[4,288,128]{2,1,0:T(8,128)(2,1)S(1)}, s16[4,288,128]{2,1,0:T(8,128)(2,1)S(1)}, u32[]{:S(2)}, u32[]{:S(2)}) collective-permute-start(s16[4,288,128]{2,1,0:T(8,128)(2,1)S(1)} %get-tuple-element.35), channel_id=1, source_target_pairs={{0,4},{4,0},{8,12},{12,8},{16,20},{20,16},{24,28},{28,24},{1,5},{5... | collective-permute-start | bytes 884744 | tf_op jit(solution)/shard_map/ppermute | solution.py:428
  94.8 15.4 %collective-permute-start.7 = (s16[4,288,128]{2,1,0:T(8,128)(2,1)}, s16[4,288,128]{2,1,0:T(8,128)(2,1)S(1)}, u32[]{:S(2)}, u32[]{:S(2)}) collective-permute-start(s16[4,288,128]{2,1,0:T(8,128)(2,1)} %get-tuple-element.36), channel_id=1, source_target_pairs={{0,8},{4,12},{8,0},{12,4},{16,24},{20,28},{24,16},{28,20},{1,9},{5... | collective-permute-start | bytes 884744 | tf_op jit(solution)/shard_map/ppermute | solution.py:428
  95.0 16.6 %collective-permute-start.8 = (s16[4,288,128]{2,1,0:T(8,128)(2,1)S(1)}, s16[4,288,128]{2,1,0:T(8,128)(2,1)S(1)}, u32[]{:S(2)}, u32[]{:S(2)}) collective-permute-start(s16[4,288,128]{2,1,0:T(8,128)(2,1)S(1)} %get-tuple-element.37), channel_id=1, source_target_pairs={{0,12},{4,8},{8,4},{12,0},{16,28},{20,24},{24,20},{28,16},{1,13},{... | collective-permute-start | bytes 884744 | tf_op jit(solution)/shard_map/ppermute | solution.py:428
  99.9 14.6 %collective-permute-start.10 = (s16[4,288,128]{2,1,0:T(8,128)(2,1)}, s16[4,288,128]{2,1,0:T(8,128)(2,1)S(1)}, u32[]{:S(2)}, u32[]{:S(2)}) collective-permute-start(s16[4,288,128]{2,1,0:T(8,128)(2,1)} %get-tuple-element.39), channel_id=1, source_target_pairs={{0,4},{4,0},{8,12},{12,8},{16,20},{20,16},{24,28},{28,24},{1,5},{5... | collective-permute-start | bytes 884744 | tf_op jit(solution)/shard_map/ppermute | solution.py:428
  99.9 14.6 %collective-permute-start.11 = (s16[4,288,128]{2,1,0:T(8,128)(2,1)}, s16[4,288,128]{2,1,0:T(8,128)(2,1)S(1)}, u32[]{:S(2)}, u32[]{:S(2)}) collective-permute-start(s16[4,288,128]{2,1,0:T(8,128)(2,1)} %get-tuple-element.40), channel_id=1, source_target_pairs={{0,8},{4,12},{8,0},{12,4},{16,24},{20,28},{24,16},{28,20},{1,9},{5... | collective-permute-start | bytes 884744 | tf_op jit(solution)/shard_map/ppermute | solution.py:428
  106.2 11.6 %collective-permute-start.12 = (s16[4,288,128]{2,1,0:T(8,128)(2,1)}, s16[4,288,128]{2,1,0:T(8,128)(2,1)S(1)}, u32[]{:S(2)}, u32[]{:S(2)}) collective-permute-start(s16[4,288,128]{2,1,0:T(8,128)(2,1)} %get-tuple-element.41), channel_id=1, source_target_pairs={{0,12},{4,8},{8,4},{12,0},{16,28},{20,24},{24,20},{28,16},{1,13},{... | collective-permute-start | bytes 884744 | tf_op jit(solution)/shard_map/ppermute | solution.py:428
  120.8 10.0 %copy-start.20 = (f32[24,1]{1,0:T(8,128)S(1)}, f32[24,1]{1,0:T(8,128)}, u32[]{:S(2)}) copy-start(f32[24,1]{1,0:T(8,128)} %copy-done.19) | copy-start | bytes 292
  120.8 17.6 %copy-start.16 = (f32[7,24]{0,1:T(8,128)S(1)}, f32[7,24]{0,1:T(8,128)}, u32[]{:S(2)}) copy-start(f32[7,24]{0,1:T(8,128)} %copy-done.15) | copy-start | bytes 2020
  127.3 12.7 %copy-start.8 = (s16[4,288,128]{2,1,0:T(8,128)(2,1)}, s16[4,288,128]{2,1,0:T(8,128)(2,1)S(1)}, u32[]{:S(2)}) copy-start(s16[4,288,128]{2,1,0:T(8,128)(2,1)S(1)} %get-tuple-element.42.refs_0_) | copy-start | bytes 884740
  127.3 12.7 %copy-start.12 = (s16[4,288,128]{2,1,0:T(8,128)(2,1)}, s16[4,288,128]{2,1,0:T(8,128)(2,1)S(1)}, u32[]{:S(2)}) copy-start(s16[4,288,128]{2,1,0:T(8,128)(2,1)S(1)} %get-tuple-element.45) | copy-start | bytes 884740
  127.3 12.7 %copy-start.13 = (s16[4,288,128]{2,1,0:T(8,128)(2,1)}, s16[4,288,128]{2,1,0:T(8,128)(2,1)S(1)}, u32[]{:S(2)}) copy-start(s16[4,288,128]{2,1,0:T(8,128)(2,1)S(1)} %get-tuple-element.44) | copy-start | bytes 884740
  140.0 46.6 %copy-start.4 = (f32[8,36864]{1,0:T(8,128)S(1)}, f32[8,36864]{1,0:T(8,128)}, u32[]{:S(2)}) copy-start(f32[8,36864]{1,0:T(8,128)} %x_ref.1) | copy-start | bytes 3538948
  140.0 46.6 %copy-start.6 = (f32[8,36864]{1,0:T(8,128)S(1)}, f32[8,36864]{1,0:T(8,128)}, u32[]{:S(2)}) copy-start(f32[8,36864]{1,0:T(8,128)} %m_ref.1) | copy-start | bytes 3538948
  146.7 25.6 %all-to-all-start = ((f32[8,8,7]{1,2,0:T(8,128)}), f32[8,8,7]{1,2,0:T(8,128)}, u32[]{:S(2)}, u32[]{:S(2)}) async-start(f32[8,8,7]{1,2,0:T(8,128)} %copy.769), calls=%async_computation | async-start | bytes 65536 | tf_op jit(solution)/shard_map/all_to_all | solution.py:478
  150.7 7.4 %collective-permute-start.13 = (s16[4,288,128]{2,1,0:T(8,128)(2,1)}, s16[4,288,128]{2,1,0:T(8,128)(2,1)S(1)}, u32[]{:S(2)}, u32[]{:S(2)}) collective-permute-start(s16[4,288,128]{2,1,0:T(8,128)(2,1)} %copy-done.14), channel_id=1, source_target_pairs={{0,4},{4,0},{8,12},{12,8},{16,20},{20,16},{24,28},{28,24},{1,5},{5... | collective-permute-start | bytes 884744 | tf_op jit(solution)/shard_map/ppermute | solution.py:428
  152.5 6.9 %collective-permute-start.14 = (s16[4,288,128]{2,1,0:T(8,128)(2,1)}, s16[4,288,128]{2,1,0:T(8,128)(2,1)S(1)}, u32[]{:S(2)}, u32[]{:S(2)}) collective-permute-start(s16[4,288,128]{2,1,0:T(8,128)(2,1)} %copy-done.13), channel_id=1, source_target_pairs={{0,8},{4,12},{8,0},{12,4},{16,24},{20,28},{24,16},{28,20},{1,9},{5... | collective-permute-start | bytes 884744 | tf_op jit(solution)/shard_map/ppermute | solution.py:428
  154.0 9.9 %collective-permute-start.15 = (s16[4,288,128]{2,1,0:T(8,128)(2,1)}, s16[4,288,128]{2,1,0:T(8,128)(2,1)S(1)}, u32[]{:S(2)}, u32[]{:S(2)}) collective-permute-start(s16[4,288,128]{2,1,0:T(8,128)(2,1)} %copy-done.12), channel_id=1, source_target_pairs={{0,12},{4,8},{8,4},{12,0},{16,28},{20,24},{24,20},{28,16},{1,13},{... | collective-permute-start | bytes 884744 | tf_op jit(solution)/shard_map/ppermute | solution.py:428
  168.0 18.7 %collective-permute-start.16 = (s16[8,288,128]{2,1,0:T(8,128)(2,1)}, s16[8,288,128]{2,1,0:T(8,128)(2,1)}, u32[]{:S(2)}, u32[]{:S(2)}) collective-permute-start(s16[8,288,128]{2,1,0:T(8,128)(2,1)} %fold_slots.1), channel_id=1, source_target_pairs={{0,16},{4,20},{8,24},{12,28},{16,0},{20,4},{24,8},{28,12},{1,17},{... | collective-permute-start | bytes 1769480 | tf_op jit(solution)/shard_map/ppermute | solution.py:428
  (34 other events, 127.0 us)

commit v2 on v1

v2 whole, which is shorter than its diff:
```python
import functools
import math

import jax
import jax.numpy as jnp
from jax import lax
from jax.experimental import pallas as pl
from jax.experimental.pallas import tpu as pltpu
from jax.sharding import PartitionSpec as P

HEIGHT = 288
WIDTH = 512
START = 50
NPIX = 147456
LANES = 128
SWAP_PARTS = 2

beta_one = 0.9
beta_two = 0.999
adam_eps = 1e-08
depth_rate = 0.05
camera_rate = 0.01
pose_rate = 0.01

DEPTH_MID = 2.25
DEPTH_STEP = 1.75 / 32766.0
VIEW_BOUND = 340.0
CODE_UNIT = 8.0
INTS = jnp.int16
SUMS = 11
COEFS = 16

SMEM = pl.BlockSpec(memory_space=pltpu.SMEM)
VMEM = pl.BlockSpec(memory_space=pltpu.VMEM)
COST = pl.CostEstimate(flops=1, bytes_accessed=1, transcendentals=0)
PARAMS = pltpu.CompilerParams(vmem_limit_bytes=32 * 1024 * 1024)


def code_scale(bound):
    return 32766.0 / math.log2(1.0 + bound / CODE_UNIT)


def encode(magnitude, negative, bound):
    steps = (jnp.log2(1.0 + magnitude) * code_scale(bound) + 0.5).astype(jnp.int32)
    steps = jnp.minimum(steps, 32767)
    return jnp.where(negative, -steps, steps).astype(INTS)


def decode(code, bound):
    steps = code.astype(jnp.int32)
    size = jnp.abs(steps).astype(jnp.float32) * (1.0 / code_scale(bound))
    value = CODE_UNIT * jnp.exp2(size) - CODE_UNIT
    return jnp.where(steps < 0, -value, value)


def letter_kernel(image_ref, camera_ref, out_ref):
    shards, rows, _ = out_ref.shape
    lane = lax.broadcasted_iota(jnp.int32, (1, LANES), 1)
    names = jnp.zeros((1, LANES), jnp.int32)
    for r in range(2 * image_ref.shape[1]):
        names = jnp.where(lane == r, image_ref[r % 2, r // 2], names)
    for i in range(shards):
        out_ref[i, 0 : rows - 1, 0:7] = camera_ref[...]
        out_ref[i, rows - 1 : rows] = names.astype(jnp.float32)


def letters_of(pair_images, cameras, shards):
    images = cameras.shape[0]
    return pl.pallas_call(
        letter_kernel,
        out_shape=jax.ShapeDtypeStruct((shards, images + 1, LANES), jnp.float32),
        in_specs=[SMEM, VMEM],
        out_specs=VMEM,
        cost_estimate=COST,
        name="letters_of",
    )(pair_images, cameras)


def over(number, size):
    if size & (size - 1):
        return lax.div(number, size)
    return lax.shift_right_logical(number, size.bit_length() - 1)


def table_kernel(half, cap, images, me_ref, *refs):
    list_ref, tab_ref, count_ref = refs
    me = me_ref[0]
    shards = 2 * half
    asked = shards * cap
    requests = list_ref.shape[1]

    @pl.loop(0, 2 * asked, unroll=8)
    def _(i):
        tab_ref[i] = -1

    tab_ref[2 * asked] = me & (half - 1)

    @pl.loop(0, 2 * shards, unroll=8)
    def _(i):
        count_ref[i] = 0

    def put(cell, value):
        rank = count_ref[cell]
        tab_ref[cell * cap + jnp.minimum(rank, cap - 1)] = value
        count_ref[cell] = rank + 1

    for k in range(half):
        asker = me ^ k

        @pl.loop(0, requests, unroll=2)
        def _(r):
            image = list_ref[asker, r]
            owner = over(image, images)
            mine = owner == me

            @pl.when(mine | (owner == (me ^ half)))
            def _():
                put(jnp.where(mine, k, half + k), image - owner * images)

    @pl.loop(0, requests, unroll=2)
    def _(r):
        image = list_ref[me, r]
        owner = over(image, images)
        put(shards + (owner ^ me), r)


def slot_tables(me, lists, half, cap, images):
    return pl.pallas_call(
        functools.partial(table_kernel, half, cap, images),
        out_shape=jax.ShapeDtypeStruct((4 * half * cap + 1,), jnp.int32),
        in_specs=[SMEM, SMEM],
        out_specs=SMEM,
        scratch_shapes=[pltpu.SMEM((4 * half,), jnp.int32)],
        cost_estimate=COST,
        name="slot_tables",
    )(me, lists)


def pack_kernel(first, half, tab_ref, *refs):
    map_refs, slot_refs = refs[:-half], refs[-half:]
    rows = map_refs[0].shape[1]
    for k, slot_ref in enumerate(slot_refs):

        @pl.loop(0, slot_ref.shape[0])
        def _(c):
            image = jnp.maximum(tab_ref[first + k * slot_ref.shape[0] + c], 0)
            for i, map_ref in enumerate(map_refs):
                slot_ref[c, i * rows : (i + 1) * rows] = map_ref[image]


def pack_slots(table, maps, first, half, cap):
    rows = sum(part.shape[1] for part in maps)
    return pl.pallas_call(
        functools.partial(pack_kernel, first, half),
        out_shape=[jax.ShapeDtypeStruct((cap, rows, LANES), INTS)] * half,
        in_specs=[SMEM] + [VMEM] * len(maps),
        out_specs=[VMEM] * half,
        compiler_params=PARAMS,
        cost_estimate=COST,
        name="pack_slots",
    )(table, *maps)


def columns_and_lines(top):
    across = WIDTH // LANES
    line = lax.broadcasted_iota(jnp.int32, (16, LANES), 0)
    lane = lax.broadcasted_iota(jnp.int32, (16, LANES), 1)
    columns = ((line % across) * LANES + lane).astype(jnp.float32) + (0.5 - 0.5 * WIDTH)
    return columns, (line // across).astype(jnp.float32) + top


def ray_start(columns, lines, coef):
    ray = [columns * coef(j) + (lines * coef(3 + j) + coef(6 + j)) for j in range(3)]
    step = [coef(3 + j) * (16.0 * LANES / WIDTH) for j in range(3)]
    return ray, step


def prepare_kernel(row_ref, coef_ref, point_ref, weight_ref, view_ref, slope_ref, wide):
    rows = view_ref.shape[2]
    columns, lines = columns_and_lines(row_ref[0])

    @pl.loop(0, point_ref.shape[0])
    def _(pair):
        for q in range(4):
            source = point_ref.at[pair, q] if q < 3 else weight_ref.at[pair]
            wide[q] = source[...].astype(jnp.float32)
        for v in range(2):
            view = 2 * pair + v

            def coef(i):
                return coef_ref[view, i]

            ray, step = ray_start(columns, lines, coef)
            shift = [coef(9 + j) for j in range(3)]
            gain = coef(12)
            for t in range(0, rows, 16):
                here = slice(t, t + 16)
                part = [wide[q, pl.ds(2 * t + v, 16, stride=2), :] for q in range(4)]
                for q in range(4):
                    view_ref[view, q, here] = part[q].astype(jnp.bfloat16)
                weight = part[3] * gain
                slope = weight * (ray[0] * ray[0] + ray[1] * ray[1] + ray[2] * ray[2])
                rest = [ray[j] * (shift[j] - part[j]) for j in range(3)]
                slope_ref[view, 0, here] = slope * DEPTH_STEP
                slope_ref[view, 1, here] = slope * DEPTH_MID + weight * (
                    rest[0] + rest[1] + rest[2]
                )
                ray = [ray[j] + step[j] for j in range(3)]


def prepare_views(row, coefs, points, weights):
    pairs, _, _, pixels = points.shape
    rows = pixels // LANES
    points = (
        points.transpose(0, 2, 1, 3)
        .reshape(pairs, 3, 2, rows, LANES)
        .transpose(0, 1, 3, 2, 4)
        .reshape(pairs, 3, 2 * rows, LANES)
    )
    weights = (
        weights.reshape(pairs, 2, rows, LANES).transpose(0, 2, 1, 3).reshape(pairs, 2 * rows, LANES)
    )
    return pl.pallas_call(
        prepare_kernel,
        out_shape=[
            jax.ShapeDtypeStruct((2 * pairs, 4, rows, LANES), jnp.bfloat16),
            jax.ShapeDtypeStruct((2 * pairs, 2, rows, LANES), jnp.float32),
        ],
        in_specs=[SMEM, SMEM, VMEM, VMEM],
        out_specs=[VMEM, VMEM],
        scratch_shapes=[pltpu.VMEM((4, 2 * rows, LANES), jnp.float32)],
        compiler_params=PARAMS,
        cost_estimate=COST,
        name="prepare_views",
    )(row, coefs, points, weights)


def slots_at(refs, k, tab_ref):
    return refs[k] if len(refs) > 1 else refs[0].at[k ^ tab_ref[tab_ref.shape[0] - 1]]


def grad_kernel(first, half, cap, tab_ref, slope_ref, *refs):
    depth_refs, grad_refs = refs[:half], refs[half:]
    rows = depth_refs[0].shape[1]
    for k in range(half):
        depth_ref = depth_refs[k]
        grad_ref = slots_at(grad_refs, k, tab_ref)

        @pl.loop(0, cap)
        def _(c):
            view = tab_ref[first + k * cap + c]

            @pl.when(view >= 0)
            def _():
                for t in range(0, rows, 16):
                    here = slice(t, t + 16)
                    code = depth_ref[c, here].astype(jnp.int32).astype(jnp.float32)
                    along = code * slope_ref[view, 0, here] + slope_ref[view, 1, here]
                    grad_ref[c, here] = encode(jnp.abs(along), along < 0.0, VIEW_BOUND)


def depth_grads(table, slopes, depths, first, half, cap, by_rank):
    rows = depths[0].shape[1]
    if by_rank:
        out = [jax.ShapeDtypeStruct((half, cap, rows, LANES), INTS)]
    else:
        out = [jax.ShapeDtypeStruct((cap, rows, LANES), INTS)] * half
    return pl.pallas_call(
        functools.partial(grad_kernel, first, half, cap),
        out_shape=out,
        in_specs=[SMEM] + [VMEM] * (1 + half),
        out_specs=[VMEM] * len(out),
        compiler_params=PARAMS,
        cost_estimate=COST,
        name="depth_grads",
    )(table, slopes, *depths)


def sum_kernel(first, half, cap, tab_ref, coef_ref, row_ref, view_ref, *refs):
    depth_refs = refs[:-2]
    sum_ref, depth_all = refs[-2:]
    slots, rows, _ = depth_all.shape
    for k in range(half):
        depth_ref = depth_refs[k]
        depth_all[k * cap : (k + 1) * cap] = depth_ref[...]
    sum_ref[...] = jnp.zeros_like(sum_ref)
    columns, lines = columns_and_lines(row_ref[0])

    @pl.loop(0, slots)
    def _(s):
        view = tab_ref[first + s]

        @pl.when(view >= 0)
        def _():
            def coef(i):
                return coef_ref[view, i]

            ray, step = ray_start(columns, lines, coef)
            shift = [coef(9 + j) for j in range(3)]
            totals = [None] * SUMS

            def add(i, value):
                value = value[:8] + value[8:]
                totals[i] = value if totals[i] is None else totals[i] + value

            for t in range(0, rows, 16):
                here = slice(t, t + 16)
                point = [view_ref[view, j, here].astype(jnp.float32) for j in range(3)]
                weight = view_ref[view, 3, here].astype(jnp.float32)
                depth = (
                    depth_all[s, here].astype(jnp.int32).astype(jnp.float32) * DEPTH_STEP
                    + DEPTH_MID
                )
                pull = [weight * (depth * ray[j] + (shift[j] - point[j])) for j in range(3)]
                along = pull[0] * ray[0] + pull[1] * ray[1] + pull[2] * ray[2]
                for j in range(3):
                    add(j, pull[j])
                    add(8 + j, depth * pull[j])
                    a, b = (j + 1) % 3, (j + 2) % 3
                    add(3 + j, point[a] * pull[b] - point[b] * pull[a])
                add(6, point[0] * pull[0] + point[1] * pull[1] + point[2] * pull[2])
                add(7, depth * along)
                ray = [ray[j] + step[j] for j in range(3)]
            for i in range(SUMS):
                sum_ref[view, i : i + 1] = jnp.sum(totals[i], axis=0, keepdims=True)


def view_sums(table, coefs, row, views, depths, first, half, cap):
    rows = depths[0].shape[1]
    return pl.pallas_call(
        functools.partial(sum_kernel, first, half, cap),
        out_shape=jax.ShapeDtypeStruct((views.shape[0], COEFS, LANES), jnp.float32),
        in_specs=[SMEM, SMEM, SMEM] + [VMEM] * (1 + len(depths)),
        out_specs=VMEM,
        scratch_shapes=[pltpu.VMEM((half * cap, rows, LANES), INTS)],
        compiler_params=PARAMS,
        cost_estimate=COST,
        name="view_sums",
    )(table, coefs, row, views, *depths)


def fold(first, half, cap, tab_ref, slot_refs, total_ref):
    total_ref[...] = jnp.zeros_like(total_ref)
    for k in range(half):
        slot_ref = slots_at(slot_refs, k, tab_ref)

        @pl.loop(0, cap)
        def _(c):
            image = tab_ref[first + k * cap + c]

            @pl.when(image >= 0)
            def _():
                total_ref[image] += decode(slot_ref[c], VIEW_BOUND)


def fold_kernel(first, cap, bound, half, tab_ref, *refs):
    slot_refs, out_refs, total = refs[:half], refs[half:-1], refs[-1]
    fold(first, half, cap, tab_ref, slot_refs, total)
    rows = out_refs[0].shape[1]
    for part, out_ref in enumerate(out_refs):

        @pl.loop(0, total.shape[0])
        def _(i):
            value = total[i, part * rows : (part + 1) * rows]
            out_ref[i] = encode(jnp.abs(value) * (1.0 / CODE_UNIT), value < 0.0, bound)


def fold_slots(table, slots, first, images, cap, bound, parts):
    rows = slots[0].shape[1]
    return pl.pallas_call(
        functools.partial(fold_kernel, first, cap, bound, len(slots)),
        out_shape=[jax.ShapeDtypeStruct((images, rows // parts, LANES), INTS)] * parts,
        in_specs=[SMEM] + [VMEM] * len(slots),
        out_specs=[VMEM] * parts,
        scratch_shapes=[pltpu.VMEM((images, rows, LANES), jnp.float32)],
        compiler_params=PARAMS,
        cost_estimate=COST,
        name="fold_slots",
    )(table, *slots)


def local_kernel(first, half, cap, tab_ref, *refs):
    fold(first, half, cap, tab_ref, refs[:-1], refs[-1])


def fold_local(table, slots, first, images, half, cap):
    rows = slots[0].shape[-2]
    return pl.pallas_call(
        functools.partial(local_kernel, first, half, cap),
        out_shape=jax.ShapeDtypeStruct((images, rows, LANES), jnp.float32),
        in_specs=[SMEM] + [VMEM] * len(slots),
        out_specs=VMEM,
        compiler_params=PARAMS,
        cost_estimate=COST,
        name="fold_local",
    )(table, *slots)


def adam_step(values, moment, second, gradient, step_rate):
    step_count = START + 1
    moment = beta_one * moment + (1.0 - beta_one) * gradient
    second = beta_two * second + (1.0 - beta_two) * gradient * gradient
    fix_one = 1.0 - beta_one**step_count
    fix_two = 1.0 - beta_two**step_count
    values = values - step_rate * (moment / fix_one) / (jnp.sqrt(second / fix_two) + adam_eps)
    return (values, moment, second)


def depth_kernel(bound, local_ref, far_ref, x_ref, m_ref, s_ref, *refs):
    nx_ref, nm_ref, ns_ref, grad = refs[-4:]
    images, rows, _ = local_ref.shape
    for i in range(images):
        grad[i * rows : (i + 1) * rows] = local_ref[i] + decode(far_ref[i], bound)
    for t in range(rows):
        here = slice(t * LANES, (t + 1) * LANES)
        gradient = grad[pl.ds(t, images, stride=rows), :]
        nx_ref[:, here], nm_ref[:, here], ns_ref[:, here] = adam_step(
            x_ref[:, here], m_ref[:, here], s_ref[:, here], gradient, depth_rate
        )


def update_depths(local, far, values, moment, second, bound, chunk, done):
    images, rows, _ = far.shape
    block = 48
    steps = rows // block
    first = chunk * steps
    wide = pl.BlockSpec((images, block * LANES), lambda t: (0, first + t))
    return pl.pallas_call(
        functools.partial(depth_kernel, bound),
        grid=(steps,),
        out_shape=[jax.ShapeDtypeStruct(values.shape, jnp.float32)] * 3,
        in_specs=[
            pl.BlockSpec((images, block, LANES), lambda t: (0, first + t, 0)),
            pl.BlockSpec((images, block, LANES), lambda t: (0, t, 0)),
            wide,
            wide,
            wide,
        ]
        + [pl.BlockSpec(memory_space=pl.ANY)] * len(done),
        out_specs=[wide, wide, wide],
        input_output_aliases={5 + i: i for i in range(len(done))},
        scratch_shapes=[pltpu.VMEM((images * block, LANES), jnp.float32)],
        compiler_params=PARAMS,
        cost_estimate=COST,
        name="update_depths",
    )(local, far, values, moment, second, *done)


def rotation(first, middle, last):
    inverse = 1.0 / (1.0 + first * first + middle * middle + last * last)
    return (
        (1.0 + first * first - middle * middle - last * last) * inverse,
        2.0 * (first * middle - last) * inverse,
        2.0 * (first * last + middle) * inverse,
        2.0 * (first * middle + last) * inverse,
        (1.0 - first * first + middle * middle - last * last) * inverse,
        2.0 * (middle * last - first) * inverse,
        2.0 * (first * last - middle) * inverse,
        2.0 * (middle * last + first) * inverse,
        (1.0 - first * first - middle * middle + last * last) * inverse,
    )


def cross(a, b):
    return [a[(j + 1) % 3] * b[(j + 2) % 3] - a[(j + 2) % 3] * b[(j + 1) % 3] for j in range(3)]


def turn_gradient(spin, torque):
    factor = 2.0 / (1.0 + spin[0] * spin[0] + spin[1] * spin[1] + spin[2] * spin[2])
    swing = cross(spin, torque)
    return [factor * (torque[j] + swing[j]) for j in range(3)]


def view_parts(cam_ref, pose_ref):
    cams = [cam_ref[:, i : i + 1] for i in range(7)]
    poses = [pose_ref[:, i : i + 1] for i in range(7)]
    cam = rotation(cams[1], cams[2], cams[3])
    pose = rotation(poses[0], poses[1], poses[2])
    scale = jnp.exp(poses[6])
    back = jnp.exp(-poses[6])
    gap = [cams[4 + k] - poses[3 + k] for k in range(3)]
    both = [
        [sum(pose[3 * k + j] * cam[3 * k + i] for k in range(3)) for i in range(3)] for j in range(3)
    ]
    matrix = [[both[j][i] * back for i in range(3)] for j in range(3)]
    shift = [sum(pose[3 * k + j] * gap[k] for k in range(3)) * back for j in range(3)]
    return cams, poses, both, pose, scale, matrix, shift


def coef_kernel(images, image_ref, all_ref, pair_ref, out_ref, cam_ref, pose_ref):
    views = cam_ref.shape[0]
    for r in range(views):
        image = image_ref[r % 2, r // 2]
        owner = over(image, images)
        cam_ref[r : r + 1, :] = all_ref[owner, pl.ds(image - owner * images, 1), 0:7]
        pose_ref[r : r + 1, :] = pair_ref[r // 2 : r // 2 + 1, :]
    cams, _, _, _, scale, matrix, shift = view_parts(cam_ref, pose_ref)
    inverse_focal = jnp.exp(-cams[0]) * (1.0 / WIDTH)
    rows = [matrix[j][0] * inverse_focal for j in range(3)]
    rows += [matrix[j][1] * inverse_focal for j in range(3)]
    rows += [matrix[j][2] for j in range(3)]
    rows += shift
    rows += [scale * scale * (1.0 / CODE_UNIT)]
    for i, row in enumerate(rows):
        out_ref[:, i : i + 1] = row


def view_coefs(pair_images, mail, pair_poses, images):
    views = 2 * pair_poses.shape[0]
    return pl.pallas_call(
        functools.partial(coef_kernel, images),
        out_shape=[
            jax.ShapeDtypeStruct((views, COEFS), jnp.float32),
            jax.ShapeDtypeStruct((views, 7), jnp.float32),
            jax.ShapeDtypeStruct((views, 7), jnp.float32),
        ],
        in_specs=[SMEM, VMEM, VMEM],
        out_specs=[VMEM, VMEM, VMEM],
        cost_estimate=COST,
        name="view_coefs",
    )(pair_images, mail, pair_poses)


def term_kernel(image_ref, cam_ref, pose_ref, *refs):
    cams, poses, both, pose, scale, matrix, shift = view_parts(cam_ref, pose_ref)
    sum_refs, (small_ref, terms, turns) = refs[:-3], refs[-3:]
    views = cam_ref.shape[0]
    sums = jnp.sum(sum(ref[...] for ref in sum_refs), axis=2)
    sums = [sums[:, i : i + 1] for i in range(SUMS)]
    square = scale * scale
    force, torque, stretch, drawn, lever = sums[0:3], sums[3:6], sums[6], sums[7], sums[8:11]
    push = [scale * sum(pose[3 * k + j] * force[j] for j in range(3)) for k in range(3)]
    swing = cross(shift, force)
    arm = [torque[j] - swing[j] for j in range(3)]
    camera_torque = [square * sum(both[j][i] * arm[j] for j in range(3)) for i in range(3)]
    pose_torque = [-square * torque[j] for j in range(3)]
    focal = -square * (drawn - sum(matrix[j][2] * lever[j] for j in range(3)))
    camera = [focal] + turn_gradient(cams[1:4], camera_torque) + push
    posed = (
        turn_gradient(poses[0:3], pose_torque) + [-value for value in push] + [-square * stretch]
    )
    terms[...] = jnp.zeros_like(terms)
    turns[...] = jnp.zeros_like(turns)
    for i in range(7):
        terms[:, i : i + 1] = camera[i]
        turns[:, i : i + 1] = posed[i]
    both_views = turns[pl.ds(0, views // 2, stride=2), :] + turns[pl.ds(1, views // 2, stride=2), :]
    images = small_ref.shape[0] - views // 2
    small_ref[0:images] = jnp.zeros((images, 7), jnp.float32)
    for r in range(views):
        here = pl.ds(image_ref[r % 2, r // 2], 1)
        small_ref[here, :] += terms[r : r + 1, 0:7]
    small_ref[images:] = both_views[:, 0:7]


def view_terms(pair_images, cams, poses, sums, images):
    views = cams.shape[0]
    return pl.pallas_call(
        term_kernel,
        out_shape=jax.ShapeDtypeStruct((images + views // 2, 7), jnp.float32),
        in_specs=[SMEM] + [VMEM] * (2 + len(sums)),
        out_specs=VMEM,
        scratch_shapes=[pltpu.VMEM((views, LANES), jnp.float32)] * 2,
        cost_estimate=COST,
        name="view_terms",
    )(pair_images, cams, poses, *sums)


def small_kernel(mail_ref, pose_ref, *refs):
    values, outs = refs[:6], refs[6:]
    camera_grad = jnp.sum(mail_ref[...], axis=0) * (1.0 / NPIX)
    pose_grad = pose_ref[...] * (1.0 / NPIX)
    for i, (gradient, rate) in enumerate(((camera_grad, camera_rate), (pose_grad, pose_rate))):
        new = adam_step(*(ref[...] for ref in values[3 * i : 3 * i + 3]), gradient, rate)
        for ref, value in zip(outs[3 * i : 3 * i + 3], new):
            ref[...] = value


def update_small(mail, pose_grad, cameras, poses):
    return pl.pallas_call(
        small_kernel,
        out_shape=[jax.ShapeDtypeStruct(value.shape, jnp.float32) for value in cameras + poses],
        in_specs=[VMEM] * 8,
        out_specs=[VMEM] * 6,
        cost_estimate=COST,
        name="update_small",
    )(mail, pose_grad, *cameras, *poses)


def body(
    pair_images,
    depths,
    depth_moment,
    depth_second,
    cameras,
    camera_moment,
    camera_second,
    pair_poses,
    pair_moment,
    pair_second,
    pointmaps,
    confidence,
):
    shards = lax.axis_size("img")
    half = shards // 2
    me = lax.axis_index("img")
    rep = lax.axis_index("rep")
    images, row_len = depths.shape
    pairs = pair_images.shape[0]
    requests = 2 * pairs
    cap = max(2, 3 * pairs // shards)
    rows = row_len // LANES
    far_bound = VIEW_BOUND * half * cap

    def swap(value, k):
        return lax.ppermute(value, "img", [(i, i ^ k) for i in range(shards)])

    slots = half * cap

    def exchange(values):
        return [values[0]] + [swap(values[k], k) for k in range(1, half)]

    tie = lax.optimization_barrier

    names = pair_images.T
    letters = letters_of(names, cameras, shards)
    codes = jnp.round((depths - DEPTH_MID) * (1.0 / DEPTH_STEP)).astype(INTS)
    codes = codes.reshape(images, rows, LANES)
    size = rows // SWAP_PARTS
    parts = [codes[:, c * size : (c + 1) * size] for c in range(SWAP_PARTS)]
    letters, parts[1:] = tie((letters, parts[1:]))
    mail = lax.all_to_all(letters, "img", 0, 0, tiled=True)
    far = [swap(part, half) for part in parts]

    lists = mail[:, images, :requests].astype(jnp.int32)
    table = slot_tables(me.reshape(1), lists, half, cap, images)
    near = pack_slots(table, [codes], 0, half, cap)
    mail, near = tie((mail, near))
    near = exchange(near)
    coefs, cams, poses = view_coefs(names, mail, pair_poses, images)
    row = rep * (row_len // WIDTH)
    row = (row.astype(jnp.float32) + (0.5 - 0.5 * HEIGHT)).reshape(1)
    far, coefs = tie((far, coefs))
    asked = pack_slots(table, far, slots, half, cap)
    coefs, asked = tie((coefs, asked))
    asked = exchange(asked)
    views, slopes = prepare_views(row, coefs, pointmaps, confidence)

    near_sums = view_sums(table, coefs, row, views, near, 2 * slots, half, cap)
    near_grads = depth_grads(table, slopes, near, 2 * slots, half, cap, False)
    asked, near_sums, near_grads = tie((asked, near_sums, near_grads))
    far_grads = depth_grads(table, slopes, asked, 3 * slots, half, cap, False)
    asked, far_grads = tie((asked, far_grads))
    back = exchange(far_grads)
    far_sums = view_sums(table, coefs, row, views, asked, 3 * slots, half, cap)
    back, far_sums = tie((back, far_sums))
    folded = fold_slots(table, back, slots, images, cap, far_bound, 1)
    folded, far_sums = tie((folded, far_sums))
    far_codes = [swap(part, half) for part in folded]
    small = view_terms(names, cams, poses, [near_sums, far_sums], shards * images)
    near_grads, small = tie((near_grads, small))
    near_total = fold_local(table, exchange(near_grads), 0, images, half, cap)
    done = []
    for c in range(1):
        done = update_depths(
            near_total, far_codes[c], depths, depth_moment, depth_second, far_bound, c, done
        )

    bit = 1
    while bit < lax.axis_size("rep"):
        small = small + lax.ppermute(
            small, "rep", [(i, i ^ bit) for i in range(lax.axis_size("rep"))]
        )
        bit *= 2
    camera_mail = lax.all_to_all(
        small[: shards * images].reshape(shards, images, 7), "img", 0, 0, tiled=True
    )
    new = update_small(
        camera_mail,
        small[shards * images :].T,
        [cameras, camera_moment, camera_second],
        [pair_poses.T, pair_moment.T, pair_second.T],
    )
    return (*done, *new[:3], *(value.T for value in new[3:]))


def solution(mesh):
    return jax.shard_map(
        body,
        mesh=mesh,
        in_specs=(
            P("img", None),
            P("img", "rep"),
            P("img", "rep"),
            P("img", "rep"),
            P("img", None),
            P("img", None),
            P("img", None),
            P("img", None),
            P("img", None),
            P("img", None),
            P("img", None, None, "rep"),
            P("img", None, "rep"),
        ),
        out_specs=(
            P("img", "rep"),
            P("img", "rep"),
            P("img", "rep"),
            P("img", None),
            P("img", None),
            P("img", None),
            P("img", None),
            P("img", None),
            P("img", None),
        ),
        check_vma=False,
    )
```

time: 195 us -> 125 us (0.64)
  blocking collectives: 52.8 us -> 0 us
  other arithmetic: 28.8 us -> 2.14 us
  local copies, waits for them, and re-layouts: 33.1 us -> 11.9 us
  waiting for transfers between devices: 20.3 us -> 36.2 us
  Pallas kernels: 31.7 us -> 40.8 us
  starting transfers between devices: 25.1 us -> 32.5 us
    all_gather x1 -> x0, blocking collectives: 46.1 us -> none  [body(): all_cameras = lax.all_gather(cameras, 'img', axis=0, tiled=True)]
    all_to_all x1 -> x2, waiting for transfers between devices: 0.01 us -> 28 us  [the longest x1 14.6 us: body(): mail = lax.all_to_all(letters, 'img', 0, 0, tiled=True)]
    ppermute x17 -> x15, waiting for transfers between devices: 20.3 us -> 4.9 us  [swap(): return lax.ppermute(value, 'img', [(i, i ^ k) for i in range(shards)])]
    mul x14 -> x0, other arithmetic: 12 us -> none  [the longest x2 3.11 us: turn_gradient(): return [factor * (torque[j] + swing[j]) for j in range(3)]]
    unnamed x104 -> x40, local copies, waits for them, and re-layouts: 20.6 us -> 8.81 us
    pallas_call x8 -> x14, Pallas kernels: 27.4 us -> 38.3 us  [the longest x2 10.4 us: view_sums(): pl.pallas_call(functools.partial(sum_kernel, first, half, cap), out_shape...]
    all_to_all x1 -> x2, starting transfers between devices: 3.95 us -> 11.2 us  [the longest x1 7.25 us: body(): mail = lax.all_to_all(letters, 'img', 0, 0, tiled=True)]
    another operation x20 -> x0, local copies, waits for them, and re-layouts: 7.03 us -> none  [the longest x15 3.81 us: body(): list(sums.T[:SUMS])]
  transfers between devices with their start and end apart: 18 -> 19, of which waited for: 7 -> 7; matrix products, arithmetic and copies ran while one was open for 14% -> 3% of each run, Pallas kernels for 11% -> 25%
where the time goes in v2:
time: 125 us; the launch traced here: 124 us
  Pallas kernels  40.8 us (33%)
  waiting for transfers between devices  36.2 us (29%)
  starting transfers between devices  32.5 us (26%)
  local copies, waits for them, and re-layouts  11.9 us (10%)
  other arithmetic  2.14 us (2%)
    ppermute x15, starting transfers between devices, swap(): return lax.ppermute(value, 'img', [(i, i ^ k) for i in range(shards)])  19.7 us
    all_to_all x1, waiting for transfers between devices, body(): mail = lax.all_to_all(letters, 'img', 0, 0, tiled=True)  14.6 us
    all_to_all x1, waiting for transfers between devices, body(): lax.all_to_all(small[:shards * images].reshape(shards, images, 7), 'img',...  13.4 us
    pallas_call x2, Pallas kernels, view_sums(): pl.pallas_call(functools.partial(sum_kernel, first, half, cap), out_shape...  10.4 us
    unnamed x40, local copies, waits for them, and re-layouts  8.81 us
    all_to_all x1, starting transfers between devices, body(): mail = lax.all_to_all(letters, 'img', 0, 0, tiled=True)  7.25 us
    pallas_call x2, Pallas kernels, depth_grads(): pl.pallas_call(functools.partial(grad_kernel, first, half, cap), out_shap...  5.3 us
    ppermute x15, waiting for transfers between devices, swap(): return lax.ppermute(value, 'img', [(i, i ^ k) for i in range(shards)])  4.9 us
  transfers between devices with their start and end apart: 19, of which 7 were waited for; matrix products, arithmetic and copies ran while one was open for 3% of the time, Pallas kernels for 25%

profile of v2, /device:TPU:0, one launch (start us, length us, event | category | flops | bytes accessed | tf_op | source)
XLA Modules:
  0.0 124.4 jit_solution(3342120462585180060)
XLA Ops:
  0.6 1.5 %fusion = s16[1,8,288,128]{3,1,2,0:T(8,128)(2,1)S(1)} fusion(f32[8,36864]{1,0:T(8,128)} %x_ref.1), kind=kLoop, calls=%fused_computation.1 | loop fusion | flops 1179648 | bytes 1769472
  4.5 7.3 %all-to-all-start = ((f32[8,9,128]{2,1,0:T(8,128)}), f32[8,9,128]{2,1,0:T(8,128)S(1)}, u32[]{:S(2)}, u32[]{:S(2)}) async-start(f32[8,9,128]{2,1,0:T(8,128)} %letters_of.1), calls=%async_computation | async-start | bytes 131072 | tf_op jit(solution)/shard_map/all_to_all | solution.py:632
  11.7 2.9 %collective-permute-start = (s16[8,144,128]{2,1,0:T(8,128)(2,1)}, s16[8,144,128]{2,1,0:T(8,128)(2,1)S(1)}, u32[]{:S(2)}, u32[]{:S(2)}) collective-permute-start(s16[8,144,128]{2,1,0:T(8,128)(2,1)} %get-tuple-element.157), channel_id=1, source_target_pairs={{0,16},{4,20},{8,24},{12,28},{16,0},{20,4},{24,8},{28,12},{1,17},{... | collective-permute-start | bytes 884744 | tf_op jit(solution)/shard_map/ppermute | solution.py:616
  14.7 14.6 %all-to-all-done.all_ref = f32[8,9,128]{2,1,0:T(8,128)S(1)} async-done(((f32[8,9,128]{2,1,0:T(8,128)}), f32[8,9,128]{2,1,0:T(8,128)S(1)}, u32[]{:S(2)}, u32[]{:S(2)}) %all-to-all-start) | async-done | bytes 36896 | tf_op jit(solution)/shard_map/all_to_all | solution.py:632
  29.9 2.5 %slot_tables.1.tab_ref = s32[65]{0:T(128)} custom-call(s32[1]{0:T(128)} %bitcast.me_ref, s32[8,24]{1,0:T(8,128)} %bitcast.37), custom_call_target="tpu_custom_call" | custom-call | flops 1 | bytes 1 | tf_op jit(solution)/shard_map/slot_tables/pallas_call | solution.py:128
  33.1 1.4 %pack_slots.2 = (s16[4,288,128]{2,1,0:T(8,128)(2,1)S(1)}, s16[4,288,128]{2,1,0:T(8,128)(2,1)}, s16[4,288,128]{2,1,0:T(8,128)(2,1)S(1)}, s16[4,288,128]{2,1,0:T(8,128)(2,1)S(1)}) custom-call(s32[65]{0:T(128)S(1)} %copy-done.11, s16[8,288,128]{2,1,0:T(8,128)(2,1)S(1)} %bitcast.33), custom_call_target="tpu_custom_call" | custom-call | flops 1 | bytes 1 | tf_op jit(solution)/shard_map/pack_slots/pallas_call | solution.py:153
  36.0 1.4 %collective-permute-start.5 = (s16[4,288,128]{2,1,0:T(8,128)(2,1)}, s16[4,288,128]{2,1,0:T(8,128)(2,1)S(1)}, u32[]{:S(2)}, u32[]{:S(2)}) collective-permute-start(s16[4,288,128]{2,1,0:T(8,128)(2,1)} %get-tuple-element.105), channel_id=1, source_target_pairs={{0,4},{4,0},{8,12},{12,8},{16,20},{20,16},{24,28},{28,24},{1,5},{5... | collective-permute-start | bytes 884744 | tf_op jit(solution)/shard_map/ppermute | solution.py:616
  38.1 2.0 %collective-permute-start.7 = (s16[4,288,128]{2,1,0:T(8,128)(2,1)}, s16[4,288,128]{2,1,0:T(8,128)(2,1)}, u32[]{:S(2)}, u32[]{:S(2)}) collective-permute-start(s16[4,288,128]{2,1,0:T(8,128)(2,1)} %copy-done.15), channel_id=1, source_target_pairs={{0,12},{4,8},{8,4},{12,0},{16,28},{20,24},{24,20},{28,16},{1,13},{... | collective-permute-start | bytes 884744 | tf_op jit(solution)/shard_map/ppermute | solution.py:616
  40.1 1.9 %view_coefs.1 = (f32[24,16]{1,0:T(8,128)}, f32[24,7]{1,0:T(8,128)}, f32[24,7]{1,0:T(8,128)}) custom-call(s32[2,12]{1,0:T(2,128)} %bitcast.40, f32[8,9,128]{2,1,0:T(8,128)} %copy-done.17, f32[12,7]{1,0:T(8,128)} %copy.21.pair_ref), custom_call_target="tpu_custom_call" | custom-call | flops 1 | bytes 1 | tf_op jit(solution)/shard_map/view_coefs/pallas_call | solution.py:510
  42.7 2.1 %pack_slots.3 = (s16[4,288,128]{2,1,0:T(8,128)(2,1)S(1)}, s16[4,288,128]{2,1,0:T(8,128)(2,1)}, s16[4,288,128]{2,1,0:T(8,128)(2,1)}, s16[4,288,128]{2,1,0:T(8,128)(2,1)}) custom-call(s32[65]{0:T(128)S(1)} %copy-done.12, s16[8,144,128]{2,1,0:T(8,128)(2,1)S(1)} %collective-permute-done.refs_0_, s16[8,144,128]{2,1,0:T(8,128)(2,1)} %collective-permute-done.1.refs_1_), custom_call_target="tpu_custom_call" | custom-call | flops 1 | bytes 1 | tf_op jit(solution)/shard_map/pack_slots/pallas_call | solution.py:153
  44.8 1.4 %collective-permute-start.2 = (s16[4,288,128]{2,1,0:T(8,128)(2,1)}, s16[4,288,128]{2,1,0:T(8,128)(2,1)S(1)}, u32[]{:S(2)}, u32[]{:S(2)}) collective-permute-start(s16[4,288,128]{2,1,0:T(8,128)(2,1)} %get-tuple-element.99), channel_id=1, source_target_pairs={{0,4},{4,0},{8,12},{12,8},{16,20},{20,16},{24,28},{28,24},{1,5},{5... | collective-permute-start | bytes 884744 | tf_op jit(solution)/shard_map/ppermute | solution.py:616
  46.3 2.0 %collective-permute-start.4 = (s16[4,288,128]{2,1,0:T(8,128)(2,1)}, s16[4,288,128]{2,1,0:T(8,128)(2,1)}, u32[]{:S(2)}, u32[]{:S(2)}) collective-permute-start(s16[4,288,128]{2,1,0:T(8,128)(2,1)} %get-tuple-element.101), channel_id=1, source_target_pairs={{0,12},{4,8},{8,4},{12,0},{16,28},{20,24},{24,20},{28,16},{1,13},{... | collective-permute-start | bytes 884744 | tf_op jit(solution)/shard_map/ppermute | solution.py:616
  48.3 2.5 %copy-done = bf16[12,2,3,36864]{3,1,2,0:T(2,128)(2,1)S(1)} copy-done((bf16[12,2,3,36864]{3,1,2,0:T(2,128)(2,1)S(1)}, bf16[12,2,3,36864]{3,1,2,0:T(2,128)(2,1)}, u32[]{:S(2)}) %copy-start) | copy-done | bytes 5308440
  51.5 4.7 %prepare_views.1 = (bf16[24,4,288,128]{3,2,1,0:T(8,128)(2,1)S(1)}, f32[24,2,288,128]{3,2,1,0:T(8,128)S(1)}) custom-call(f32[1]{0:T(128)} %bitcast.3.row_ref, f32[24,16]{1,0:T(8,128)S(1)} %copy-done.9, bf16[12,3,576,128]{3,2,1,0:T(8,128)(2,1)S(1)} %bitcast.31, bf16[12,576,128]{2,1,0:T(8,128)(2,1)S(1)} %bitcast.34), custom_call_target="tpu_custom_call" | custom-call | flops 1 | bytes 1 | tf_op jit(solution)/shard_map/prepare_views/pallas_call | solution.py:223
  56.2 4.5 %view_sums.2.refs_0_ = f32[24,16,128]{2,1,0:T(8,128)S(1)} custom-call(s32[65]{0:T(128)S(1)} %copy-done.13, f32[24,16]{1,0:T(8,128)S(1)} %copy-done.10, f32[1]{0:T(128)} %bitcast.3.row_ref, bf16[24,4,288,128]{3,2,1,0:T(8,128)(2,1)S(1)} %get-tuple-element.103.view_ref, s16[4,288,128]{2,1,0:T(8,128)(2,1)S(1)} %get-tuple-element.104.refs_0_, ...), custom_call_target="tpu_custom_call" | custom-call | flops 1 | bytes 1 | tf_op jit(solution)/shard_map/view_sums/pallas_call | solution.py:330
  61.5 2.9 %depth_grads.2 = (s16[4,288,128]{2,1,0:T(8,128)(2,1)S(1)}, s16[4,288,128]{2,1,0:T(8,128)(2,1)}, s16[4,288,128]{2,1,0:T(8,128)(2,1)}, s16[4,288,128]{2,1,0:T(8,128)(2,1)S(1)}) custom-call(s32[65]{0:T(128)S(1)} %copy-done.13, f32[24,2,288,128]{3,2,1,0:T(8,128)S(1)} %get-tuple-element.108.slope_ref, s16[4,288,128]{2,1,0:T(8,128)(2,1)S(1)} %get-tuple-element.104.refs_0_, ...), custom_call_target="tpu_custom_call" | custom-call | flops 1 | bytes 1 | tf_op jit(solution)/shard_map/depth_grads/pallas_call | solution.py:268
  65.7 2.4 %depth_grads.3 = (s16[4,288,128]{2,1,0:T(8,128)(2,1)S(1)}, s16[4,288,128]{2,1,0:T(8,128)(2,1)S(1)}, s16[4,288,128]{2,1,0:T(8,128)(2,1)S(1)}, s16[4,288,128]{2,1,0:T(8,128)(2,1)S(1)}) custom-call(s32[65]{0:T(128)S(1)} %copy-done.13, f32[24,2,288,128]{3,2,1,0:T(8,128)S(1)} %get-tuple-element.108.slope_ref, s16[4,288,128]{2,1,0:T(8,128)(2,1)S(1)} %get-tuple-element.132.refs_0_, ...), custom_call_target="tpu_custom_call" | custom-call | flops 1 | bytes 1 | tf_op jit(solution)/shard_map/depth_grads/pallas_call | solution.py:268
  68.2 1.6 %collective-permute-start.8 = (s16[4,288,128]{2,1,0:T(8,128)(2,1)S(1)}, s16[4,288,128]{2,1,0:T(8,128)(2,1)S(1)}, u32[]{:S(2)}, u32[]{:S(2)}) collective-permute-start(s16[4,288,128]{2,1,0:T(8,128)(2,1)S(1)} %get-tuple-element.129), channel_id=1, source_target_pairs={{0,4},{4,0},{8,12},{12,8},{16,20},{20,16},{24,28},{28,24},{1,5},{5... | collective-permute-start | bytes 884744 | tf_op jit(solution)/shard_map/ppermute | solution.py:616
  69.8 2.0 %collective-permute-start.10 = (s16[4,288,128]{2,1,0:T(8,128)(2,1)S(1)}, s16[4,288,128]{2,1,0:T(8,128)(2,1)S(1)}, u32[]{:S(2)}, u32[]{:S(2)}) collective-permute-start(s16[4,288,128]{2,1,0:T(8,128)(2,1)S(1)} %get-tuple-element.131), channel_id=1, source_target_pairs={{0,12},{4,8},{8,4},{12,0},{16,28},{20,24},{24,20},{28,16},{1,13},{... | collective-permute-start | bytes 884744 | tf_op jit(solution)/shard_map/ppermute | solution.py:616
  71.7 5.8 %view_sums.3.refs_1_ = f32[24,16,128]{2,1,0:T(8,128)S(1)} custom-call(s32[65]{0:T(128)S(1)} %copy-done.13, f32[24,16]{1,0:T(8,128)S(1)} %copy-done.10, f32[1]{0:T(128)} %bitcast.3.row_ref, bf16[24,4,288,128]{3,2,1,0:T(8,128)(2,1)S(1)} %get-tuple-element.103.view_ref, s16[4,288,128]{2,1,0:T(8,128)(2,1)S(1)} %get-tuple-element.132.refs_0_, ...), custom_call_target="tpu_custom_call" | custom-call | flops 1 | bytes 1 | tf_op jit(solution)/shard_map/view_sums/pallas_call | solution.py:330
  79.5 3.0 %collective-permute-done.10.refs_3_ = s16[4,288,128]{2,1,0:T(8,128)(2,1)S(1)} collective-permute-done((s16[4,288,128]{2,1,0:T(8,128)(2,1)S(1)}, s16[4,288,128]{2,1,0:T(8,128)(2,1)S(1)}, u32[]{:S(2)}, u32[]{:S(2)}) %collective-permute-start.10) | collective-permute-done | bytes 294944 | tf_op jit(solution)/shard_map/ppermute | solution.py:616
  82.5 2.0 %fold_slots.1 = s16[8,288,128]{2,1,0:T(8,128)(2,1)S(1)} custom-call(s32[65]{0:T(128)S(1)} %copy-done.13, s16[4,288,128]{2,1,0:T(8,128)(2,1)S(1)} %get-tuple-element.136.refs_0_, s16[4,288,128]{2,1,0:T(8,128)(2,1)S(1)} %collective-permute-done.8.refs_1_, s16[4,288,128]{2,1,0:T(8,128)(2,1)S(1)} %collective-permute-done.9.refs_2_, ...), custom_call_target="tpu_custom_call" | custom-call | flops 1 | bytes 1 | tf_op jit(solution)/shard_map/fold_slots/pallas_call | solution.py:370
  84.5 2.7 %collective-permute-start.14 = (s16[8,288,128]{2,1,0:T(8,128)(2,1)S(1)}, s16[8,288,128]{2,1,0:T(8,128)(2,1)S(1)}, u32[]{:S(2)}, u32[]{:S(2)}) collective-permute-start(s16[8,288,128]{2,1,0:T(8,128)(2,1)S(1)} %fold_slots.1), channel_id=1, source_target_pairs={{0,16},{4,20},{8,24},{12,28},{16,0},{20,4},{24,8},{28,12},{1,17},{... | collective-permute-start | bytes 1769480 | tf_op jit(solution)/shard_map/ppermute | solution.py:616
  87.2 2.7 %view_terms.1 = f32[76,7]{1,0:T(8,128)} custom-call(s32[2,12]{1,0:T(2,128)} %bitcast.41, f32[24,7]{1,0:T(8,128)} %get-tuple-element.117.cam_ref, f32[24,7]{1,0:T(8,128)} %get-tuple-element.118.pose_ref, f32[24,16,128]{2,1,0:T(8,128)} %copy-done.5, f32[24,16,128]{2,1,0:T(8,128)} %copy-done.6), custom_call_target="tpu_custom_call" | custom-call | flops 1 | bytes 1 | tf_op jit(solution)/shard_map/view_terms/pallas_call | solution.py:558
  89.9 1.7 %collective-permute-start.11 = (s16[4,288,128]{2,1,0:T(8,128)(2,1)}, s16[4,288,128]{2,1,0:T(8,128)(2,1)S(1)}, u32[]{:S(2)}, u32[]{:S(2)}) collective-permute-start(s16[4,288,128]{2,1,0:T(8,128)(2,1)} %get-tuple-element.143), channel_id=1, source_target_pairs={{0,4},{4,0},{8,12},{12,8},{16,20},{20,16},{24,28},{28,24},{1,5},{5... | collective-permute-start | bytes 884744 | tf_op jit(solution)/shard_map/ppermute | solution.py:616
  95.4 1.5 %collective-permute-start.16 = (f32[76,7]{0,1:T(8,128)S(1)}, f32[76,7]{0,1:T(8,128)S(1)}, u32[]{:S(2)}, u32[]{:S(2)}) collective-permute-start(f32[76,7]{0,1:T(8,128)S(1)} %add.11), channel_id=1, source_target_pairs={{0,2},{1,3},{2,0},{3,1},{4,6},{5,7},{6,4},{7,5},{8,10},{9,11},{10,... | collective-permute-start | bytes 6392 | tf_op jit(solution)/shard_map/ppermute | solution.py:671
  96.9 2.1 %collective-permute-done.16 = f32[76,7]{0,1:T(8,128)S(1)} collective-permute-done((f32[76,7]{0,1:T(8,128)S(1)}, f32[76,7]{0,1:T(8,128)S(1)}, u32[]{:S(2)}, u32[]{:S(2)}) %collective-permute-start.16) | collective-permute-done | bytes 2160 | tf_op jit(solution)/shard_map/ppermute | solution.py:671
  99.7 4.0 %all-to-all-start.1 = ((f32[8,8,7]{2,1,0:T(8,128)}), f32[8,8,7]{2,1,0:T(8,128)}, u32[]{:S(2)}, u32[]{:S(2)}) async-start(f32[8,8,7]{2,1,0:T(8,128)} %bitcast.35), calls=%async_computation.1 | async-start | bytes 65536 | tf_op jit(solution)/shard_map/all_to_all | solution.py:675
  104.4 13.4 %all-to-all-done.1.mail_ref = f32[8,8,7]{2,1,0:T(8,128)} async-done(((f32[8,8,7]{2,1,0:T(8,128)}), f32[8,8,7]{2,1,0:T(8,128)}, u32[]{:S(2)}, u32[]{:S(2)}) %all-to-all-start.1) | async-done | bytes 1824 | tf_op jit(solution)/shard_map/all_to_all | solution.py:675
  117.8 1.4 %update_small.1 = (f32[8,7]{1,0:T(8,128)}, f32[8,7]{1,0:T(8,128)}, f32[8,7]{1,0:T(8,128)}, f32[7,12]{1,0:T(8,128)}, f32[7,12]{1,0:T(8,128)}, /*index=5*/f32[7,12]{1,0:T(8,128)}) custom-call(f32[8,8,7]{2,1,0:T(8,128)} %all-to-all-done.1.mail_ref, f32[7,12]{1,0:T(8,128)} %slice_bitcast_fusion.pose_ref, f32[8,7]{1,0:T(8,128)} %refs_0_.1, f32[8,7]{1,0:T(8,128)} %refs_1_.1, ...), custom_call_target="tpu_custom_call" | custom-call | flops 1 | bytes 1 | tf_op jit(solution)/shard_map/update_small/pallas_call | solution.py:580
  119.3 1.6 %fold_local.1.local_ref = f32[8,288,128]{2,1,0:T(8,128)S(1)} custom-call(s32[65]{0:T(128)S(1)} %copy-done.13, s16[4,288,128]{2,1,0:T(8,128)(2,1)S(1)} %copy-done.8, s16[4,288,128]{2,1,0:T(8,128)(2,1)S(1)} %collective-permute-done.11.refs_1_, s16[4,288,128]{2,1,0:T(8,128)(2,1)S(1)} %collective-permute-done.12.refs_2_, ...), custom_call_target="tpu_custom_call" | custom-call | flops 1 | bytes 1 | tf_op jit(solution)/shard_map/fold_local/pallas_call | solution.py:388
  120.9 3.5 %update_depths.1 = (f32[8,36864]{1,0:T(8,128)}, f32[8,36864]{1,0:T(8,128)}, f32[8,36864]{1,0:T(8,128)}) custom-call(f32[8,288,128]{2,1,0:T(8,128)S(1)} %fold_local.1.local_ref, s16[8,288,128]{2,1,0:T(8,128)(2,1)S(1)} %collective-permute-done.14.far_ref, f32[8,36864]{1,0:T(8,128)S(1)} %copy-done.1, f32[8,36864]{1,0:T(8,128)S(1)} %copy-done.3, ...), custom_call_target="tpu_custom_call" | custom-call | flops 1 | bytes 1 | tf_op jit(solution)/shard_map/update_depths/pallas_call | solution.py:428
  (69 shorter events, 16.3 us)
Async XLA Ops:
  2.2 35.2 %copy-start.18 = (f32[12,7]{0,1:T(8,128)S(1)}, f32[12,7]{0,1:T(8,128)}, u32[]{:S(2)}) copy-start(f32[12,7]{0,1:T(8,128)} %param.19) | copy-start | bytes 1012
  2.3 46.0 %copy-start.2 = (bf16[12,2,36864]{2,1,0:T(2,128)(2,1)S(1)}, bf16[12,2,36864]{2,1,0:T(2,128)(2,1)}, u32[]{:S(2)}) copy-start(bf16[12,2,36864]{2,1,0:T(2,128)(2,1)} %param.23) | copy-start | bytes 5308420
  4.5 24.8 %all-to-all-start = ((f32[8,9,128]{2,1,0:T(8,128)}), f32[8,9,128]{2,1,0:T(8,128)S(1)}, u32[]{:S(2)}, u32[]{:S(2)}) async-start(f32[8,9,128]{2,1,0:T(8,128)} %letters_of.1), calls=%async_computation | async-start | bytes 131072 | tf_op jit(solution)/shard_map/all_to_all | solution.py:632
  11.7 30.3 %collective-permute-start = (s16[8,144,128]{2,1,0:T(8,128)(2,1)}, s16[8,144,128]{2,1,0:T(8,128)(2,1)S(1)}, u32[]{:S(2)}, u32[]{:S(2)}) collective-permute-start(s16[8,144,128]{2,1,0:T(8,128)(2,1)} %get-tuple-element.157), channel_id=1, source_target_pairs={{0,16},{4,20},{8,24},{12,28},{16,0},{20,4},{24,8},{28,12},{1,17},{... | collective-permute-start | bytes 884744 | tf_op jit(solution)/shard_map/ppermute | solution.py:616
  14.7 27.4 %collective-permute-start.1 = (s16[8,144,128]{2,1,0:T(8,128)(2,1)}, s16[8,144,128]{2,1,0:T(8,128)(2,1)}, u32[]{:S(2)}, u32[]{:S(2)}) collective-permute-start(s16[8,144,128]{2,1,0:T(8,128)(2,1)} %get-tuple-element.84), channel_id=1, source_target_pairs={{0,16},{4,20},{8,24},{12,28},{16,0},{20,4},{24,8},{28,12},{1,17},{... | collective-permute-start | bytes 884744 | tf_op jit(solution)/shard_map/ppermute | solution.py:616
  34.5 0.7 copy-start.15
  35.3 0.7 copy-start.16
  36.0 10.3 %collective-permute-start.5 = (s16[4,288,128]{2,1,0:T(8,128)(2,1)}, s16[4,288,128]{2,1,0:T(8,128)(2,1)S(1)}, u32[]{:S(2)}, u32[]{:S(2)}) collective-permute-start(s16[4,288,128]{2,1,0:T(8,128)(2,1)} %get-tuple-element.105), channel_id=1, source_target_pairs={{0,4},{4,0},{8,12},{12,8},{16,20},{20,16},{24,28},{28,24},{1,5},{5... | collective-permute-start | bytes 884744 | tf_op jit(solution)/shard_map/ppermute | solution.py:616
  38.1 18.1 %collective-permute-start.6 = (s16[4,288,128]{2,1,0:T(8,128)(2,1)}, s16[4,288,128]{2,1,0:T(8,128)(2,1)S(1)}, u32[]{:S(2)}, u32[]{:S(2)}) collective-permute-start(s16[4,288,128]{2,1,0:T(8,128)(2,1)} %copy-done.16), channel_id=1, source_target_pairs={{0,8},{4,12},{8,0},{12,4},{16,24},{20,28},{24,16},{28,20},{1,9},{5... | collective-permute-start | bytes 884744 | tf_op jit(solution)/shard_map/ppermute | solution.py:616
  38.1 18.1 %collective-permute-start.7 = (s16[4,288,128]{2,1,0:T(8,128)(2,1)}, s16[4,288,128]{2,1,0:T(8,128)(2,1)}, u32[]{:S(2)}, u32[]{:S(2)}) collective-permute-start(s16[4,288,128]{2,1,0:T(8,128)(2,1)} %copy-done.15), channel_id=1, source_target_pairs={{0,12},{4,8},{8,4},{12,0},{16,28},{20,24},{24,20},{28,16},{1,13},{... | collective-permute-start | bytes 884744 | tf_op jit(solution)/shard_map/ppermute | solution.py:616
  44.8 20.3 %collective-permute-start.2 = (s16[4,288,128]{2,1,0:T(8,128)(2,1)}, s16[4,288,128]{2,1,0:T(8,128)(2,1)S(1)}, u32[]{:S(2)}, u32[]{:S(2)}) collective-permute-start(s16[4,288,128]{2,1,0:T(8,128)(2,1)} %get-tuple-element.99), channel_id=1, source_target_pairs={{0,4},{4,0},{8,12},{12,8},{16,20},{20,16},{24,28},{28,24},{1,5},{5... | collective-permute-start | bytes 884744 | tf_op jit(solution)/shard_map/ppermute | solution.py:616
  46.2 18.8 %collective-permute-start.3 = (s16[4,288,128]{2,1,0:T(8,128)(2,1)}, s16[4,288,128]{2,1,0:T(8,128)(2,1)S(1)}, u32[]{:S(2)}, u32[]{:S(2)}) collective-permute-start(s16[4,288,128]{2,1,0:T(8,128)(2,1)} %get-tuple-element.100), channel_id=1, source_target_pairs={{0,8},{4,12},{8,0},{12,4},{16,24},{20,28},{24,16},{28,20},{1,9},{5... | collective-permute-start | bytes 884744 | tf_op jit(solution)/shard_map/ppermute | solution.py:616
  46.3 19.5 %collective-permute-start.4 = (s16[4,288,128]{2,1,0:T(8,128)(2,1)}, s16[4,288,128]{2,1,0:T(8,128)(2,1)}, u32[]{:S(2)}, u32[]{:S(2)}) collective-permute-start(s16[4,288,128]{2,1,0:T(8,128)(2,1)} %get-tuple-element.101), channel_id=1, source_target_pairs={{0,12},{4,8},{8,4},{12,0},{16,28},{20,24},{24,20},{28,16},{1,13},{... | collective-permute-start | bytes 884744 | tf_op jit(solution)/shard_map/ppermute | solution.py:616
  48.3 2.5 %copy-start = (bf16[12,2,3,36864]{3,1,2,0:T(2,128)(2,1)S(1)}, bf16[12,2,3,36864]{3,1,2,0:T(2,128)(2,1)}, u32[]{:S(2)}) copy-start(bf16[12,2,3,36864]{3,1,2,0:T(2,128)(2,1)} %param.22) | copy-start | bytes 15925252
  51.5 4.7 %copy-start.10 = (f32[24,16]{1,0:T(8,128)S(1)}, f32[24,16]{1,0:T(8,128)}, u32[]{:S(2)}) copy-start(f32[24,16]{1,0:T(8,128)} %get-tuple-element.102.coef_ref) | copy-start | bytes 4612
  51.5 4.7 %copy-start.13 = (s32[65]{0:T(128)S(1)}, s32[65]{0:T(128)}, u32[]{:S(2)}) copy-start(s32[65]{0:T(128)} %slot_tables.1.tab_ref) | copy-start | bytes 784
  64.3 0.7 copy-start.7
  65.1 3.1 %copy-start.14 = (s16[4,288,128]{2,1,0:T(8,128)(2,1)}, s16[4,288,128]{2,1,0:T(8,128)(2,1)S(1)}, u32[]{:S(2)}) copy-start(s16[4,288,128]{2,1,0:T(8,128)(2,1)S(1)} %get-tuple-element.145) | copy-start | bytes 884740
  68.2 10.1 %collective-permute-start.8 = (s16[4,288,128]{2,1,0:T(8,128)(2,1)S(1)}, s16[4,288,128]{2,1,0:T(8,128)(2,1)S(1)}, u32[]{:S(2)}, u32[]{:S(2)}) collective-permute-start(s16[4,288,128]{2,1,0:T(8,128)(2,1)S(1)} %get-tuple-element.129), channel_id=1, source_target_pairs={{0,4},{4,0},{8,12},{12,8},{16,20},{20,16},{24,28},{28,24},{1,5},{5... | collective-permute-start | bytes 884744 | tf_op jit(solution)/shard_map/ppermute | solution.py:616
  69.8 9.7 %collective-permute-start.9 = (s16[4,288,128]{2,1,0:T(8,128)(2,1)S(1)}, s16[4,288,128]{2,1,0:T(8,128)(2,1)S(1)}, u32[]{:S(2)}, u32[]{:S(2)}) collective-permute-start(s16[4,288,128]{2,1,0:T(8,128)(2,1)S(1)} %get-tuple-element.130), channel_id=1, source_target_pairs={{0,8},{4,12},{8,0},{12,4},{16,24},{20,28},{24,16},{28,20},{1,9},{5... | collective-permute-start | bytes 884744 | tf_op jit(solution)/shard_map/ppermute | solution.py:616
  69.8 12.7 %collective-permute-start.10 = (s16[4,288,128]{2,1,0:T(8,128)(2,1)S(1)}, s16[4,288,128]{2,1,0:T(8,128)(2,1)S(1)}, u32[]{:S(2)}, u32[]{:S(2)}) collective-permute-start(s16[4,288,128]{2,1,0:T(8,128)(2,1)S(1)} %get-tuple-element.131), channel_id=1, source_target_pairs={{0,12},{4,8},{8,4},{12,0},{16,28},{20,24},{24,20},{28,16},{1,13},{... | collective-permute-start | bytes 884744 | tf_op jit(solution)/shard_map/ppermute | solution.py:616
  78.3 41.0 %copy-start.8 = (s16[4,288,128]{2,1,0:T(8,128)(2,1)S(1)}, s16[4,288,128]{2,1,0:T(8,128)(2,1)}, u32[]{:S(2)}) copy-start(s16[4,288,128]{2,1,0:T(8,128)(2,1)} %copy-done.7) | copy-start | bytes 884740
  82.5 38.4 %copy-start.4 = (f32[8,36864]{1,0:T(8,128)S(1)}, f32[8,36864]{1,0:T(8,128)}, u32[]{:S(2)}) copy-start(f32[8,36864]{1,0:T(8,128)} %s_ref.1) | copy-start | bytes 3538948
  84.5 36.4 %collective-permute-start.14 = (s16[8,288,128]{2,1,0:T(8,128)(2,1)S(1)}, s16[8,288,128]{2,1,0:T(8,128)(2,1)S(1)}, u32[]{:S(2)}, u32[]{:S(2)}) collective-permute-start(s16[8,288,128]{2,1,0:T(8,128)(2,1)S(1)} %fold_slots.1), channel_id=1, source_target_pairs={{0,16},{4,20},{8,24},{12,28},{16,0},{20,4},{24,8},{28,12},{1,17},{... | collective-permute-start | bytes 1769480 | tf_op jit(solution)/shard_map/ppermute | solution.py:616
  89.9 29.4 %collective-permute-start.11 = (s16[4,288,128]{2,1,0:T(8,128)(2,1)}, s16[4,288,128]{2,1,0:T(8,128)(2,1)S(1)}, u32[]{:S(2)}, u32[]{:S(2)}) collective-permute-start(s16[4,288,128]{2,1,0:T(8,128)(2,1)} %get-tuple-element.143), channel_id=1, source_target_pairs={{0,4},{4,0},{8,12},{12,8},{16,20},{20,16},{24,28},{28,24},{1,5},{5... | collective-permute-start | bytes 884744 | tf_op jit(solution)/shard_map/ppermute | solution.py:616
  91.6 27.6 %collective-permute-start.12 = (s16[4,288,128]{2,1,0:T(8,128)(2,1)}, s16[4,288,128]{2,1,0:T(8,128)(2,1)S(1)}, u32[]{:S(2)}, u32[]{:S(2)}) collective-permute-start(s16[4,288,128]{2,1,0:T(8,128)(2,1)} %get-tuple-element.144), channel_id=1, source_target_pairs={{0,8},{4,12},{8,0},{12,4},{16,24},{20,28},{24,16},{28,20},{1,9},{5... | collective-permute-start | bytes 884744 | tf_op jit(solution)/shard_map/ppermute | solution.py:616
  92.5 26.8 %collective-permute-start.13 = (s16[4,288,128]{2,1,0:T(8,128)(2,1)}, s16[4,288,128]{2,1,0:T(8,128)(2,1)S(1)}, u32[]{:S(2)}, u32[]{:S(2)}) collective-permute-start(s16[4,288,128]{2,1,0:T(8,128)(2,1)} %copy-done.14), channel_id=1, source_target_pairs={{0,12},{4,8},{8,4},{12,0},{16,28},{20,24},{24,20},{28,16},{1,13},{... | collective-permute-start | bytes 884744 | tf_op jit(solution)/shard_map/ppermute | solution.py:616
  94.2 1.2 collective-permute-start.15
  95.4 3.6 %collective-permute-start.16 = (f32[76,7]{0,1:T(8,128)S(1)}, f32[76,7]{0,1:T(8,128)S(1)}, u32[]{:S(2)}, u32[]{:S(2)}) collective-permute-start(f32[76,7]{0,1:T(8,128)S(1)} %add.11), channel_id=1, source_target_pairs={{0,2},{1,3},{2,0},{3,1},{4,6},{5,7},{6,4},{7,5},{8,10},{9,11},{10,... | collective-permute-start | bytes 6392 | tf_op jit(solution)/shard_map/ppermute | solution.py:671
  99.7 18.1 %all-to-all-start.1 = ((f32[8,8,7]{2,1,0:T(8,128)}), f32[8,8,7]{2,1,0:T(8,128)}, u32[]{:S(2)}, u32[]{:S(2)}) async-start(f32[8,8,7]{2,1,0:T(8,128)} %bitcast.35), calls=%async_computation.1 | async-start | bytes 65536 | tf_op jit(solution)/shard_map/all_to_all | solution.py:675
  119.2 1.7 %copy-start.1 = (f32[8,36864]{1,0:T(8,128)S(1)}, f32[8,36864]{1,0:T(8,128)}, u32[]{:S(2)}) copy-start(f32[8,36864]{1,0:T(8,128)} %x_ref.1) | copy-start | bytes 3538948
  119.2 1.7 %copy-start.3 = (f32[8,36864]{1,0:T(8,128)S(1)}, f32[8,36864]{1,0:T(8,128)}, u32[]{:S(2)}) copy-start(f32[8,36864]{1,0:T(8,128)} %m_ref.1) | copy-start | bytes 3538948
  (6 other events, 4.0 us)

commit v3 on v2

--- a/solution.py
+++ b/solution.py
@@ -138,14 +138,16 @@
 
 def pack_kernel(first, half, tab_ref, *refs):
     map_refs, slot_refs = refs[:-half], refs[-half:]
-    rows = map_refs[0].shape[1]
     for k, slot_ref in enumerate(slot_refs):
 
         @pl.loop(0, slot_ref.shape[0])
         def _(c):
             image = jnp.maximum(tab_ref[first + k * slot_ref.shape[0] + c], 0)
-            for i, map_ref in enumerate(map_refs):
-                slot_ref[c, i * rows : (i + 1) * rows] = map_ref[image]
+            first_row = 0
+            for map_ref in map_refs:
+                rows = map_ref.shape[1]
+                slot_ref[c, first_row : first_row + rows] = map_ref[image]
+                first_row += rows
 
 
 def pack_slots(table, maps, first, half, cap):
@@ -626,8 +628,8 @@
     letters = letters_of(names, cameras, shards)
     codes = jnp.round((depths - DEPTH_MID) * (1.0 / DEPTH_STEP)).astype(INTS)
     codes = codes.reshape(images, rows, LANES)
-    size = rows // SWAP_PARTS
-    parts = [codes[:, c * size : (c + 1) * size] for c in range(SWAP_PARTS)]
+    first = rows // 48 * 16 * 2
+    parts = [codes[:, :first], codes[:, first:]]
     letters, parts[1:] = tie((letters, parts[1:]))
     mail = lax.all_to_all(letters, "img", 0, 0, tiled=True)
     far = [swap(part, half) for part in parts]
@@ -640,11 +642,9 @@
     coefs, cams, poses = view_coefs(names, mail, pair_poses, images)
     row = rep * (row_len // WIDTH)
     row = (row.astype(jnp.float32) + (0.5 - 0.5 * HEIGHT)).reshape(1)
-    far, coefs = tie((far, coefs))
-    asked = pack_slots(table, far, slots, half, cap)
-    coefs, asked = tie((coefs, asked))
-    asked = exchange(asked)
     views, slopes = prepare_views(row, coefs, pointmaps, confidence)
+    far, slopes = tie((far, slopes))
+    asked = exchange(pack_slots(table, far, slots, half, cap))
 
     near_sums = view_sums(table, coefs, row, views, near, 2 * slots, half, cap)
     near_grads = depth_grads(table, slopes, near, 2 * slots, half, cap, False)
@@ -675,6 +675,7 @@
     camera_mail = lax.all_to_all(
         small[: shards * images].reshape(shards, images, 7), "img", 0, 0, tiled=True
     )
+    camera_mail, done = tie((camera_mail, done))
     new = update_small(
         camera_mail,
         small[shards * images :].T,

time: 125 us -> 118 us (0.944)
  Pallas kernels: 40.8 us -> 38.5 us
  local copies, waits for them, and re-layouts: 11.9 us -> 9.72 us
  waiting for transfers between devices: 36.2 us -> 34.3 us
    ppermute x15, waiting for transfers between devices: 4.9 us -> 20.6 us  [swap(): return lax.ppermute(value, 'img', [(i, i ^ k) for i in range(shards)])]
    all_to_all x1, waiting for transfers between devices: 13.4 us -> 0.01 us  [body(): lax.all_to_all(small[:shards * images].reshape(shards, images, 7), 'img',...]
    all_to_all x1, waiting for transfers between devices: 14.6 us -> 10.5 us  [body(): mail = lax.all_to_all(letters, 'img', 0, 0, tiled=True)]
    unnamed x40 -> x32, local copies, waits for them, and re-layouts: 8.81 us -> 6.05 us
  transfers between devices with their start and end apart: 19 -> 19, of which waited for: 7 -> 9; matrix products, arithmetic and copies ran while one was open for 3% -> 4% of each run, Pallas kernels for 25% -> 27%
where the time goes in v3:
time: 118 us
  Pallas kernels  38.5 us (33%)
  waiting for transfers between devices  34.3 us (29%)
  starting transfers between devices  32.3 us (27%)
  local copies, waits for them, and re-layouts  9.72 us (8%)
  other arithmetic  2.14 us (2%)
    ppermute x15, waiting for transfers between devices, swap(): return lax.ppermute(value, 'img', [(i, i ^ k) for i in range(shards)])  20.6 us
    ppermute x15, starting transfers between devices, swap(): return lax.ppermute(value, 'img', [(i, i ^ k) for i in range(shards)])  19.3 us
    all_to_all x1, waiting for transfers between devices, body(): mail = lax.all_to_all(letters, 'img', 0, 0, tiled=True)  10.5 us
    pallas_call x2, Pallas kernels, view_sums(): pl.pallas_call(functools.partial(sum_kernel, first, half, cap), out_shape...  9.88 us
    all_to_all x1, starting transfers between devices, body(): mail = lax.all_to_all(letters, 'img', 0, 0, tiled=True)  7.25 us
    unnamed x32, local copies, waits for them, and re-layouts  6.05 us
    pallas_call x1, Pallas kernels, prepare_views(): pl.pallas_call(prepare_kernel, out_shape=[jax.ShapeDtypeStruct((2 * pairs...  4.67 us
    pallas_call x2, Pallas kernels, depth_grads(): pl.pallas_call(functools.partial(grad_kernel, first, half, cap), out_shap...  4.44 us
  transfers between devices with their start and end apart: 19, of which 9 were waited for; matrix products, arithmetic and copies ran while one was open for 4% of the time, Pallas kernels for 27%

profile of v3, /device:TPU:0, one launch (start us, length us, event | category | flops | bytes accessed | tf_op | source)
XLA Modules:
  0.0 117.8 jit_solution(9112268499790509476)
XLA Ops:
  0.6 1.5 %fusion = s16[1,8,288,128]{3,1,2,0:T(8,128)(2,1)S(1)} fusion(f32[8,36864]{1,0:T(8,128)} %x_ref.1), kind=kLoop, calls=%fused_computation.1 | loop fusion | flops 1179648 | bytes 1769472
  3.0 1.3 %letters_of.1 = f32[8,9,128]{2,1,0:T(8,128)} custom-call(s32[2,12]{1,0:T(2,128)} %bitcast.40, f32[8,7]{1,0:T(8,128)} %refs_0_.1), custom_call_target="tpu_custom_call" | custom-call | flops 1 | bytes 1 | tf_op jit(solution)/shard_map/letters_of/pallas_call | solution.py:69
  4.3 7.3 %all-to-all-start = ((f32[8,9,128]{2,1,0:T(8,128)}), f32[8,9,128]{2,1,0:T(8,128)S(1)}, u32[]{:S(2)}, u32[]{:S(2)}) async-start(f32[8,9,128]{2,1,0:T(8,128)} %letters_of.1), calls=%async_computation | async-start | bytes 131072 | tf_op jit(solution)/shard_map/all_to_all | solution.py:634
  12.3 2.9 %collective-permute-start = (s16[8,192,128]{2,1,0:T(8,128)(2,1)}, s16[8,192,128]{2,1,0:T(8,128)(2,1)S(1)}, u32[]{:S(2)}, u32[]{:S(2)}) collective-permute-start(s16[8,192,128]{2,1,0:T(8,128)(2,1)} %slice.22), channel_id=1, source_target_pairs={{0,16},{4,20},{8,24},{12,28},{16,0},{20,4},{24,8},{28,12},{1,17},{... | collective-permute-start | bytes 1179656 | tf_op jit(solution)/shard_map/ppermute | solution.py:618
  15.3 10.5 %all-to-all-done.all_ref = f32[8,9,128]{2,1,0:T(8,128)S(1)} async-done(((f32[8,9,128]{2,1,0:T(8,128)}), f32[8,9,128]{2,1,0:T(8,128)S(1)}, u32[]{:S(2)}, u32[]{:S(2)}) %all-to-all-start) | async-done | bytes 36896 | tf_op jit(solution)/shard_map/all_to_all | solution.py:634
  26.4 2.5 %slot_tables.1.tab_ref = s32[65]{0:T(128)} custom-call(s32[1]{0:T(128)} %bitcast.me_ref, s32[8,24]{1,0:T(8,128)} %bitcast.38), custom_call_target="tpu_custom_call" | custom-call | flops 1 | bytes 1 | tf_op jit(solution)/shard_map/slot_tables/pallas_call | solution.py:128
  29.5 1.5 %pack_slots.2 = (s16[4,288,128]{2,1,0:T(8,128)(2,1)S(1)}, s16[4,288,128]{2,1,0:T(8,128)(2,1)}, s16[4,288,128]{2,1,0:T(8,128)(2,1)}, s16[4,288,128]{2,1,0:T(8,128)(2,1)S(1)}) custom-call(s32[65]{0:T(128)S(1)} %copy-done.9, s16[8,288,128]{2,1,0:T(8,128)(2,1)S(1)} %bitcast.34), custom_call_target="tpu_custom_call" | custom-call | flops 1 | bytes 1 | tf_op jit(solution)/shard_map/pack_slots/pallas_call | solution.py:155
  32.5 3.5 %collective-permute-start.7 = (s16[4,288,128]{2,1,0:T(8,128)(2,1)}, s16[4,288,128]{2,1,0:T(8,128)(2,1)S(1)}, u32[]{:S(2)}, u32[]{:S(2)}) collective-permute-start(s16[4,288,128]{2,1,0:T(8,128)(2,1)} %copy-done.12), channel_id=1, source_target_pairs={{0,12},{4,8},{8,4},{12,0},{16,28},{20,24},{24,20},{28,16},{1,13},{... | collective-permute-start | bytes 884744 | tf_op jit(solution)/shard_map/ppermute | solution.py:618
  36.0 1.9 %view_coefs.1 = (f32[24,16]{1,0:T(8,128)}, f32[24,7]{1,0:T(8,128)}, f32[24,7]{1,0:T(8,128)}) custom-call(s32[2,12]{1,0:T(2,128)} %bitcast.41, f32[8,9,128]{2,1,0:T(8,128)} %copy-done.13, f32[12,7]{1,0:T(8,128)} %copy.21.pair_ref), custom_call_target="tpu_custom_call" | custom-call | flops 1 | bytes 1 | tf_op jit(solution)/shard_map/view_coefs/pallas_call | solution.py:512
  37.9 2.5 %copy-done = bf16[12,2,3,36864]{3,1,2,0:T(2,128)(2,1)S(1)} copy-done((bf16[12,2,3,36864]{3,1,2,0:T(2,128)(2,1)S(1)}, bf16[12,2,3,36864]{3,1,2,0:T(2,128)(2,1)}, u32[]{:S(2)}) %copy-start) | copy-done | bytes 5308440
  41.1 4.7 %prepare_views.1 = (bf16[24,4,288,128]{3,2,1,0:T(8,128)(2,1)S(1)}, f32[24,2,288,128]{3,2,1,0:T(8,128)S(1)}) custom-call(f32[1]{0:T(128)} %bitcast.3.row_ref, f32[24,16]{1,0:T(8,128)S(1)} %copy-done.7, bf16[12,3,576,128]{3,2,1,0:T(8,128)(2,1)S(1)} %bitcast.31, bf16[12,576,128]{2,1,0:T(8,128)(2,1)S(1)} %bitcast.35), custom_call_target="tpu_custom_call" | custom-call | flops 1 | bytes 1 | tf_op jit(solution)/shard_map/prepare_views/pallas_call | solution.py:225
  47.2 2.9 %collective-permute-start.4 = (s16[4,288,128]{2,1,0:T(8,128)(2,1)S(1)}, s16[4,288,128]{2,1,0:T(8,128)(2,1)S(1)}, u32[]{:S(2)}, u32[]{:S(2)}) collective-permute-start(s16[4,288,128]{2,1,0:T(8,128)(2,1)S(1)} %get-tuple-element.96), channel_id=1, source_target_pairs={{0,12},{4,8},{8,4},{12,0},{16,28},{20,24},{24,20},{28,16},{1,13},{... | collective-permute-start | bytes 884744 | tf_op jit(solution)/shard_map/ppermute | solution.py:618
  50.1 5.7 %collective-permute-done.7.refs_3_ = s16[4,288,128]{2,1,0:T(8,128)(2,1)S(1)} collective-permute-done((s16[4,288,128]{2,1,0:T(8,128)(2,1)}, s16[4,288,128]{2,1,0:T(8,128)(2,1)S(1)}, u32[]{:S(2)}, u32[]{:S(2)}) %collective-permute-start.7) | collective-permute-done | bytes 294944 | tf_op jit(solution)/shard_map/ppermute | solution.py:618
  55.8 5.3 %view_sums.2.refs_0_ = f32[24,16,128]{2,1,0:T(8,128)S(1)} custom-call(s32[65]{0:T(128)S(1)} %copy-done.10, f32[24,16]{1,0:T(8,128)S(1)} %copy-done.8, f32[1]{0:T(128)} %bitcast.3.row_ref, bf16[24,4,288,128]{3,2,1,0:T(8,128)(2,1)S(1)} %get-tuple-element.97.view_ref, s16[4,288,128]{2,1,0:T(8,128)(2,1)S(1)} %get-tuple-element.98.refs_0_, ...), custom_call_target="tpu_custom_call" | custom-call | flops 1 | bytes 1 | tf_op jit(solution)/shard_map/view_sums/pallas_call | solution.py:332
  61.1 2.7 %depth_grads.2 = (s16[4,288,128]{2,1,0:T(8,128)(2,1)S(1)}, s16[4,288,128]{2,1,0:T(8,128)(2,1)}, s16[4,288,128]{2,1,0:T(8,128)(2,1)}, s16[4,288,128]{2,1,0:T(8,128)(2,1)S(1)}) custom-call(s32[65]{0:T(128)S(1)} %copy-done.10, f32[24,2,288,128]{3,2,1,0:T(8,128)S(1)} %get-tuple-element.102.slope_ref, s16[4,288,128]{2,1,0:T(8,128)(2,1)S(1)} %get-tuple-element.98.refs_0_, ...), custom_call_target="tpu_custom_call" | custom-call | flops 1 | bytes 1 | tf_op jit(solution)/shard_map/depth_grads/pallas_call | solution.py:270
  64.6 1.7 %depth_grads.3 = (s16[4,288,128]{2,1,0:T(8,128)(2,1)S(1)}, s16[4,288,128]{2,1,0:T(8,128)(2,1)S(1)}, s16[4,288,128]{2,1,0:T(8,128)(2,1)S(1)}, s16[4,288,128]{2,1,0:T(8,128)(2,1)S(1)}) custom-call(s32[65]{0:T(128)S(1)} %copy-done.10, f32[24,2,288,128]{3,2,1,0:T(8,128)S(1)} %get-tuple-element.102.slope_ref, s16[4,288,128]{2,1,0:T(8,128)(2,1)S(1)} %get-tuple-element.126.refs_0_, ...), custom_call_target="tpu_custom_call" | custom-call | flops 1 | bytes 1 | tf_op jit(solution)/shard_map/depth_grads/pallas_call | solution.py:270
  66.5 3.4 %collective-permute-start.10 = (s16[4,288,128]{2,1,0:T(8,128)(2,1)S(1)}, s16[4,288,128]{2,1,0:T(8,128)(2,1)S(1)}, u32[]{:S(2)}, u32[]{:S(2)}) collective-permute-start(s16[4,288,128]{2,1,0:T(8,128)(2,1)S(1)} %get-tuple-element.125), channel_id=1, source_target_pairs={{0,12},{4,8},{8,4},{12,0},{16,28},{20,24},{24,20},{28,16},{1,13},{... | collective-permute-start | bytes 884744 | tf_op jit(solution)/shard_map/ppermute | solution.py:618
  69.9 4.6 %view_sums.3.refs_1_ = f32[24,16,128]{2,1,0:T(8,128)S(1)} custom-call(s32[65]{0:T(128)S(1)} %copy-done.10, f32[24,16]{1,0:T(8,128)S(1)} %copy-done.8, f32[1]{0:T(128)} %bitcast.3.row_ref, bf16[24,4,288,128]{3,2,1,0:T(8,128)(2,1)S(1)} %get-tuple-element.97.view_ref, s16[4,288,128]{2,1,0:T(8,128)(2,1)S(1)} %get-tuple-element.126.refs_0_, ...), custom_call_target="tpu_custom_call" | custom-call | flops 1 | bytes 1 | tf_op jit(solution)/shard_map/view_sums/pallas_call | solution.py:332
  75.7 3.2 %collective-permute-done.10.refs_3_ = s16[4,288,128]{2,1,0:T(8,128)(2,1)S(1)} collective-permute-done((s16[4,288,128]{2,1,0:T(8,128)(2,1)S(1)}, s16[4,288,128]{2,1,0:T(8,128)(2,1)S(1)}, u32[]{:S(2)}, u32[]{:S(2)}) %collective-permute-start.10) | collective-permute-done | bytes 294944 | tf_op jit(solution)/shard_map/ppermute | solution.py:618
  78.8 2.2 %fold_slots.1 = s16[8,288,128]{2,1,0:T(8,128)(2,1)S(1)} custom-call(s32[65]{0:T(128)S(1)} %copy-done.10, s16[4,288,128]{2,1,0:T(8,128)(2,1)S(1)} %get-tuple-element.130.refs_0_, s16[4,288,128]{2,1,0:T(8,128)(2,1)S(1)} %collective-permute-done.8.refs_1_, s16[4,288,128]{2,1,0:T(8,128)(2,1)S(1)} %collective-permute-done.9.refs_2_, ...), custom_call_target="tpu_custom_call" | custom-call | flops 1 | bytes 1 | tf_op jit(solution)/shard_map/fold_slots/pallas_call | solution.py:372
  81.0 2.1 %collective-permute-start.16 = (s16[8,288,128]{2,1,0:T(8,128)(2,1)S(1)}, s16[8,288,128]{2,1,0:T(8,128)(2,1)S(1)}, u32[]{:S(2)}, u32[]{:S(2)}) collective-permute-start(s16[8,288,128]{2,1,0:T(8,128)(2,1)S(1)} %fold_slots.1), channel_id=1, source_target_pairs={{0,16},{4,20},{8,24},{12,28},{16,0},{20,4},{24,8},{28,12},{1,17},{... | collective-permute-start | bytes 1769480 | tf_op jit(solution)/shard_map/ppermute | solution.py:618
  83.2 2.7 %view_terms.1 = f32[76,7]{1,0:T(8,128)} custom-call(s32[2,12]{1,0:T(2,128)} %bitcast.42, f32[24,7]{1,0:T(8,128)} %get-tuple-element.111.cam_ref, f32[24,7]{1,0:T(8,128)} %get-tuple-element.112.pose_ref, f32[24,16,128]{2,1,0:T(8,128)} %copy-done.5, f32[24,16,128]{2,1,0:T(8,128)} %copy-done.6), custom_call_target="tpu_custom_call" | custom-call | flops 1 | bytes 1 | tf_op jit(solution)/shard_map/view_terms/pallas_call | solution.py:560
  85.9 2.1 %collective-permute-start.13 = (s16[4,288,128]{2,1,0:T(8,128)(2,1)}, s16[4,288,128]{2,1,0:T(8,128)(2,1)S(1)}, u32[]{:S(2)}, u32[]{:S(2)}) collective-permute-start(s16[4,288,128]{2,1,0:T(8,128)(2,1)} %get-tuple-element.138), channel_id=1, source_target_pairs={{0,4},{4,0},{8,12},{12,8},{16,20},{20,16},{24,28},{28,24},{1,5},{5... | collective-permute-start | bytes 884744 | tf_op jit(solution)/shard_map/ppermute | solution.py:618
  88.0 1.6 %collective-permute-start.14 = (s16[4,288,128]{2,1,0:T(8,128)(2,1)}, s16[4,288,128]{2,1,0:T(8,128)(2,1)S(1)}, u32[]{:S(2)}, u32[]{:S(2)}) collective-permute-start(s16[4,288,128]{2,1,0:T(8,128)(2,1)} %get-tuple-element.139), channel_id=1, source_target_pairs={{0,8},{4,12},{8,0},{12,4},{16,24},{20,28},{24,16},{28,20},{1,9},{5... | collective-permute-start | bytes 884744 | tf_op jit(solution)/shard_map/ppermute | solution.py:618
  91.6 1.5 %collective-permute-start.12 = (f32[76,7]{0,1:T(8,128)S(1)}, f32[76,7]{0,1:T(8,128)S(1)}, u32[]{:S(2)}, u32[]{:S(2)}) collective-permute-start(f32[76,7]{0,1:T(8,128)S(1)} %add.11), channel_id=1, source_target_pairs={{0,2},{1,3},{2,0},{3,1},{4,6},{5,7},{6,4},{7,5},{8,10},{9,11},{10,... | collective-permute-start | bytes 6392 | tf_op jit(solution)/shard_map/ppermute | solution.py:671
  93.1 2.1 %collective-permute-done.12 = f32[76,7]{0,1:T(8,128)S(1)} collective-permute-done((f32[76,7]{0,1:T(8,128)S(1)}, f32[76,7]{0,1:T(8,128)S(1)}, u32[]{:S(2)}, u32[]{:S(2)}) %collective-permute-start.12) | collective-permute-done | bytes 2160 | tf_op jit(solution)/shard_map/ppermute | solution.py:671
  95.9 4.2 %all-to-all-start.1 = ((f32[8,8,7]{2,1,0:T(8,128)}), f32[8,8,7]{2,1,0:T(8,128)}, u32[]{:S(2)}, u32[]{:S(2)}) async-start(f32[8,8,7]{2,1,0:T(8,128)} %bitcast.36), calls=%async_computation.1 | async-start | bytes 65536 | tf_op jit(solution)/shard_map/all_to_all | solution.py:675
  100.8 7.3 %collective-permute-done.14.refs_2_ = s16[4,288,128]{2,1,0:T(8,128)(2,1)S(1)} collective-permute-done((s16[4,288,128]{2,1,0:T(8,128)(2,1)}, s16[4,288,128]{2,1,0:T(8,128)(2,1)S(1)}, u32[]{:S(2)}, u32[]{:S(2)}) %collective-permute-start.14) | collective-permute-done | bytes 294944 | tf_op jit(solution)/shard_map/ppermute | solution.py:618
  108.1 3.1 %collective-permute-done.15.refs_3_ = s16[4,288,128]{2,1,0:T(8,128)(2,1)S(1)} collective-permute-done((s16[4,288,128]{2,1,0:T(8,128)(2,1)}, s16[4,288,128]{2,1,0:T(8,128)(2,1)S(1)}, u32[]{:S(2)}, u32[]{:S(2)}) %collective-permute-start.15) | collective-permute-done | bytes 294944 | tf_op jit(solution)/shard_map/ppermute | solution.py:618
  111.2 1.6 %fold_local.1.local_ref = f32[8,288,128]{2,1,0:T(8,128)S(1)} custom-call(s32[65]{0:T(128)S(1)} %copy-done.10, s16[4,288,128]{2,1,0:T(8,128)(2,1)S(1)} %get-tuple-element.137.refs_0_, s16[4,288,128]{2,1,0:T(8,128)(2,1)S(1)} %collective-permute-done.13.refs_1_, s16[4,288,128]{2,1,0:T(8,128)(2,1)S(1)} %collective-permute-done.14.refs_2_, ...), custom_call_target="tpu_custom_call" | custom-call | flops 1 | bytes 1 | tf_op jit(solution)/shard_map/fold_local/pallas_call | solution.py:390
  112.9 3.5 %update_depths.1 = (f32[8,36864]{1,0:T(8,128)}, f32[8,36864]{1,0:T(8,128)}, f32[8,36864]{1,0:T(8,128)}) custom-call(f32[8,288,128]{2,1,0:T(8,128)S(1)} %fold_local.1.local_ref, s16[8,288,128]{2,1,0:T(8,128)(2,1)S(1)} %collective-permute-done.16.far_ref, f32[8,36864]{1,0:T(8,128)S(1)} %copy-done.1, f32[8,36864]{1,0:T(8,128)S(1)} %copy-done.3, ...), custom_call_target="tpu_custom_call" | custom-call | flops 1 | bytes 1 | tf_op jit(solution)/shard_map/update_depths/pallas_call | solution.py:430
  116.4 1.4 %update_small.1 = (f32[8,7]{1,0:T(8,128)}, f32[8,7]{1,0:T(8,128)}, f32[8,7]{1,0:T(8,128)}, f32[7,12]{1,0:T(8,128)}, f32[7,12]{1,0:T(8,128)}, /*index=5*/f32[7,12]{1,0:T(8,128)}) custom-call(f32[8,8,7]{2,1,0:T(8,128)} %all-to-all-done.1.mail_ref, f32[7,12]{1,0:T(8,128)} %slice_bitcast_fusion.pose_ref, f32[8,7]{1,0:T(8,128)} %refs_0_.1, f32[8,7]{1,0:T(8,128)} %refs_1_.1, ...), custom_call_target="tpu_custom_call" | custom-call | flops 1 | bytes 1 | tf_op jit(solution)/shard_map/update_small/pallas_call | solution.py:582
  (62 shorter events, 11.8 us)
Async XLA Ops:
  2.2 29.6 %copy-start.14 = (f32[12,7]{0,1:T(8,128)S(1)}, f32[12,7]{0,1:T(8,128)}, u32[]{:S(2)}) copy-start(f32[12,7]{0,1:T(8,128)} %param.19) | copy-start | bytes 1012
  2.3 35.6 %copy-start.2 = (bf16[12,2,36864]{2,1,0:T(2,128)(2,1)S(1)}, bf16[12,2,36864]{2,1,0:T(2,128)(2,1)}, u32[]{:S(2)}) copy-start(bf16[12,2,36864]{2,1,0:T(2,128)(2,1)} %param.23) | copy-start | bytes 5308420
  4.3 21.4 %all-to-all-start = ((f32[8,9,128]{2,1,0:T(8,128)}), f32[8,9,128]{2,1,0:T(8,128)S(1)}, u32[]{:S(2)}, u32[]{:S(2)}) async-start(f32[8,9,128]{2,1,0:T(8,128)} %letters_of.1), calls=%async_computation | async-start | bytes 131072 | tf_op jit(solution)/shard_map/all_to_all | solution.py:634
  12.3 33.5 %collective-permute-start = (s16[8,192,128]{2,1,0:T(8,128)(2,1)}, s16[8,192,128]{2,1,0:T(8,128)(2,1)S(1)}, u32[]{:S(2)}, u32[]{:S(2)}) collective-permute-start(s16[8,192,128]{2,1,0:T(8,128)(2,1)} %slice.22), channel_id=1, source_target_pairs={{0,16},{4,20},{8,24},{12,28},{16,0},{20,4},{24,8},{28,12},{1,17},{... | collective-permute-start | bytes 1179656 | tf_op jit(solution)/shard_map/ppermute | solution.py:618
  31.1 0.7 copy-start.12
  31.8 15.4 %collective-permute-start.5 = (s16[4,288,128]{2,1,0:T(8,128)(2,1)}, s16[4,288,128]{2,1,0:T(8,128)(2,1)S(1)}, u32[]{:S(2)}, u32[]{:S(2)}) collective-permute-start(s16[4,288,128]{2,1,0:T(8,128)(2,1)} %get-tuple-element.99), channel_id=1, source_target_pairs={{0,4},{4,0},{8,12},{12,8},{16,20},{20,16},{24,28},{28,24},{1,5},{5... | collective-permute-start | bytes 884744 | tf_op jit(solution)/shard_map/ppermute | solution.py:618
  31.8 14.0 %collective-permute-start.1 = (s16[8,96,128]{2,1,0:T(8,128)(2,1)}, s16[8,96,128]{2,1,0:T(8,128)(2,1)S(1)}, u32[]{:S(2)}, u32[]{:S(2)}) collective-permute-start(s16[8,96,128]{2,1,0:T(8,128)(2,1)} %slice.20), channel_id=1, source_target_pairs={{0,16},{4,20},{8,24},{12,28},{16,0},{20,4},{24,8},{28,12},{1,17},{... | collective-permute-start | bytes 589832 | tf_op jit(solution)/shard_map/ppermute | solution.py:618
  32.5 17.6 %collective-permute-start.6 = (s16[4,288,128]{2,1,0:T(8,128)(2,1)}, s16[4,288,128]{2,1,0:T(8,128)(2,1)S(1)}, u32[]{:S(2)}, u32[]{:S(2)}) collective-permute-start(s16[4,288,128]{2,1,0:T(8,128)(2,1)} %get-tuple-element.100), channel_id=1, source_target_pairs={{0,8},{4,12},{8,0},{12,4},{16,24},{20,28},{24,16},{28,20},{1,9},{5... | collective-permute-start | bytes 884744 | tf_op jit(solution)/shard_map/ppermute | solution.py:618
  32.5 23.3 %collective-permute-start.7 = (s16[4,288,128]{2,1,0:T(8,128)(2,1)}, s16[4,288,128]{2,1,0:T(8,128)(2,1)S(1)}, u32[]{:S(2)}, u32[]{:S(2)}) collective-permute-start(s16[4,288,128]{2,1,0:T(8,128)(2,1)} %copy-done.12), channel_id=1, source_target_pairs={{0,12},{4,8},{8,4},{12,0},{16,28},{20,24},{24,20},{28,16},{1,13},{... | collective-permute-start | bytes 884744 | tf_op jit(solution)/shard_map/ppermute | solution.py:618
  37.9 2.5 %copy-start = (bf16[12,2,3,36864]{3,1,2,0:T(2,128)(2,1)S(1)}, bf16[12,2,3,36864]{3,1,2,0:T(2,128)(2,1)}, u32[]{:S(2)}) copy-start(bf16[12,2,3,36864]{3,1,2,0:T(2,128)(2,1)} %param.22) | copy-start | bytes 15925252
  40.4 0.7 copy-start.7
  41.1 4.7 %copy-start.10 = (s32[65]{0:T(128)S(1)}, s32[65]{0:T(128)}, u32[]{:S(2)}) copy-start(s32[65]{0:T(128)} %slot_tables.1.tab_ref) | copy-start | bytes 784
  41.1 14.7 %copy-start.8 = (f32[24,16]{1,0:T(8,128)S(1)}, f32[24,16]{1,0:T(8,128)}, u32[]{:S(2)}) copy-start(f32[24,16]{1,0:T(8,128)} %get-tuple-element.89.coef_ref) | copy-start | bytes 4612
  46.6 17.3 %collective-permute-start.2 = (s16[4,288,128]{2,1,0:T(8,128)(2,1)S(1)}, s16[4,288,128]{2,1,0:T(8,128)(2,1)S(1)}, u32[]{:S(2)}, u32[]{:S(2)}) collective-permute-start(s16[4,288,128]{2,1,0:T(8,128)(2,1)S(1)} %get-tuple-element.94), channel_id=1, source_target_pairs={{0,4},{4,0},{8,12},{12,8},{16,20},{20,16},{24,28},{28,24},{1,5},{5... | collective-permute-start | bytes 884744 | tf_op jit(solution)/shard_map/ppermute | solution.py:618
  46.6 17.2 %collective-permute-start.3 = (s16[4,288,128]{2,1,0:T(8,128)(2,1)S(1)}, s16[4,288,128]{2,1,0:T(8,128)(2,1)S(1)}, u32[]{:S(2)}, u32[]{:S(2)}) collective-permute-start(s16[4,288,128]{2,1,0:T(8,128)(2,1)S(1)} %get-tuple-element.95), channel_id=1, source_target_pairs={{0,8},{4,12},{8,0},{12,4},{16,24},{20,28},{24,16},{28,20},{1,9},{5... | collective-permute-start | bytes 884744 | tf_op jit(solution)/shard_map/ppermute | solution.py:618
  47.2 17.4 %collective-permute-start.4 = (s16[4,288,128]{2,1,0:T(8,128)(2,1)S(1)}, s16[4,288,128]{2,1,0:T(8,128)(2,1)S(1)}, u32[]{:S(2)}, u32[]{:S(2)}) collective-permute-start(s16[4,288,128]{2,1,0:T(8,128)(2,1)S(1)} %get-tuple-element.96), channel_id=1, source_target_pairs={{0,12},{4,8},{8,4},{12,0},{16,28},{20,24},{24,20},{28,16},{1,13},{... | collective-permute-start | bytes 884744 | tf_op jit(solution)/shard_map/ppermute | solution.py:618
  61.1 2.7 %copy-start.5 = (f32[24,16,128]{2,1,0:T(8,128)}, f32[24,16,128]{2,1,0:T(8,128)S(1)}, u32[]{:S(2)}) copy-start(f32[24,16,128]{2,1,0:T(8,128)S(1)} %view_sums.2.refs_0_) | copy-start | bytes 589828
  63.8 2.5 %copy-start.11 = (s16[4,288,128]{2,1,0:T(8,128)(2,1)}, s16[4,288,128]{2,1,0:T(8,128)(2,1)S(1)}, u32[]{:S(2)}) copy-start(s16[4,288,128]{2,1,0:T(8,128)(2,1)S(1)} %get-tuple-element.140) | copy-start | bytes 884740
  66.3 9.3 %collective-permute-start.8 = (s16[4,288,128]{2,1,0:T(8,128)(2,1)S(1)}, s16[4,288,128]{2,1,0:T(8,128)(2,1)S(1)}, u32[]{:S(2)}, u32[]{:S(2)}) collective-permute-start(s16[4,288,128]{2,1,0:T(8,128)(2,1)S(1)} %get-tuple-element.123), channel_id=1, source_target_pairs={{0,4},{4,0},{8,12},{12,8},{16,20},{20,16},{24,28},{28,24},{1,5},{5... | collective-permute-start | bytes 884744 | tf_op jit(solution)/shard_map/ppermute | solution.py:618
  66.4 9.3 %collective-permute-start.9 = (s16[4,288,128]{2,1,0:T(8,128)(2,1)S(1)}, s16[4,288,128]{2,1,0:T(8,128)(2,1)S(1)}, u32[]{:S(2)}, u32[]{:S(2)}) collective-permute-start(s16[4,288,128]{2,1,0:T(8,128)(2,1)S(1)} %get-tuple-element.124), channel_id=1, source_target_pairs={{0,8},{4,12},{8,0},{12,4},{16,24},{20,28},{24,16},{28,20},{1,9},{5... | collective-permute-start | bytes 884744 | tf_op jit(solution)/shard_map/ppermute | solution.py:618
  66.5 12.3 %collective-permute-start.10 = (s16[4,288,128]{2,1,0:T(8,128)(2,1)S(1)}, s16[4,288,128]{2,1,0:T(8,128)(2,1)S(1)}, u32[]{:S(2)}, u32[]{:S(2)}) collective-permute-start(s16[4,288,128]{2,1,0:T(8,128)(2,1)S(1)} %get-tuple-element.125), channel_id=1, source_target_pairs={{0,12},{4,8},{8,4},{12,0},{16,28},{20,24},{24,20},{28,16},{1,13},{... | collective-permute-start | bytes 884744 | tf_op jit(solution)/shard_map/ppermute | solution.py:618
  74.5 0.7 copy-start.6
  78.8 34.0 %copy-start.4 = (f32[8,36864]{1,0:T(8,128)S(1)}, f32[8,36864]{1,0:T(8,128)}, u32[]{:S(2)}) copy-start(f32[8,36864]{1,0:T(8,128)} %s_ref.1) | copy-start | bytes 3538948
  81.0 31.8 %collective-permute-start.16 = (s16[8,288,128]{2,1,0:T(8,128)(2,1)S(1)}, s16[8,288,128]{2,1,0:T(8,128)(2,1)S(1)}, u32[]{:S(2)}, u32[]{:S(2)}) collective-permute-start(s16[8,288,128]{2,1,0:T(8,128)(2,1)S(1)} %fold_slots.1), channel_id=1, source_target_pairs={{0,16},{4,20},{8,24},{12,28},{16,0},{20,4},{24,8},{28,12},{1,17},{... | collective-permute-start | bytes 1769480 | tf_op jit(solution)/shard_map/ppermute | solution.py:618
  85.9 14.9 %collective-permute-start.13 = (s16[4,288,128]{2,1,0:T(8,128)(2,1)}, s16[4,288,128]{2,1,0:T(8,128)(2,1)S(1)}, u32[]{:S(2)}, u32[]{:S(2)}) collective-permute-start(s16[4,288,128]{2,1,0:T(8,128)(2,1)} %get-tuple-element.138), channel_id=1, source_target_pairs={{0,4},{4,0},{8,12},{12,8},{16,20},{20,16},{24,28},{28,24},{1,5},{5... | collective-permute-start | bytes 884744 | tf_op jit(solution)/shard_map/ppermute | solution.py:618
  88.0 20.2 %collective-permute-start.14 = (s16[4,288,128]{2,1,0:T(8,128)(2,1)}, s16[4,288,128]{2,1,0:T(8,128)(2,1)S(1)}, u32[]{:S(2)}, u32[]{:S(2)}) collective-permute-start(s16[4,288,128]{2,1,0:T(8,128)(2,1)} %get-tuple-element.139), channel_id=1, source_target_pairs={{0,8},{4,12},{8,0},{12,4},{16,24},{20,28},{24,16},{28,20},{1,9},{5... | collective-permute-start | bytes 884744 | tf_op jit(solution)/shard_map/ppermute | solution.py:618
  89.6 21.6 %collective-permute-start.15 = (s16[4,288,128]{2,1,0:T(8,128)(2,1)}, s16[4,288,128]{2,1,0:T(8,128)(2,1)S(1)}, u32[]{:S(2)}, u32[]{:S(2)}) collective-permute-start(s16[4,288,128]{2,1,0:T(8,128)(2,1)} %copy-done.11), channel_id=1, source_target_pairs={{0,12},{4,8},{8,4},{12,0},{16,28},{20,24},{24,20},{28,16},{1,13},{... | collective-permute-start | bytes 884744 | tf_op jit(solution)/shard_map/ppermute | solution.py:618
  90.4 1.2 collective-permute-start.11
  91.6 3.6 %collective-permute-start.12 = (f32[76,7]{0,1:T(8,128)S(1)}, f32[76,7]{0,1:T(8,128)S(1)}, u32[]{:S(2)}, u32[]{:S(2)}) collective-permute-start(f32[76,7]{0,1:T(8,128)S(1)} %add.11), channel_id=1, source_target_pairs={{0,2},{1,3},{2,0},{3,1},{4,6},{5,7},{6,4},{7,5},{8,10},{9,11},{10,... | collective-permute-start | bytes 6392 | tf_op jit(solution)/shard_map/ppermute | solution.py:671
  95.9 20.4 %all-to-all-start.1 = ((f32[8,8,7]{2,1,0:T(8,128)}), f32[8,8,7]{2,1,0:T(8,128)}, u32[]{:S(2)}, u32[]{:S(2)}) async-start(f32[8,8,7]{2,1,0:T(8,128)} %bitcast.36), calls=%async_computation.1 | async-start | bytes 65536 | tf_op jit(solution)/shard_map/all_to_all | solution.py:675
  100.8 12.0 %copy-start.1 = (f32[8,36864]{1,0:T(8,128)S(1)}, f32[8,36864]{1,0:T(8,128)}, u32[]{:S(2)}) copy-start(f32[8,36864]{1,0:T(8,128)} %x_ref.1) | copy-start | bytes 3538948
  100.8 12.1 %copy-start.3 = (f32[8,36864]{1,0:T(8,128)S(1)}, f32[8,36864]{1,0:T(8,128)}, u32[]{:S(2)}) copy-start(f32[8,36864]{1,0:T(8,128)} %m_ref.1) | copy-start | bytes 3538948
  (2 other events, 1.3 us)

commit v4 on v3

--- a/solution.py
+++ b/solution.py
@@ -25,6 +25,7 @@
 DEPTH_MID = 2.25
 DEPTH_STEP = 1.75 / 32766.0
 VIEW_BOUND = 340.0
+SLOT_UNIT = VIEW_BOUND / 32766.0**2
 CODE_UNIT = 8.0
 INTS = jnp.int16
 SUMS = 11
@@ -33,7 +34,17 @@
 SMEM = pl.BlockSpec(memory_space=pltpu.SMEM)
 VMEM = pl.BlockSpec(memory_space=pltpu.VMEM)
 COST = pl.CostEstimate(flops=1, bytes_accessed=1, transcendentals=0)
-PARAMS = pltpu.CompilerParams(vmem_limit_bytes=32 * 1024 * 1024)
+PARAMS = pltpu.CompilerParams(vmem_limit_bytes=16 * 1024 * 1024)
+
+
+def encode_slot(value):
+    root = value * lax.rsqrt(jnp.maximum(jnp.abs(value), 1e-20))
+    return jnp.round(root).astype(jnp.int32).astype(INTS)
+
+
+def decode_slot(code):
+    root = code.astype(jnp.int32).astype(jnp.float32)
+    return root * jnp.abs(root)
 
 
 def code_scale(bound):
@@ -258,7 +269,7 @@
                     here = slice(t, t + 16)
                     code = depth_ref[c, here].astype(jnp.int32).astype(jnp.float32)
                     along = code * slope_ref[view, 0, here] + slope_ref[view, 1, here]
-                    grad_ref[c, here] = encode(jnp.abs(along), along < 0.0, VIEW_BOUND)
+                    grad_ref[c, here] = encode_slot(along)
 
 
 def depth_grads(table, slopes, depths, first, half, cap, by_rank):
@@ -352,7 +363,7 @@
 
             @pl.when(image >= 0)
             def _():
-                total_ref[image] += decode(slot_ref[c], VIEW_BOUND)
+                total_ref[image] += decode_slot(slot_ref[c])
 
 
 def fold_kernel(first, cap, bound, half, tab_ref, *refs):
@@ -364,7 +375,9 @@
         @pl.loop(0, total.shape[0])
         def _(i):
             value = total[i, part * rows : (part + 1) * rows]
-            out_ref[i] = encode(jnp.abs(value) * (1.0 / CODE_UNIT), value < 0.0, bound)
+            out_ref[i] = encode(
+                jnp.abs(value) * (SLOT_UNIT / CODE_UNIT), value < 0.0, bound
+            )
 
 
 def fold_slots(table, slots, first, images, cap, bound, parts):
@@ -412,7 +425,9 @@
     nx_ref, nm_ref, ns_ref, grad = refs[-4:]
     images, rows, _ = local_ref.shape
     for i in range(images):
-        grad[i * rows : (i + 1) * rows] = local_ref[i] + decode(far_ref[i], bound)
+        grad[i * rows : (i + 1) * rows] = local_ref[i] * SLOT_UNIT + decode(
+            far_ref[i], bound
+        )
     for t in range(rows):
         here = slice(t * LANES, (t + 1) * LANES)
         gradient = grad[pl.ds(t, images, stride=rows), :]
@@ -502,7 +517,7 @@
     rows += [matrix[j][1] * inverse_focal for j in range(3)]
     rows += [matrix[j][2] for j in range(3)]
     rows += shift
-    rows += [scale * scale * (1.0 / CODE_UNIT)]
+    rows += [scale * scale * (1.0 / SLOT_UNIT)]
     for i, row in enumerate(rows):
         out_ref[:, i : i + 1] = row
 
@@ -628,7 +643,7 @@
     letters = letters_of(names, cameras, shards)
     codes = jnp.round((depths - DEPTH_MID) * (1.0 / DEPTH_STEP)).astype(INTS)
     codes = codes.reshape(images, rows, LANES)
-    first = rows // 48 * 16 * 2
+    first = rows // 2
     parts = [codes[:, :first], codes[:, first:]]
     letters, parts[1:] = tie((letters, parts[1:]))
     mail = lax.all_to_all(letters, "img", 0, 0, tiled=True)

time: 118 us -> 114 us (0.966)
  starting transfers between devices: 32.3 us -> 30.1 us
  Pallas kernels: 38.5 us -> 37.1 us
  local copies, waits for them, and re-layouts: 9.72 us -> 8.39 us
    all_to_all x1, waiting for transfers between devices: 10.5 us -> 14.6 us  [body(): mail = lax.all_to_all(letters, 'img', 0, 0, tiled=True)]
    ppermute x15, waiting for transfers between devices: 20.6 us -> 16.8 us  [swap(): return lax.ppermute(value, 'img', [(i, i ^ k) for i in range(shards)])]
    ppermute x15, starting transfers between devices: 19.3 us -> 17.1 us  [swap(): return lax.ppermute(value, 'img', [(i, i ^ k) for i in range(shards)])]
    unnamed x32 -> x30, local copies, waits for them, and re-layouts: 6.05 us -> 5.33 us
  transfers between devices with their start and end apart: 19 -> 19, of which waited for: 9 -> 9; matrix products, arithmetic and copies ran while one was open for 4% -> 3% of each run, Pallas kernels for 27% -> 28%
where the time goes in v4:
time: 114 us; the launch traced here: 113 us
  Pallas kernels  37.1 us (33%)
  waiting for transfers between devices  34.7 us (30%)
  starting transfers between devices  30.1 us (26%)
  local copies, waits for them, and re-layouts  8.39 us (7%)
  other arithmetic  2.14 us (2%)
    ppermute x15, starting transfers between devices, swap(): return lax.ppermute(value, 'img', [(i, i ^ k) for i in range(shards)])  17.1 us
    ppermute x15, waiting for transfers between devices, swap(): return lax.ppermute(value, 'img', [(i, i ^ k) for i in range(shards)])  16.8 us
    all_to_all x1, waiting for transfers between devices, body(): mail = lax.all_to_all(letters, 'img', 0, 0, tiled=True)  14.6 us
    pallas_call x2, Pallas kernels, view_sums(): pl.pallas_call(functools.partial(sum_kernel, first, half, cap), out_shape...  9.88 us
    all_to_all x1, starting transfers between devices, body(): mail = lax.all_to_all(letters, 'img', 0, 0, tiled=True)  7.25 us
    unnamed x30, local copies, waits for them, and re-layouts  5.33 us
    pallas_call x1, Pallas kernels, prepare_views(): pl.pallas_call(prepare_kernel, out_shape=[jax.ShapeDtypeStruct((2 * pairs...  4.67 us
    all_to_all x1, starting transfers between devices, body(): lax.all_to_all(small[:shards * images].reshape(shards, images, 7), 'img',...  4.18 us
  transfers between devices with their start and end apart: 19, of which 9 were waited for; matrix products, arithmetic and copies ran while one was open for 3% of the time, Pallas kernels for 28%

profile of v4, /device:TPU:0, one launch (start us, length us, event | category | flops | bytes accessed | tf_op | source)
XLA Modules:
  0.0 113.3 jit_solution(441408785615074185)
XLA Ops:
  0.6 1.5 %fusion = s16[1,8,288,128]{3,1,2,0:T(8,128)(2,1)S(1)} fusion(f32[8,36864]{1,0:T(8,128)} %x_ref.1), kind=kLoop, calls=%fused_computation.1 | loop fusion | flops 1179648 | bytes 1769472
  4.5 7.3 %all-to-all-start = ((f32[8,9,128]{2,1,0:T(8,128)}), f32[8,9,128]{2,1,0:T(8,128)S(1)}, u32[]{:S(2)}, u32[]{:S(2)}) async-start(f32[8,9,128]{2,1,0:T(8,128)} %letters_of.1), calls=%async_computation | async-start | bytes 131072 | tf_op jit(solution)/shard_map/all_to_all | solution.py:649
  11.7 2.9 %collective-permute-start = (s16[8,144,128]{2,1,0:T(8,128)(2,1)}, s16[8,144,128]{2,1,0:T(8,128)(2,1)S(1)}, u32[]{:S(2)}, u32[]{:S(2)}) collective-permute-start(s16[8,144,128]{2,1,0:T(8,128)(2,1)} %get-tuple-element.155), channel_id=1, source_target_pairs={{0,16},{4,20},{8,24},{12,28},{16,0},{20,4},{24,8},{28,12},{1,17},{... | collective-permute-start | bytes 884744 | tf_op jit(solution)/shard_map/ppermute | solution.py:633
  14.7 14.6 %all-to-all-done.all_ref = f32[8,9,128]{2,1,0:T(8,128)S(1)} async-done(((f32[8,9,128]{2,1,0:T(8,128)}), f32[8,9,128]{2,1,0:T(8,128)S(1)}, u32[]{:S(2)}, u32[]{:S(2)}) %all-to-all-start) | async-done | bytes 36896 | tf_op jit(solution)/shard_map/all_to_all | solution.py:649
  29.9 2.5 %slot_tables.1.tab_ref = s32[65]{0:T(128)} custom-call(s32[1]{0:T(128)} %bitcast.me_ref, s32[8,24]{1,0:T(8,128)} %bitcast.37), custom_call_target="tpu_custom_call" | custom-call | flops 1 | bytes 1 | tf_op jit(solution)/shard_map/slot_tables/pallas_call | solution.py:139
  33.1 1.5 %pack_slots.2 = (s16[4,288,128]{2,1,0:T(8,128)(2,1)S(1)}, s16[4,288,128]{2,1,0:T(8,128)(2,1)}, s16[4,288,128]{2,1,0:T(8,128)(2,1)}, s16[4,288,128]{2,1,0:T(8,128)(2,1)S(1)}) custom-call(s32[65]{0:T(128)S(1)} %copy-done.9, s16[8,288,128]{2,1,0:T(8,128)(2,1)S(1)} %bitcast.33), custom_call_target="tpu_custom_call" | custom-call | flops 1 | bytes 1 | tf_op jit(solution)/shard_map/pack_slots/pallas_call | solution.py:166
  34.6 1.4 %collective-permute-start.5 = (s16[4,288,128]{2,1,0:T(8,128)(2,1)}, s16[4,288,128]{2,1,0:T(8,128)(2,1)S(1)}, u32[]{:S(2)}, u32[]{:S(2)}) collective-permute-start(s16[4,288,128]{2,1,0:T(8,128)(2,1)} %get-tuple-element.99), channel_id=1, source_target_pairs={{0,4},{4,0},{8,12},{12,8},{16,20},{20,16},{24,28},{28,24},{1,5},{5... | collective-permute-start | bytes 884744 | tf_op jit(solution)/shard_map/ppermute | solution.py:633
  36.8 2.0 %collective-permute-start.7 = (s16[4,288,128]{2,1,0:T(8,128)(2,1)S(1)}, s16[4,288,128]{2,1,0:T(8,128)(2,1)S(1)}, u32[]{:S(2)}, u32[]{:S(2)}) collective-permute-start(s16[4,288,128]{2,1,0:T(8,128)(2,1)S(1)} %get-tuple-element.101), channel_id=1, source_target_pairs={{0,12},{4,8},{8,4},{12,0},{16,28},{20,24},{24,20},{28,16},{1,13},{... | collective-permute-start | bytes 884744 | tf_op jit(solution)/shard_map/ppermute | solution.py:633
  38.8 1.9 %view_coefs.1 = (f32[24,16]{1,0:T(8,128)}, f32[24,7]{1,0:T(8,128)}, f32[24,7]{1,0:T(8,128)}) custom-call(s32[2,12]{1,0:T(2,128)} %bitcast.40, f32[8,9,128]{2,1,0:T(8,128)} %copy-done.12, f32[12,7]{1,0:T(8,128)} %copy.21.pair_ref), custom_call_target="tpu_custom_call" | custom-call | flops 1 | bytes 1 | tf_op jit(solution)/shard_map/view_coefs/pallas_call | solution.py:527
  40.7 2.5 %copy-done = bf16[12,2,3,36864]{3,1,2,0:T(2,128)(2,1)S(1)} copy-done((bf16[12,2,3,36864]{3,1,2,0:T(2,128)(2,1)S(1)}, bf16[12,2,3,36864]{3,1,2,0:T(2,128)(2,1)}, u32[]{:S(2)}) %copy-start) | copy-done | bytes 5308440
  43.9 4.7 %prepare_views.1 = (bf16[24,4,288,128]{3,2,1,0:T(8,128)(2,1)S(1)}, f32[24,2,288,128]{3,2,1,0:T(8,128)S(1)}) custom-call(f32[1]{0:T(128)} %bitcast.3.row_ref, f32[24,16]{1,0:T(8,128)S(1)} %copy-done.7, bf16[12,3,576,128]{3,2,1,0:T(8,128)(2,1)S(1)} %bitcast.31, bf16[12,576,128]{2,1,0:T(8,128)(2,1)S(1)} %bitcast.34), custom_call_target="tpu_custom_call" | custom-call | flops 1 | bytes 1 | tf_op jit(solution)/shard_map/prepare_views/pallas_call | solution.py:236
  49.8 1.5 %collective-permute-start.2 = (s16[4,288,128]{2,1,0:T(8,128)(2,1)S(1)}, s16[4,288,128]{2,1,0:T(8,128)(2,1)S(1)}, u32[]{:S(2)}, u32[]{:S(2)}) collective-permute-start(s16[4,288,128]{2,1,0:T(8,128)(2,1)S(1)} %get-tuple-element.94), channel_id=1, source_target_pairs={{0,4},{4,0},{8,12},{12,8},{16,20},{20,16},{24,28},{28,24},{1,5},{5... | collective-permute-start | bytes 884744 | tf_op jit(solution)/shard_map/ppermute | solution.py:633
  51.3 2.0 %collective-permute-start.4 = (s16[4,288,128]{2,1,0:T(8,128)(2,1)S(1)}, s16[4,288,128]{2,1,0:T(8,128)(2,1)S(1)}, u32[]{:S(2)}, u32[]{:S(2)}) collective-permute-start(s16[4,288,128]{2,1,0:T(8,128)(2,1)S(1)} %get-tuple-element.96), channel_id=1, source_target_pairs={{0,12},{4,8},{8,4},{12,0},{16,28},{20,24},{24,20},{28,16},{1,13},{... | collective-permute-start | bytes 884744 | tf_op jit(solution)/shard_map/ppermute | solution.py:633
  53.4 2.1 %collective-permute-done.7.refs_3_ = s16[4,288,128]{2,1,0:T(8,128)(2,1)S(1)} collective-permute-done((s16[4,288,128]{2,1,0:T(8,128)(2,1)S(1)}, s16[4,288,128]{2,1,0:T(8,128)(2,1)S(1)}, u32[]{:S(2)}, u32[]{:S(2)}) %collective-permute-start.7) | collective-permute-done | bytes 294944 | tf_op jit(solution)/shard_map/ppermute | solution.py:633
  55.5 4.9 %view_sums.2.refs_0_ = f32[24,16,128]{2,1,0:T(8,128)S(1)} custom-call(s32[65]{0:T(128)S(1)} %copy-done.10, f32[24,16]{1,0:T(8,128)S(1)} %copy-done.8, f32[1]{0:T(128)} %bitcast.3.row_ref, bf16[24,4,288,128]{3,2,1,0:T(8,128)(2,1)S(1)} %get-tuple-element.97.view_ref, s16[4,288,128]{2,1,0:T(8,128)(2,1)S(1)} %get-tuple-element.98.refs_0_, ...), custom_call_target="tpu_custom_call" | custom-call | flops 1 | bytes 1 | tf_op jit(solution)/shard_map/view_sums/pallas_call | solution.py:343
  60.4 2.2 %depth_grads.2 = (s16[4,288,128]{2,1,0:T(8,128)(2,1)S(1)}, s16[4,288,128]{2,1,0:T(8,128)(2,1)}, s16[4,288,128]{2,1,0:T(8,128)(2,1)}, s16[4,288,128]{2,1,0:T(8,128)(2,1)S(1)}) custom-call(s32[65]{0:T(128)S(1)} %copy-done.10, f32[24,2,288,128]{3,2,1,0:T(8,128)S(1)} %get-tuple-element.102.slope_ref, s16[4,288,128]{2,1,0:T(8,128)(2,1)S(1)} %get-tuple-element.98.refs_0_, ...), custom_call_target="tpu_custom_call" | custom-call | flops 1 | bytes 1 | tf_op jit(solution)/shard_map/depth_grads/pallas_call | solution.py:281
  62.7 1.6 %collective-permute-done.4.refs_3_ = s16[4,288,128]{2,1,0:T(8,128)(2,1)S(1)} collective-permute-done((s16[4,288,128]{2,1,0:T(8,128)(2,1)S(1)}, s16[4,288,128]{2,1,0:T(8,128)(2,1)S(1)}, u32[]{:S(2)}, u32[]{:S(2)}) %collective-permute-start.4) | collective-permute-done | bytes 294944 | tf_op jit(solution)/shard_map/ppermute | solution.py:633
  64.3 1.4 %depth_grads.3 = (s16[4,288,128]{2,1,0:T(8,128)(2,1)S(1)}, s16[4,288,128]{2,1,0:T(8,128)(2,1)S(1)}, s16[4,288,128]{2,1,0:T(8,128)(2,1)S(1)}, s16[4,288,128]{2,1,0:T(8,128)(2,1)S(1)}) custom-call(s32[65]{0:T(128)S(1)} %copy-done.10, f32[24,2,288,128]{3,2,1,0:T(8,128)S(1)} %get-tuple-element.102.slope_ref, s16[4,288,128]{2,1,0:T(8,128)(2,1)S(1)} %get-tuple-element.126.refs_0_, ...), custom_call_target="tpu_custom_call" | custom-call | flops 1 | bytes 1 | tf_op jit(solution)/shard_map/depth_grads/pallas_call | solution.py:281
  66.2 3.1 %collective-permute-start.10 = (s16[4,288,128]{2,1,0:T(8,128)(2,1)S(1)}, s16[4,288,128]{2,1,0:T(8,128)(2,1)S(1)}, u32[]{:S(2)}, u32[]{:S(2)}) collective-permute-start(s16[4,288,128]{2,1,0:T(8,128)(2,1)S(1)} %get-tuple-element.125), channel_id=1, source_target_pairs={{0,12},{4,8},{8,4},{12,0},{16,28},{20,24},{24,20},{28,16},{1,13},{... | collective-permute-start | bytes 884744 | tf_op jit(solution)/shard_map/ppermute | solution.py:633
  69.3 4.9 %view_sums.3.refs_1_ = f32[24,16,128]{2,1,0:T(8,128)S(1)} custom-call(s32[65]{0:T(128)S(1)} %copy-done.10, f32[24,16]{1,0:T(8,128)S(1)} %copy-done.8, f32[1]{0:T(128)} %bitcast.3.row_ref, bf16[24,4,288,128]{3,2,1,0:T(8,128)(2,1)S(1)} %get-tuple-element.97.view_ref, s16[4,288,128]{2,1,0:T(8,128)(2,1)S(1)} %get-tuple-element.126.refs_0_, ...), custom_call_target="tpu_custom_call" | custom-call | flops 1 | bytes 1 | tf_op jit(solution)/shard_map/view_sums/pallas_call | solution.py:343
  75.1 3.7 %collective-permute-done.10.refs_3_ = s16[4,288,128]{2,1,0:T(8,128)(2,1)S(1)} collective-permute-done((s16[4,288,128]{2,1,0:T(8,128)(2,1)S(1)}, s16[4,288,128]{2,1,0:T(8,128)(2,1)S(1)}, u32[]{:S(2)}, u32[]{:S(2)}) %collective-permute-start.10) | collective-permute-done | bytes 294944 | tf_op jit(solution)/shard_map/ppermute | solution.py:633
  78.8 1.7 %fold_slots.1 = s16[8,288,128]{2,1,0:T(8,128)(2,1)S(1)} custom-call(s32[65]{0:T(128)S(1)} %copy-done.10, s16[4,288,128]{2,1,0:T(8,128)(2,1)S(1)} %get-tuple-element.130.refs_0_, s16[4,288,128]{2,1,0:T(8,128)(2,1)S(1)} %collective-permute-done.8.refs_1_, s16[4,288,128]{2,1,0:T(8,128)(2,1)S(1)} %collective-permute-done.9.refs_2_, ...), custom_call_target="tpu_custom_call" | custom-call | flops 1 | bytes 1 | tf_op jit(solution)/shard_map/fold_slots/pallas_call | solution.py:385
  80.5 2.7 %view_terms.1 = f32[76,7]{1,0:T(8,128)} custom-call(s32[2,12]{1,0:T(2,128)} %bitcast.41, f32[24,7]{1,0:T(8,128)} %get-tuple-element.111.cam_ref, f32[24,7]{1,0:T(8,128)} %get-tuple-element.112.pose_ref, f32[24,16,128]{2,1,0:T(8,128)} %copy-done.5, f32[24,16,128]{2,1,0:T(8,128)} %copy-done.6), custom_call_target="tpu_custom_call" | custom-call | flops 1 | bytes 1 | tf_op jit(solution)/shard_map/view_terms/pallas_call | solution.py:575
  83.3 1.4 %collective-permute-start.13 = (s16[4,288,128]{2,1,0:T(8,128)(2,1)}, s16[4,288,128]{2,1,0:T(8,128)(2,1)S(1)}, u32[]{:S(2)}, u32[]{:S(2)}) collective-permute-start(s16[4,288,128]{2,1,0:T(8,128)(2,1)} %get-tuple-element.138), channel_id=1, source_target_pairs={{0,4},{4,0},{8,12},{12,8},{16,20},{20,16},{24,28},{28,24},{1,5},{5... | collective-permute-start | bytes 884744 | tf_op jit(solution)/shard_map/ppermute | solution.py:633
  84.6 1.7 %collective-permute-start.14 = (s16[4,288,128]{2,1,0:T(8,128)(2,1)}, s16[4,288,128]{2,1,0:T(8,128)(2,1)S(1)}, u32[]{:S(2)}, u32[]{:S(2)}) collective-permute-start(s16[4,288,128]{2,1,0:T(8,128)(2,1)} %get-tuple-element.139), channel_id=1, source_target_pairs={{0,8},{4,12},{8,0},{12,4},{16,24},{20,28},{24,16},{28,20},{1,9},{5... | collective-permute-start | bytes 884744 | tf_op jit(solution)/shard_map/ppermute | solution.py:633
  88.8 1.5 %collective-permute-start.12 = (f32[76,7]{0,1:T(8,128)S(1)}, f32[76,7]{0,1:T(8,128)S(1)}, u32[]{:S(2)}, u32[]{:S(2)}) collective-permute-start(f32[76,7]{0,1:T(8,128)S(1)} %add.11), channel_id=1, source_target_pairs={{0,2},{1,3},{2,0},{3,1},{4,6},{5,7},{6,4},{7,5},{8,10},{9,11},{10,... | collective-permute-start | bytes 6392 | tf_op jit(solution)/shard_map/ppermute | solution.py:686
  90.3 2.1 %collective-permute-done.12 = f32[76,7]{0,1:T(8,128)S(1)} collective-permute-done((f32[76,7]{0,1:T(8,128)S(1)}, f32[76,7]{0,1:T(8,128)S(1)}, u32[]{:S(2)}, u32[]{:S(2)}) %collective-permute-start.12) | collective-permute-done | bytes 2160 | tf_op jit(solution)/shard_map/ppermute | solution.py:686
  93.1 4.2 %all-to-all-start.1 = ((f32[8,8,7]{2,1,0:T(8,128)}), f32[8,8,7]{2,1,0:T(8,128)}, u32[]{:S(2)}, u32[]{:S(2)}) async-start(f32[8,8,7]{2,1,0:T(8,128)} %bitcast.35), calls=%async_computation.1 | async-start | bytes 65536 | tf_op jit(solution)/shard_map/all_to_all | solution.py:690
  97.9 6.6 %collective-permute-done.14.refs_2_ = s16[4,288,128]{2,1,0:T(8,128)(2,1)S(1)} collective-permute-done((s16[4,288,128]{2,1,0:T(8,128)(2,1)}, s16[4,288,128]{2,1,0:T(8,128)(2,1)S(1)}, u32[]{:S(2)}, u32[]{:S(2)}) %collective-permute-start.14) | collective-permute-done | bytes 294944 | tf_op jit(solution)/shard_map/ppermute | solution.py:633
  104.5 2.6 %collective-permute-done.15.refs_3_ = s16[4,288,128]{2,1,0:T(8,128)(2,1)S(1)} collective-permute-done((s16[4,288,128]{2,1,0:T(8,128)(2,1)}, s16[4,288,128]{2,1,0:T(8,128)(2,1)S(1)}, u32[]{:S(2)}, u32[]{:S(2)}) %collective-permute-start.15) | collective-permute-done | bytes 294944 | tf_op jit(solution)/shard_map/ppermute | solution.py:633
  108.3 3.5 %update_depths.1 = (f32[8,36864]{1,0:T(8,128)}, f32[8,36864]{1,0:T(8,128)}, f32[8,36864]{1,0:T(8,128)}) custom-call(f32[8,288,128]{2,1,0:T(8,128)S(1)} %fold_local.1.local_ref, s16[8,288,128]{2,1,0:T(8,128)(2,1)S(1)} %collective-permute-done.16.far_ref, f32[8,36864]{1,0:T(8,128)S(1)} %copy-done.1, f32[8,36864]{1,0:T(8,128)S(1)} %copy-done.3, ...), custom_call_target="tpu_custom_call" | custom-call | flops 1 | bytes 1 | tf_op jit(solution)/shard_map/update_depths/pallas_call | solution.py:445
  111.8 1.4 %update_small.1 = (f32[8,7]{1,0:T(8,128)}, f32[8,7]{1,0:T(8,128)}, f32[8,7]{1,0:T(8,128)}, f32[7,12]{1,0:T(8,128)}, f32[7,12]{1,0:T(8,128)}, /*index=5*/f32[7,12]{1,0:T(8,128)}) custom-call(f32[8,8,7]{2,1,0:T(8,128)} %all-to-all-done.1.mail_ref, f32[7,12]{1,0:T(8,128)} %slice_bitcast_fusion.pose_ref, f32[8,7]{1,0:T(8,128)} %refs_0_.1, f32[8,7]{1,0:T(8,128)} %refs_1_.1, ...), custom_call_target="tpu_custom_call" | custom-call | flops 1 | bytes 1 | tf_op jit(solution)/shard_map/update_small/pallas_call | solution.py:597
  (59 shorter events, 12.6 us)
Async XLA Ops:
  2.2 33.9 %copy-start.13 = (f32[12,7]{0,1:T(8,128)S(1)}, f32[12,7]{0,1:T(8,128)}, u32[]{:S(2)}) copy-start(f32[12,7]{0,1:T(8,128)} %param.19) | copy-start | bytes 1012
  2.3 38.4 %copy-start.2 = (bf16[12,2,36864]{2,1,0:T(2,128)(2,1)S(1)}, bf16[12,2,36864]{2,1,0:T(2,128)(2,1)}, u32[]{:S(2)}) copy-start(bf16[12,2,36864]{2,1,0:T(2,128)(2,1)} %param.23) | copy-start | bytes 5308420
  4.5 24.8 %all-to-all-start = ((f32[8,9,128]{2,1,0:T(8,128)}), f32[8,9,128]{2,1,0:T(8,128)S(1)}, u32[]{:S(2)}, u32[]{:S(2)}) async-start(f32[8,9,128]{2,1,0:T(8,128)} %letters_of.1), calls=%async_computation | async-start | bytes 131072 | tf_op jit(solution)/shard_map/all_to_all | solution.py:649
  11.7 36.9 %collective-permute-start = (s16[8,144,128]{2,1,0:T(8,128)(2,1)}, s16[8,144,128]{2,1,0:T(8,128)(2,1)S(1)}, u32[]{:S(2)}, u32[]{:S(2)}) collective-permute-start(s16[8,144,128]{2,1,0:T(8,128)(2,1)} %get-tuple-element.155), channel_id=1, source_target_pairs={{0,16},{4,20},{8,24},{12,28},{16,0},{20,4},{24,8},{28,12},{1,17},{... | collective-permute-start | bytes 884744 | tf_op jit(solution)/shard_map/ppermute | solution.py:633
  14.7 34.0 %collective-permute-start.1 = (s16[8,144,128]{2,1,0:T(8,128)(2,1)}, s16[8,144,128]{2,1,0:T(8,128)(2,1)}, u32[]{:S(2)}, u32[]{:S(2)}) collective-permute-start(s16[8,144,128]{2,1,0:T(8,128)(2,1)} %get-tuple-element.83), channel_id=1, source_target_pairs={{0,16},{4,20},{8,24},{12,28},{16,0},{20,4},{24,8},{28,12},{1,17},{... | collective-permute-start | bytes 884744 | tf_op jit(solution)/shard_map/ppermute | solution.py:633
  32.4 0.7 copy-start.9
  34.6 16.7 %collective-permute-start.5 = (s16[4,288,128]{2,1,0:T(8,128)(2,1)}, s16[4,288,128]{2,1,0:T(8,128)(2,1)S(1)}, u32[]{:S(2)}, u32[]{:S(2)}) collective-permute-start(s16[4,288,128]{2,1,0:T(8,128)(2,1)} %get-tuple-element.99), channel_id=1, source_target_pairs={{0,4},{4,0},{8,12},{12,8},{16,20},{20,16},{24,28},{28,24},{1,5},{5... | collective-permute-start | bytes 884744 | tf_op jit(solution)/shard_map/ppermute | solution.py:633
  36.7 16.6 %collective-permute-start.6 = (s16[4,288,128]{2,1,0:T(8,128)(2,1)}, s16[4,288,128]{2,1,0:T(8,128)(2,1)S(1)}, u32[]{:S(2)}, u32[]{:S(2)}) collective-permute-start(s16[4,288,128]{2,1,0:T(8,128)(2,1)} %get-tuple-element.100), channel_id=1, source_target_pairs={{0,8},{4,12},{8,0},{12,4},{16,24},{20,28},{24,16},{28,20},{1,9},{5... | collective-permute-start | bytes 884744 | tf_op jit(solution)/shard_map/ppermute | solution.py:633
  36.8 18.7 %collective-permute-start.7 = (s16[4,288,128]{2,1,0:T(8,128)(2,1)S(1)}, s16[4,288,128]{2,1,0:T(8,128)(2,1)S(1)}, u32[]{:S(2)}, u32[]{:S(2)}) collective-permute-start(s16[4,288,128]{2,1,0:T(8,128)(2,1)S(1)} %get-tuple-element.101), channel_id=1, source_target_pairs={{0,12},{4,8},{8,4},{12,0},{16,28},{20,24},{24,20},{28,16},{1,13},{... | collective-permute-start | bytes 884744 | tf_op jit(solution)/shard_map/ppermute | solution.py:633
  40.7 2.5 %copy-start = (bf16[12,2,3,36864]{3,1,2,0:T(2,128)(2,1)S(1)}, bf16[12,2,3,36864]{3,1,2,0:T(2,128)(2,1)}, u32[]{:S(2)}) copy-start(bf16[12,2,3,36864]{3,1,2,0:T(2,128)(2,1)} %param.22) | copy-start | bytes 15925252
  43.2 0.7 copy-start.7
  43.9 4.7 %copy-start.10 = (s32[65]{0:T(128)S(1)}, s32[65]{0:T(128)}, u32[]{:S(2)}) copy-start(s32[65]{0:T(128)} %slot_tables.1.tab_ref) | copy-start | bytes 784
  43.9 11.6 %copy-start.8 = (f32[24,16]{1,0:T(8,128)S(1)}, f32[24,16]{1,0:T(8,128)}, u32[]{:S(2)}) copy-start(f32[24,16]{1,0:T(8,128)} %get-tuple-element.89.coef_ref) | copy-start | bytes 4612
  49.8 12.9 %collective-permute-start.2 = (s16[4,288,128]{2,1,0:T(8,128)(2,1)S(1)}, s16[4,288,128]{2,1,0:T(8,128)(2,1)S(1)}, u32[]{:S(2)}, u32[]{:S(2)}) collective-permute-start(s16[4,288,128]{2,1,0:T(8,128)(2,1)S(1)} %get-tuple-element.94), channel_id=1, source_target_pairs={{0,4},{4,0},{8,12},{12,8},{16,20},{20,16},{24,28},{28,24},{1,5},{5... | collective-permute-start | bytes 884744 | tf_op jit(solution)/shard_map/ppermute | solution.py:633
  51.3 11.4 %collective-permute-start.3 = (s16[4,288,128]{2,1,0:T(8,128)(2,1)S(1)}, s16[4,288,128]{2,1,0:T(8,128)(2,1)S(1)}, u32[]{:S(2)}, u32[]{:S(2)}) collective-permute-start(s16[4,288,128]{2,1,0:T(8,128)(2,1)S(1)} %get-tuple-element.95), channel_id=1, source_target_pairs={{0,8},{4,12},{8,0},{12,4},{16,24},{20,28},{24,16},{28,20},{1,9},{5... | collective-permute-start | bytes 884744 | tf_op jit(solution)/shard_map/ppermute | solution.py:633
  51.3 13.0 %collective-permute-start.4 = (s16[4,288,128]{2,1,0:T(8,128)(2,1)S(1)}, s16[4,288,128]{2,1,0:T(8,128)(2,1)S(1)}, u32[]{:S(2)}, u32[]{:S(2)}) collective-permute-start(s16[4,288,128]{2,1,0:T(8,128)(2,1)S(1)} %get-tuple-element.96), channel_id=1, source_target_pairs={{0,12},{4,8},{8,4},{12,0},{16,28},{20,24},{24,20},{28,16},{1,13},{... | collective-permute-start | bytes 884744 | tf_op jit(solution)/shard_map/ppermute | solution.py:633
  60.4 2.2 %copy-start.5 = (f32[24,16,128]{2,1,0:T(8,128)}, f32[24,16,128]{2,1,0:T(8,128)S(1)}, u32[]{:S(2)}) copy-start(f32[24,16,128]{2,1,0:T(8,128)S(1)} %view_sums.2.refs_0_) | copy-start | bytes 589828
  62.7 3.1 %copy-start.11 = (s16[4,288,128]{2,1,0:T(8,128)(2,1)}, s16[4,288,128]{2,1,0:T(8,128)(2,1)S(1)}, u32[]{:S(2)}) copy-start(s16[4,288,128]{2,1,0:T(8,128)(2,1)S(1)} %get-tuple-element.140) | copy-start | bytes 884740
  65.7 9.4 %collective-permute-start.8 = (s16[4,288,128]{2,1,0:T(8,128)(2,1)S(1)}, s16[4,288,128]{2,1,0:T(8,128)(2,1)S(1)}, u32[]{:S(2)}, u32[]{:S(2)}) collective-permute-start(s16[4,288,128]{2,1,0:T(8,128)(2,1)S(1)} %get-tuple-element.123), channel_id=1, source_target_pairs={{0,4},{4,0},{8,12},{12,8},{16,20},{20,16},{24,28},{28,24},{1,5},{5... | collective-permute-start | bytes 884744 | tf_op jit(solution)/shard_map/ppermute | solution.py:633
  66.2 8.9 %collective-permute-start.9 = (s16[4,288,128]{2,1,0:T(8,128)(2,1)S(1)}, s16[4,288,128]{2,1,0:T(8,128)(2,1)S(1)}, u32[]{:S(2)}, u32[]{:S(2)}) collective-permute-start(s16[4,288,128]{2,1,0:T(8,128)(2,1)S(1)} %get-tuple-element.124), channel_id=1, source_target_pairs={{0,8},{4,12},{8,0},{12,4},{16,24},{20,28},{24,16},{28,20},{1,9},{5... | collective-permute-start | bytes 884744 | tf_op jit(solution)/shard_map/ppermute | solution.py:633
  66.2 12.6 %collective-permute-start.10 = (s16[4,288,128]{2,1,0:T(8,128)(2,1)S(1)}, s16[4,288,128]{2,1,0:T(8,128)(2,1)S(1)}, u32[]{:S(2)}, u32[]{:S(2)}) collective-permute-start(s16[4,288,128]{2,1,0:T(8,128)(2,1)S(1)} %get-tuple-element.125), channel_id=1, source_target_pairs={{0,12},{4,8},{8,4},{12,0},{16,28},{20,24},{24,20},{28,16},{1,13},{... | collective-permute-start | bytes 884744 | tf_op jit(solution)/shard_map/ppermute | solution.py:633
  74.2 0.7 copy-start.6
  78.8 29.5 %copy-start.4 = (f32[8,36864]{1,0:T(8,128)S(1)}, f32[8,36864]{1,0:T(8,128)}, u32[]{:S(2)}) copy-start(f32[8,36864]{1,0:T(8,128)} %s_ref.1) | copy-start | bytes 3538948
  80.5 27.8 %collective-permute-start.16 = (s16[8,288,128]{2,1,0:T(8,128)(2,1)S(1)}, s16[8,288,128]{2,1,0:T(8,128)(2,1)S(1)}, u32[]{:S(2)}, u32[]{:S(2)}) collective-permute-start(s16[8,288,128]{2,1,0:T(8,128)(2,1)S(1)} %fold_slots.1), channel_id=1, source_target_pairs={{0,16},{4,20},{8,24},{12,28},{16,0},{20,4},{24,8},{28,12},{1,17},{... | collective-permute-start | bytes 1769480 | tf_op jit(solution)/shard_map/ppermute | solution.py:633
  83.3 14.7 %collective-permute-start.13 = (s16[4,288,128]{2,1,0:T(8,128)(2,1)}, s16[4,288,128]{2,1,0:T(8,128)(2,1)S(1)}, u32[]{:S(2)}, u32[]{:S(2)}) collective-permute-start(s16[4,288,128]{2,1,0:T(8,128)(2,1)} %get-tuple-element.138), channel_id=1, source_target_pairs={{0,4},{4,0},{8,12},{12,8},{16,20},{20,16},{24,28},{28,24},{1,5},{5... | collective-permute-start | bytes 884744 | tf_op jit(solution)/shard_map/ppermute | solution.py:633
  84.6 19.9 %collective-permute-start.14 = (s16[4,288,128]{2,1,0:T(8,128)(2,1)}, s16[4,288,128]{2,1,0:T(8,128)(2,1)S(1)}, u32[]{:S(2)}, u32[]{:S(2)}) collective-permute-start(s16[4,288,128]{2,1,0:T(8,128)(2,1)} %get-tuple-element.139), channel_id=1, source_target_pairs={{0,8},{4,12},{8,0},{12,4},{16,24},{20,28},{24,16},{28,20},{1,9},{5... | collective-permute-start | bytes 884744 | tf_op jit(solution)/shard_map/ppermute | solution.py:633
  86.3 20.9 %collective-permute-start.15 = (s16[4,288,128]{2,1,0:T(8,128)(2,1)}, s16[4,288,128]{2,1,0:T(8,128)(2,1)S(1)}, u32[]{:S(2)}, u32[]{:S(2)}) collective-permute-start(s16[4,288,128]{2,1,0:T(8,128)(2,1)} %copy-done.11), channel_id=1, source_target_pairs={{0,12},{4,8},{8,4},{12,0},{16,28},{20,24},{24,20},{28,16},{1,13},{... | collective-permute-start | bytes 884744 | tf_op jit(solution)/shard_map/ppermute | solution.py:633
  87.6 1.2 %collective-permute-start.11 = (f32[76,7]{0,1:T(8,128)S(1)}, f32[76,7]{0,1:T(8,128)S(1)}, u32[]{:S(2)}, u32[]{:S(2)}) collective-permute-start(f32[76,7]{0,1:T(8,128)S(1)} %copy.25), channel_id=1, source_target_pairs={{0,1},{1,0},{2,3},{3,2},{4,5},{5,4},{6,7},{7,6},{8,9},{9,8},{10,11... | collective-permute-start | bytes 6392 | tf_op jit(solution)/shard_map/ppermute | solution.py:686
  88.8 3.6 %collective-permute-start.12 = (f32[76,7]{0,1:T(8,128)S(1)}, f32[76,7]{0,1:T(8,128)S(1)}, u32[]{:S(2)}, u32[]{:S(2)}) collective-permute-start(f32[76,7]{0,1:T(8,128)S(1)} %add.11), channel_id=1, source_target_pairs={{0,2},{1,3},{2,0},{3,1},{4,6},{5,7},{6,4},{7,5},{8,10},{9,11},{10,... | collective-permute-start | bytes 6392 | tf_op jit(solution)/shard_map/ppermute | solution.py:686
  93.1 18.7 %all-to-all-start.1 = ((f32[8,8,7]{2,1,0:T(8,128)}), f32[8,8,7]{2,1,0:T(8,128)}, u32[]{:S(2)}, u32[]{:S(2)}) async-start(f32[8,8,7]{2,1,0:T(8,128)} %bitcast.35), calls=%async_computation.1 | async-start | bytes 65536 | tf_op jit(solution)/shard_map/all_to_all | solution.py:690
  97.9 10.3 %copy-start.1 = (f32[8,36864]{1,0:T(8,128)S(1)}, f32[8,36864]{1,0:T(8,128)}, u32[]{:S(2)}) copy-start(f32[8,36864]{1,0:T(8,128)} %x_ref.1) | copy-start | bytes 3538948
  97.9 10.3 %copy-start.3 = (f32[8,36864]{1,0:T(8,128)S(1)}, f32[8,36864]{1,0:T(8,128)}, u32[]{:S(2)}) copy-start(f32[8,36864]{1,0:T(8,128)} %m_ref.1) | copy-start | bytes 3538948
  (1 other events, 0.6 us)

commit v5 on v4

--- a/solution.py
+++ b/solution.py
@@ -97,16 +97,14 @@
     list_ref, tab_ref, count_ref = refs
     me = me_ref[0]
     shards = 2 * half
-    asked = shards * cap
+    spare = 2 * shards
     requests = list_ref.shape[1]
 
-    @pl.loop(0, 2 * asked, unroll=8)
+    @pl.loop(0, (spare + 1) * cap, unroll=8)
     def _(i):
         tab_ref[i] = -1
 
-    tab_ref[2 * asked] = me & (half - 1)
-
-    @pl.loop(0, 2 * shards, unroll=8)
+    @pl.loop(0, spare + 1, unroll=8)
     def _(i):
         count_ref[i] = 0
 
@@ -115,33 +113,23 @@
         tab_ref[cell * cap + jnp.minimum(rank, cap - 1)] = value
         count_ref[cell] = rank + 1
 
-    for k in range(half):
-        asker = me ^ k
-
-        @pl.loop(0, requests, unroll=2)
-        def _(r):
-            image = list_ref[asker, r]
+    @pl.loop(0, requests)
+    def _(r):
+        for k in range(half):
+            image = list_ref[me ^ k, r]
             owner = over(image, images)
-            mine = owner == me
-
-            @pl.when(mine | (owner == (me ^ half)))
-            def _():
-                put(jnp.where(mine, k, half + k), image - owner * images)
-
-    @pl.loop(0, requests, unroll=2)
-    def _(r):
-        image = list_ref[me, r]
-        owner = over(image, images)
-        put(shards + (owner ^ me), r)
+            cell = jnp.where(owner == me, k, jnp.where(owner == (me ^ half), half + k, spare))
+            put(cell, image - owner * images)
+        put(shards + (over(list_ref[me, r], images) ^ me), r)
 
 
 def slot_tables(me, lists, half, cap, images):
     return pl.pallas_call(
         functools.partial(table_kernel, half, cap, images),
-        out_shape=jax.ShapeDtypeStruct((4 * half * cap + 1,), jnp.int32),
+        out_shape=jax.ShapeDtypeStruct(((4 * half + 1) * cap,), jnp.int32),
         in_specs=[SMEM, SMEM],
         out_specs=SMEM,
-        scratch_shapes=[pltpu.SMEM((4 * half,), jnp.int32)],
+        scratch_shapes=[pltpu.SMEM((4 * half + 1,), jnp.int32)],
         cost_estimate=COST,
         name="slot_tables",
     )(me, lists)
@@ -252,12 +240,10 @@
     return refs[k] if len(refs) > 1 else refs[0].at[k ^ tab_ref[tab_ref.shape[0] - 1]]
 
 
-def grad_kernel(first, half, cap, tab_ref, slope_ref, *refs):
-    depth_refs, grad_refs = refs[:half], refs[half:]
-    rows = depth_refs[0].shape[1]
-    for k in range(half):
-        depth_ref = depth_refs[k]
-        grad_ref = slots_at(grad_refs, k, tab_ref)
+def grad_kernel(first, ks, cap, tab_ref, slope_ref, *refs):
+    depth_refs, grad_refs = refs[: len(ks)], refs[len(ks) :]
+    rows = slope_ref.shape[2]
+    for k, depth_ref, grad_ref in zip(ks, depth_refs, grad_refs):
 
         @pl.loop(0, cap)
         def _(c):
@@ -272,17 +258,13 @@
                     grad_ref[c, here] = encode_slot(along)
 
 
-def depth_grads(table, slopes, depths, first, half, cap, by_rank):
-    rows = depths[0].shape[1]
-    if by_rank:
-        out = [jax.ShapeDtypeStruct((half, cap, rows, LANES), INTS)]
-    else:
-        out = [jax.ShapeDtypeStruct((cap, rows, LANES), INTS)] * half
-    return pl.pallas_call(
-        functools.partial(grad_kernel, first, half, cap),
-        out_shape=out,
-        in_specs=[SMEM] + [VMEM] * (1 + half),
-        out_specs=[VMEM] * len(out),
+def depth_grads(table, slopes, depths, first, ks, cap):
+    rows = slopes.shape[2]
+    return pl.pallas_call(
+        functools.partial(grad_kernel, first, ks, cap),
+        out_shape=[jax.ShapeDtypeStruct((cap, rows, LANES), INTS)] * len(ks),
+        in_specs=[SMEM] + [VMEM] * (1 + len(ks)),
+        out_specs=[VMEM] * len(ks),
         compiler_params=PARAMS,
         cost_estimate=COST,
         name="depth_grads",
@@ -352,10 +334,8 @@
     )(table, coefs, row, views, *depths)
 
 
-def fold(first, half, cap, tab_ref, slot_refs, total_ref):
-    total_ref[...] = jnp.zeros_like(total_ref)
-    for k in range(half):
-        slot_ref = slots_at(slot_refs, k, tab_ref)
+def fold(first, ks, cap, tab_ref, slot_refs, total_ref):
+    for k, slot_ref in zip(ks, slot_refs):
 
         @pl.loop(0, cap)
         def _(c):
@@ -366,58 +346,55 @@
                 total_ref[image] += decode_slot(slot_ref[c])
 
 
-def fold_kernel(first, cap, bound, half, tab_ref, *refs):
-    slot_refs, out_refs, total = refs[:half], refs[half:-1], refs[-1]
-    fold(first, half, cap, tab_ref, slot_refs, total)
-    rows = out_refs[0].shape[1]
-    for part, out_ref in enumerate(out_refs):
-
-        @pl.loop(0, total.shape[0])
-        def _(i):
-            value = total[i, part * rows : (part + 1) * rows]
-            out_ref[i] = encode(
-                jnp.abs(value) * (SLOT_UNIT / CODE_UNIT), value < 0.0, bound
-            )
-
-
-def fold_slots(table, slots, first, images, cap, bound, parts):
+def total_kernel(first, ks, cap, tab_ref, *refs):
+    refs[-1][...] = jnp.zeros_like(refs[-1])
+    fold(first, ks, cap, tab_ref, refs[:-1], refs[-1])
+
+
+def fold_totals(table, slots, first, ks, images, cap):
     rows = slots[0].shape[1]
     return pl.pallas_call(
-        functools.partial(fold_kernel, first, cap, bound, len(slots)),
-        out_shape=[jax.ShapeDtypeStruct((images, rows // parts, LANES), INTS)] * parts,
-        in_specs=[SMEM] + [VMEM] * len(slots),
-        out_specs=[VMEM] * parts,
-        scratch_shapes=[pltpu.VMEM((images, rows, LANES), jnp.float32)],
-        compiler_params=PARAMS,
-        cost_estimate=COST,
-        name="fold_slots",
-    )(table, *slots)
-
-
-def local_kernel(first, half, cap, tab_ref, *refs):
-    fold(first, half, cap, tab_ref, refs[:-1], refs[-1])
-
-
-def fold_local(table, slots, first, images, half, cap):
-    rows = slots[0].shape[-2]
-    return pl.pallas_call(
-        functools.partial(local_kernel, first, half, cap),
+        functools.partial(total_kernel, first, ks, cap),
         out_shape=jax.ShapeDtypeStruct((images, rows, LANES), jnp.float32),
         in_specs=[SMEM] + [VMEM] * len(slots),
         out_specs=VMEM,
         compiler_params=PARAMS,
         cost_estimate=COST,
-        name="fold_local",
+        name="fold_totals",
     )(table, *slots)
+
+
+def add_code_kernel(first, ks, cap, bound, tab_ref, total_ref, *refs):
+    slot_refs, out_ref, more = refs[:-2], refs[-2], refs[-1]
+    more[...] = total_ref[...]
+    fold(first, ks, cap, tab_ref, slot_refs, more)
+
+    @pl.loop(0, more.shape[0])
+    def _(i):
+        value = more[i]
+        out_ref[i] = encode(jnp.abs(value) * (SLOT_UNIT / CODE_UNIT), value < 0.0, bound)
+
+
+def fold_codes(table, totals, slots, first, ks, cap, bound):
+    return pl.pallas_call(
+        functools.partial(add_code_kernel, first, ks, cap, bound),
+        out_shape=jax.ShapeDtypeStruct(totals.shape, INTS),
+        in_specs=[SMEM] + [VMEM] * (1 + len(slots)),
+        out_specs=VMEM,
+        scratch_shapes=[pltpu.VMEM(totals.shape, jnp.float32)],
+        compiler_params=PARAMS,
+        cost_estimate=COST,
+        name="fold_codes",
+    )(table, totals, *slots)
 
 
 def adam_step(values, moment, second, gradient, step_rate):
     step_count = START + 1
     moment = beta_one * moment + (1.0 - beta_one) * gradient
     second = beta_two * second + (1.0 - beta_two) * gradient * gradient
-    fix_one = 1.0 - beta_one**step_count
-    fix_two = 1.0 - beta_two**step_count
-    values = values - step_rate * (moment / fix_one) / (jnp.sqrt(second / fix_two) + adam_eps)
+    pace = step_rate / (1.0 - beta_one**step_count)
+    grown = second * (1.0 / (1.0 - beta_two**step_count))
+    values = values - (moment * pace) / (grown * lax.rsqrt(grown) + adam_eps)
     return (values, moment, second)
 
 
@@ -662,19 +639,24 @@
     asked = exchange(pack_slots(table, far, slots, half, cap))
 
     near_sums = view_sums(table, coefs, row, views, near, 2 * slots, half, cap)
-    near_grads = depth_grads(table, slopes, near, 2 * slots, half, cap, False)
-    asked, near_sums, near_grads = tie((asked, near_sums, near_grads))
-    far_grads = depth_grads(table, slopes, asked, 3 * slots, half, cap, False)
-    asked, far_grads = tie((asked, far_grads))
-    back = exchange(far_grads)
+    every, early, late = range(half), range(half - 1), range(half - 1, half)
+    near_grads = depth_grads(table, slopes, near, 2 * slots, every, cap)
+    first_asked, near_sums, near_grads = tie((asked[:-1], near_sums, near_grads))
+    far_grads = depth_grads(table, slopes, first_asked, 3 * slots, early, cap)
+    last_asked, _ = tie((asked[-1:], far_grads))
+    last_grads = depth_grads(table, slopes, last_asked, 3 * slots, late, cap)
+    back = exchange([*far_grads, *last_grads])
+    asked, _ = tie((asked, last_grads))
     far_sums = view_sums(table, coefs, row, views, asked, 3 * slots, half, cap)
-    back, far_sums = tie((back, far_sums))
-    folded = fold_slots(table, back, slots, images, cap, far_bound, 1)
+    first_back, far_sums = tie((back[:-1], far_sums))
+    totals = fold_totals(table, first_back, slots, early, images, cap)
+    last_back, totals = tie((back[-1:], totals))
+    folded = [fold_codes(table, totals, last_back, slots, late, cap, far_bound)]
     folded, far_sums = tie((folded, far_sums))
     far_codes = [swap(part, half) for part in folded]
     small = view_terms(names, cams, poses, [near_sums, far_sums], shards * images)
     near_grads, small = tie((near_grads, small))
-    near_total = fold_local(table, exchange(near_grads), 0, images, half, cap)
+    near_total = fold_totals(table, exchange(near_grads), 0, every, images, cap)
     done = []
     for c in range(1):
         done = update_depths(

time: 114 us -> 111 us (0.974)
  starting transfers between devices: 30.1 us -> 27.4 us
    ppermute x15, starting transfers between devices: 17.1 us -> 14.4 us  [swap(): return lax.ppermute(value, 'img', [(i, i ^ k) for i in range(shards)])]
    pallas_call x4 -> x6, Pallas kernels: 6.39 us -> 7.7 us  [the longest x3 4.18 us: depth_grads(): pl.pallas_call(functools.partial(grad_kernel, first, ks, cap), out_shape=...]
  transfers between devices with their start and end apart: 19 -> 19, of which waited for: 9 -> 8; matrix products, arithmetic and copies ran while one was open for 3% -> 3% of each run, Pallas kernels for 28% -> 31%
where the time goes in v5:
time: 111 us
  Pallas kernels  38.1 us (34%)
  waiting for transfers between devices  33.9 us (31%)
  starting transfers between devices  27.4 us (25%)
  local copies, waits for them, and re-layouts  8.39 us (8%)
  other arithmetic  2.14 us (2%)
    ppermute x15, waiting for transfers between devices, swap(): return lax.ppermute(value, 'img', [(i, i ^ k) for i in range(shards)])  16.1 us
    all_to_all x1, waiting for transfers between devices, body(): mail = lax.all_to_all(letters, 'img', 0, 0, tiled=True)  14.6 us
    ppermute x15, starting transfers between devices, swap(): return lax.ppermute(value, 'img', [(i, i ^ k) for i in range(shards)])  14.4 us
    pallas_call x2, Pallas kernels, view_sums(): pl.pallas_call(functools.partial(sum_kernel, first, half, cap), out_shape...  9.89 us
    all_to_all x1, starting transfers between devices, body(): mail = lax.all_to_all(letters, 'img', 0, 0, tiled=True)  7.25 us
    unnamed x30, local copies, waits for them, and re-layouts  5.33 us
    pallas_call x1, Pallas kernels, prepare_views(): pl.pallas_call(prepare_kernel, out_shape=[jax.ShapeDtypeStruct((2 * pairs...  4.67 us
    all_to_all x1, starting transfers between devices, body(): lax.all_to_all(small[:shards * images].reshape(shards, images, 7), 'img',...  4.2 us
  transfers between devices with their start and end apart: 19, of which 8 were waited for; matrix products, arithmetic and copies ran while one was open for 3% of the time, Pallas kernels for 31%

profile of v5, /device:TPU:0, one launch (start us, length us, event | category | flops | bytes accessed | tf_op | source)
XLA Modules:
  0.0 110.8 jit_solution(9268535216936926659)
XLA Ops:
  0.6 1.5 %fusion = s16[1,8,288,128]{3,1,2,0:T(8,128)(2,1)S(1)} fusion(f32[8,36864]{1,0:T(8,128)} %x_ref.1), kind=kLoop, calls=%fused_computation.1 | loop fusion | flops 1179648 | bytes 1769472
  3.1 1.3 %letters_of.1 = f32[8,9,128]{2,1,0:T(8,128)} custom-call(s32[2,12]{1,0:T(2,128)} %bitcast.39, f32[8,7]{1,0:T(8,128)} %refs_0_.1), custom_call_target="tpu_custom_call" | custom-call | flops 1 | bytes 1 | tf_op jit(solution)/shard_map/letters_of/pallas_call | solution.py:80
  4.5 7.3 %all-to-all-start = ((f32[8,9,128]{2,1,0:T(8,128)}), f32[8,9,128]{2,1,0:T(8,128)S(1)}, u32[]{:S(2)}, u32[]{:S(2)}) async-start(f32[8,9,128]{2,1,0:T(8,128)} %letters_of.1), calls=%async_computation | async-start | bytes 131072 | tf_op jit(solution)/shard_map/all_to_all | solution.py:626
  11.7 2.9 %collective-permute-start.1 = (s16[8,144,128]{2,1,0:T(8,128)(2,1)}, s16[8,144,128]{2,1,0:T(8,128)(2,1)S(1)}, u32[]{:S(2)}, u32[]{:S(2)}) collective-permute-start(s16[8,144,128]{2,1,0:T(8,128)(2,1)} %get-tuple-element.79), channel_id=1, source_target_pairs={{0,16},{4,20},{8,24},{12,28},{16,0},{20,4},{24,8},{28,12},{1,17},{... | collective-permute-start | bytes 884744 | tf_op jit(solution)/shard_map/ppermute | solution.py:610
  14.7 14.6 %all-to-all-done.all_ref = f32[8,9,128]{2,1,0:T(8,128)S(1)} async-done(((f32[8,9,128]{2,1,0:T(8,128)}), f32[8,9,128]{2,1,0:T(8,128)S(1)}, u32[]{:S(2)}, u32[]{:S(2)}) %all-to-all-start) | async-done | bytes 36896 | tf_op jit(solution)/shard_map/all_to_all | solution.py:626
  29.9 2.3 %slot_tables.1.tab_ref = s32[68]{0:T(128)} custom-call(s32[1]{0:T(128)} %bitcast.me_ref, s32[8,24]{1,0:T(8,128)} %bitcast.37), custom_call_target="tpu_custom_call" | custom-call | flops 1 | bytes 1 | tf_op jit(solution)/shard_map/slot_tables/pallas_call | solution.py:127
  32.8 1.5 %pack_slots.2 = (s16[4,288,128]{2,1,0:T(8,128)(2,1)S(1)}, s16[4,288,128]{2,1,0:T(8,128)(2,1)}, s16[4,288,128]{2,1,0:T(8,128)(2,1)}, s16[4,288,128]{2,1,0:T(8,128)(2,1)S(1)}) custom-call(s32[68]{0:T(128)S(1)} %copy-done.9, s16[8,288,128]{2,1,0:T(8,128)(2,1)S(1)} %bitcast.33), custom_call_target="tpu_custom_call" | custom-call | flops 1 | bytes 1 | tf_op jit(solution)/shard_map/pack_slots/pallas_call | solution.py:154
  34.4 1.4 %collective-permute-start.4 = (s16[4,288,128]{2,1,0:T(8,128)(2,1)}, s16[4,288,128]{2,1,0:T(8,128)(2,1)S(1)}, u32[]{:S(2)}, u32[]{:S(2)}) collective-permute-start(s16[4,288,128]{2,1,0:T(8,128)(2,1)} %get-tuple-element.94), channel_id=1, source_target_pairs={{0,4},{4,0},{8,12},{12,8},{16,20},{20,16},{24,28},{28,24},{1,5},{5... | collective-permute-start | bytes 884744 | tf_op jit(solution)/shard_map/ppermute | solution.py:610
  36.5 2.0 %collective-permute-start.6 = (s16[4,288,128]{2,1,0:T(8,128)(2,1)S(1)}, s16[4,288,128]{2,1,0:T(8,128)(2,1)S(1)}, u32[]{:S(2)}, u32[]{:S(2)}) collective-permute-start(s16[4,288,128]{2,1,0:T(8,128)(2,1)S(1)} %get-tuple-element.96), channel_id=1, source_target_pairs={{0,12},{4,8},{8,4},{12,0},{16,28},{20,24},{24,20},{28,16},{1,13},{... | collective-permute-start | bytes 884744 | tf_op jit(solution)/shard_map/ppermute | solution.py:610
  38.5 1.9 %view_coefs.1 = (f32[24,16]{1,0:T(8,128)}, f32[24,7]{1,0:T(8,128)}, f32[24,7]{1,0:T(8,128)}) custom-call(s32[2,12]{1,0:T(2,128)} %bitcast.40, f32[8,9,128]{2,1,0:T(8,128)} %copy-done.12, f32[12,7]{1,0:T(8,128)} %copy.21.pair_ref), custom_call_target="tpu_custom_call" | custom-call | flops 1 | bytes 1 | tf_op jit(solution)/shard_map/view_coefs/pallas_call | solution.py:504
  40.4 2.5 %copy-done = bf16[12,2,3,36864]{3,1,2,0:T(2,128)(2,1)S(1)} copy-done((bf16[12,2,3,36864]{3,1,2,0:T(2,128)(2,1)S(1)}, bf16[12,2,3,36864]{3,1,2,0:T(2,128)(2,1)}, u32[]{:S(2)}) %copy-start) | copy-done | bytes 5308440
  43.7 4.7 %prepare_views.1 = (bf16[24,4,288,128]{3,2,1,0:T(8,128)(2,1)S(1)}, f32[24,2,288,128]{3,2,1,0:T(8,128)S(1)}) custom-call(f32[1]{0:T(128)} %bitcast.3.row_ref, f32[24,16]{1,0:T(8,128)S(1)} %copy-done.7, bf16[12,3,576,128]{3,2,1,0:T(8,128)(2,1)S(1)} %bitcast.31, bf16[12,576,128]{2,1,0:T(8,128)(2,1)S(1)} %bitcast.34), custom_call_target="tpu_custom_call" | custom-call | flops 1 | bytes 1 | tf_op jit(solution)/shard_map/prepare_views/pallas_call | solution.py:224
  49.6 1.5 %collective-permute-start.2 = (s16[4,288,128]{2,1,0:T(8,128)(2,1)S(1)}, s16[4,288,128]{2,1,0:T(8,128)(2,1)S(1)}, u32[]{:S(2)}, u32[]{:S(2)}) collective-permute-start(s16[4,288,128]{2,1,0:T(8,128)(2,1)S(1)} %get-tuple-element.90), channel_id=1, source_target_pairs={{0,4},{4,0},{8,12},{12,8},{16,20},{20,16},{24,28},{28,24},{1,5},{5... | collective-permute-start | bytes 884744 | tf_op jit(solution)/shard_map/ppermute | solution.py:610
  51.1 2.0 %collective-permute-start.7 = (s16[4,288,128]{2,1,0:T(8,128)(2,1)S(1)}, s16[4,288,128]{2,1,0:T(8,128)(2,1)S(1)}, u32[]{:S(2)}, u32[]{:S(2)}) collective-permute-start(s16[4,288,128]{2,1,0:T(8,128)(2,1)S(1)} %get-tuple-element.109), channel_id=1, source_target_pairs={{0,12},{4,8},{8,4},{12,0},{16,28},{20,24},{24,20},{28,16},{1,13},{... | collective-permute-start | bytes 884744 | tf_op jit(solution)/shard_map/ppermute | solution.py:610
  53.1 2.4 %collective-permute-done.6.refs_3_ = s16[4,288,128]{2,1,0:T(8,128)(2,1)S(1)} collective-permute-done((s16[4,288,128]{2,1,0:T(8,128)(2,1)S(1)}, s16[4,288,128]{2,1,0:T(8,128)(2,1)S(1)}, u32[]{:S(2)}, u32[]{:S(2)}) %collective-permute-start.6) | collective-permute-done | bytes 294944 | tf_op jit(solution)/shard_map/ppermute | solution.py:610
  55.5 5.3 %view_sums.2.refs_0_ = f32[24,16,128]{2,1,0:T(8,128)S(1)} custom-call(s32[68]{0:T(128)S(1)} %copy-done.10, f32[24,16]{1,0:T(8,128)S(1)} %copy-done.8, f32[1]{0:T(128)} %bitcast.3.row_ref, bf16[24,4,288,128]{3,2,1,0:T(8,128)(2,1)S(1)} %get-tuple-element.92.view_ref, s16[4,288,128]{2,1,0:T(8,128)(2,1)S(1)} %get-tuple-element.93.refs_0_, ...), custom_call_target="tpu_custom_call" | custom-call | flops 1 | bytes 1 | tf_op jit(solution)/shard_map/view_sums/pallas_call | solution.py:325
  60.8 2.3 %depth_grads.3 = (s16[4,288,128]{2,1,0:T(8,128)(2,1)S(1)}, s16[4,288,128]{2,1,0:T(8,128)(2,1)}, s16[4,288,128]{2,1,0:T(8,128)(2,1)}, s16[4,288,128]{2,1,0:T(8,128)(2,1)S(1)}) custom-call(s32[68]{0:T(128)S(1)} %copy-done.10, f32[24,2,288,128]{3,2,1,0:T(8,128)S(1)} %get-tuple-element.97.slope_ref, s16[4,288,128]{2,1,0:T(8,128)(2,1)S(1)} %get-tuple-element.93.refs_0_, ...), custom_call_target="tpu_custom_call" | custom-call | flops 1 | bytes 1 | tf_op jit(solution)/shard_map/depth_grads/pallas_call | solution.py:263
  63.1 1.2 %depth_grads.4 = (s16[4,288,128]{2,1,0:T(8,128)(2,1)S(1)}, s16[4,288,128]{2,1,0:T(8,128)(2,1)S(1)}, s16[4,288,128]{2,1,0:T(8,128)(2,1)S(1)}) custom-call(s32[68]{0:T(128)S(1)} %copy-done.10, f32[24,2,288,128]{3,2,1,0:T(8,128)S(1)} %get-tuple-element.97.slope_ref, s16[4,288,128]{2,1,0:T(8,128)(2,1)S(1)} %get-tuple-element.117.refs_0_, ...), custom_call_target="tpu_custom_call" | custom-call | flops 1 | bytes 1 | tf_op jit(solution)/shard_map/depth_grads/pallas_call | solution.py:263
  65.0 3.0 %collective-permute-done.7.refs_0_.refs_3_ = s16[4,288,128]{2,1,0:T(8,128)(2,1)S(1)} collective-permute-done((s16[4,288,128]{2,1,0:T(8,128)(2,1)S(1)}, s16[4,288,128]{2,1,0:T(8,128)(2,1)S(1)}, u32[]{:S(2)}, u32[]{:S(2)}) %collective-permute-start.7) | collective-permute-done | bytes 294944 | tf_op jit(solution)/shard_map/ppermute | solution.py:610
  68.9 4.6 %view_sums.3.refs_1_ = f32[24,16,128]{2,1,0:T(8,128)S(1)} custom-call(s32[68]{0:T(128)S(1)} %copy-done.10, f32[24,16]{1,0:T(8,128)S(1)} %copy-done.8, f32[1]{0:T(128)} %bitcast.3.row_ref, bf16[24,4,288,128]{3,2,1,0:T(8,128)(2,1)S(1)} %get-tuple-element.92.view_ref, s16[4,288,128]{2,1,0:T(8,128)(2,1)S(1)} %get-tuple-element.117.refs_0_, ...), custom_call_target="tpu_custom_call" | custom-call | flops 1 | bytes 1 | tf_op jit(solution)/shard_map/view_sums/pallas_call | solution.py:325
  75.2 2.7 %collective-permute-done.8.refs_0_ = s16[4,288,128]{2,1,0:T(8,128)(2,1)S(1)} collective-permute-done((s16[4,288,128]{2,1,0:T(8,128)(2,1)S(1)}, s16[4,288,128]{2,1,0:T(8,128)(2,1)S(1)}, u32[]{:S(2)}, u32[]{:S(2)}) %collective-permute-start.8) | collective-permute-done | bytes 294944 | tf_op jit(solution)/shard_map/ppermute | solution.py:610
  77.9 1.3 %fold_codes.1 = s16[8,288,128]{2,1,0:T(8,128)(2,1)S(1)} custom-call(s32[68]{0:T(128)S(1)} %copy-done.10, f32[8,288,128]{2,1,0:T(8,128)S(1)} %fold_totals.2.total_ref, s16[4,288,128]{2,1,0:T(8,128)(2,1)S(1)} %collective-permute-done.8.refs_0_), custom_call_target="tpu_custom_call" | custom-call | flops 1 | bytes 1 | tf_op jit(solution)/shard_map/fold_codes/pallas_call | solution.py:379
  79.3 2.7 %view_terms.1 = f32[76,7]{1,0:T(8,128)} custom-call(s32[2,12]{1,0:T(2,128)} %bitcast.41, f32[24,7]{1,0:T(8,128)} %get-tuple-element.106.cam_ref, f32[24,7]{1,0:T(8,128)} %get-tuple-element.107.pose_ref, f32[24,16,128]{2,1,0:T(8,128)} %copy-done.5, f32[24,16,128]{2,1,0:T(8,128)} %copy-done.6), custom_call_target="tpu_custom_call" | custom-call | flops 1 | bytes 1 | tf_op jit(solution)/shard_map/view_terms/pallas_call | solution.py:552
  83.7 1.8 %collective-permute-start.15 = (s16[4,288,128]{2,1,0:T(8,128)(2,1)}, s16[4,288,128]{2,1,0:T(8,128)(2,1)S(1)}, u32[]{:S(2)}, u32[]{:S(2)}) collective-permute-start(s16[4,288,128]{2,1,0:T(8,128)(2,1)} %copy-done.11), channel_id=1, source_target_pairs={{0,12},{4,8},{8,4},{12,0},{16,28},{20,24},{24,20},{28,16},{1,13},{... | collective-permute-start | bytes 884744 | tf_op jit(solution)/shard_map/ppermute | solution.py:610
  87.6 1.5 %collective-permute-start.12 = (f32[76,7]{0,1:T(8,128)S(1)}, f32[76,7]{0,1:T(8,128)S(1)}, u32[]{:S(2)}, u32[]{:S(2)}) collective-permute-start(f32[76,7]{0,1:T(8,128)S(1)} %add.11), channel_id=1, source_target_pairs={{0,2},{1,3},{2,0},{3,1},{4,6},{5,7},{6,4},{7,5},{8,10},{9,11},{10,... | collective-permute-start | bytes 6392 | tf_op jit(solution)/shard_map/ppermute | solution.py:668
  89.1 2.1 %collective-permute-done.12 = f32[76,7]{0,1:T(8,128)S(1)} collective-permute-done((f32[76,7]{0,1:T(8,128)S(1)}, f32[76,7]{0,1:T(8,128)S(1)}, u32[]{:S(2)}, u32[]{:S(2)}) %collective-permute-start.12) | collective-permute-done | bytes 2160 | tf_op jit(solution)/shard_map/ppermute | solution.py:668
  91.9 4.2 %all-to-all-start.1 = ((f32[8,8,7]{2,1,0:T(8,128)}), f32[8,8,7]{2,1,0:T(8,128)}, u32[]{:S(2)}, u32[]{:S(2)}) async-start(f32[8,8,7]{2,1,0:T(8,128)} %bitcast.35), calls=%async_computation.1 | async-start | bytes 65536 | tf_op jit(solution)/shard_map/all_to_all | solution.py:672
  96.7 6.1 %collective-permute-done.14.refs_2_ = s16[4,288,128]{2,1,0:T(8,128)(2,1)S(1)} collective-permute-done((s16[4,288,128]{2,1,0:T(8,128)(2,1)}, s16[4,288,128]{2,1,0:T(8,128)(2,1)S(1)}, u32[]{:S(2)}, u32[]{:S(2)}) %collective-permute-start.14) | collective-permute-done | bytes 294944 | tf_op jit(solution)/shard_map/ppermute | solution.py:610
  102.9 1.8 %collective-permute-done.15.refs_3_ = s16[4,288,128]{2,1,0:T(8,128)(2,1)S(1)} collective-permute-done((s16[4,288,128]{2,1,0:T(8,128)(2,1)}, s16[4,288,128]{2,1,0:T(8,128)(2,1)S(1)}, u32[]{:S(2)}, u32[]{:S(2)}) %collective-permute-start.15) | collective-permute-done | bytes 294944 | tf_op jit(solution)/shard_map/ppermute | solution.py:610
  104.7 1.2 %fold_totals.3.local_ref = f32[8,288,128]{2,1,0:T(8,128)S(1)} custom-call(s32[68]{0:T(128)S(1)} %copy-done.10, s16[4,288,128]{2,1,0:T(8,128)(2,1)S(1)} %get-tuple-element.129.refs_0_, s16[4,288,128]{2,1,0:T(8,128)(2,1)S(1)} %collective-permute-done.13.refs_1_, s16[4,288,128]{2,1,0:T(8,128)(2,1)S(1)} %collective-permute-done.14.refs_2_, ...), custom_call_target="tpu_custom_call" | custom-call | flops 1 | bytes 1 | tf_op jit(solution)/shard_map/fold_totals/pallas_call | solution.py:356
  105.9 3.4 %update_depths.1 = (f32[8,36864]{1,0:T(8,128)}, f32[8,36864]{1,0:T(8,128)}, f32[8,36864]{1,0:T(8,128)}) custom-call(f32[8,288,128]{2,1,0:T(8,128)S(1)} %fold_totals.3.local_ref, s16[8,288,128]{2,1,0:T(8,128)(2,1)S(1)} %collective-permute-done.16.far_ref, f32[8,36864]{1,0:T(8,128)S(1)} %copy-done.1, f32[8,36864]{1,0:T(8,128)S(1)} %copy-done.3, ...), custom_call_target="tpu_custom_call" | custom-call | flops 1 | bytes 1 | tf_op jit(solution)/shard_map/update_depths/pallas_call | solution.py:422
  109.3 1.4 %update_small.1 = (f32[8,7]{1,0:T(8,128)}, f32[8,7]{1,0:T(8,128)}, f32[8,7]{1,0:T(8,128)}, f32[7,12]{1,0:T(8,128)}, f32[7,12]{1,0:T(8,128)}, /*index=5*/f32[7,12]{1,0:T(8,128)}) custom-call(f32[8,8,7]{2,1,0:T(8,128)} %all-to-all-done.1.mail_ref, f32[7,12]{1,0:T(8,128)} %slice_bitcast_fusion.pose_ref, f32[8,7]{1,0:T(8,128)} %refs_0_.1, f32[8,7]{1,0:T(8,128)} %refs_1_.1, ...), custom_call_target="tpu_custom_call" | custom-call | flops 1 | bytes 1 | tf_op jit(solution)/shard_map/update_small/pallas_call | solution.py:574
  (61 shorter events, 13.2 us)
Async XLA Ops:
  2.2 33.6 %copy-start.13 = (f32[12,7]{0,1:T(8,128)S(1)}, f32[12,7]{0,1:T(8,128)}, u32[]{:S(2)}) copy-start(f32[12,7]{0,1:T(8,128)} %param.19) | copy-start | bytes 1012
  2.3 38.2 %copy-start.2 = (bf16[12,2,36864]{2,1,0:T(2,128)(2,1)S(1)}, bf16[12,2,36864]{2,1,0:T(2,128)(2,1)}, u32[]{:S(2)}) copy-start(bf16[12,2,36864]{2,1,0:T(2,128)(2,1)} %param.23) | copy-start | bytes 5308420
  4.5 24.8 %all-to-all-start = ((f32[8,9,128]{2,1,0:T(8,128)}), f32[8,9,128]{2,1,0:T(8,128)S(1)}, u32[]{:S(2)}, u32[]{:S(2)}) async-start(f32[8,9,128]{2,1,0:T(8,128)} %letters_of.1), calls=%async_computation | async-start | bytes 131072 | tf_op jit(solution)/shard_map/all_to_all | solution.py:626
  11.7 36.6 %collective-permute-start.1 = (s16[8,144,128]{2,1,0:T(8,128)(2,1)}, s16[8,144,128]{2,1,0:T(8,128)(2,1)S(1)}, u32[]{:S(2)}, u32[]{:S(2)}) collective-permute-start(s16[8,144,128]{2,1,0:T(8,128)(2,1)} %get-tuple-element.79), channel_id=1, source_target_pairs={{0,16},{4,20},{8,24},{12,28},{16,0},{20,4},{24,8},{28,12},{1,17},{... | collective-permute-start | bytes 884744 | tf_op jit(solution)/shard_map/ppermute | solution.py:610
  14.7 33.7 %collective-permute-start = (s16[8,144,128]{2,1,0:T(8,128)(2,1)}, s16[8,144,128]{2,1,0:T(8,128)(2,1)}, u32[]{:S(2)}, u32[]{:S(2)}) collective-permute-start(s16[8,144,128]{2,1,0:T(8,128)(2,1)} %get-tuple-element.147), channel_id=1, source_target_pairs={{0,16},{4,20},{8,24},{12,28},{16,0},{20,4},{24,8},{28,12},{1,17},{... | collective-permute-start | bytes 884744 | tf_op jit(solution)/shard_map/ppermute | solution.py:610
  32.2 0.7 copy-start.9
  34.4 16.7 %collective-permute-start.4 = (s16[4,288,128]{2,1,0:T(8,128)(2,1)}, s16[4,288,128]{2,1,0:T(8,128)(2,1)S(1)}, u32[]{:S(2)}, u32[]{:S(2)}) collective-permute-start(s16[4,288,128]{2,1,0:T(8,128)(2,1)} %get-tuple-element.94), channel_id=1, source_target_pairs={{0,4},{4,0},{8,12},{12,8},{16,20},{20,16},{24,28},{28,24},{1,5},{5... | collective-permute-start | bytes 884744 | tf_op jit(solution)/shard_map/ppermute | solution.py:610
  36.5 16.6 %collective-permute-start.5 = (s16[4,288,128]{2,1,0:T(8,128)(2,1)}, s16[4,288,128]{2,1,0:T(8,128)(2,1)S(1)}, u32[]{:S(2)}, u32[]{:S(2)}) collective-permute-start(s16[4,288,128]{2,1,0:T(8,128)(2,1)} %get-tuple-element.95), channel_id=1, source_target_pairs={{0,8},{4,12},{8,0},{12,4},{16,24},{20,28},{24,16},{28,20},{1,9},{5... | collective-permute-start | bytes 884744 | tf_op jit(solution)/shard_map/ppermute | solution.py:610
  36.5 19.0 %collective-permute-start.6 = (s16[4,288,128]{2,1,0:T(8,128)(2,1)S(1)}, s16[4,288,128]{2,1,0:T(8,128)(2,1)S(1)}, u32[]{:S(2)}, u32[]{:S(2)}) collective-permute-start(s16[4,288,128]{2,1,0:T(8,128)(2,1)S(1)} %get-tuple-element.96), channel_id=1, source_target_pairs={{0,12},{4,8},{8,4},{12,0},{16,28},{20,24},{24,20},{28,16},{1,13},{... | collective-permute-start | bytes 884744 | tf_op jit(solution)/shard_map/ppermute | solution.py:610
  40.4 2.5 %copy-start = (bf16[12,2,3,36864]{3,1,2,0:T(2,128)(2,1)S(1)}, bf16[12,2,3,36864]{3,1,2,0:T(2,128)(2,1)}, u32[]{:S(2)}) copy-start(bf16[12,2,3,36864]{3,1,2,0:T(2,128)(2,1)} %param.22) | copy-start | bytes 15925252
  43.0 0.7 copy-start.7
  43.7 4.7 %copy-start.10 = (s32[68]{0:T(128)S(1)}, s32[68]{0:T(128)}, u32[]{:S(2)}) copy-start(s32[68]{0:T(128)} %slot_tables.1.tab_ref) | copy-start | bytes 820
  43.7 11.8 %copy-start.8 = (f32[24,16]{1,0:T(8,128)S(1)}, f32[24,16]{1,0:T(8,128)}, u32[]{:S(2)}) copy-start(f32[24,16]{1,0:T(8,128)} %get-tuple-element.85.coef_ref) | copy-start | bytes 4612
  49.6 13.5 %collective-permute-start.2 = (s16[4,288,128]{2,1,0:T(8,128)(2,1)S(1)}, s16[4,288,128]{2,1,0:T(8,128)(2,1)S(1)}, u32[]{:S(2)}, u32[]{:S(2)}) collective-permute-start(s16[4,288,128]{2,1,0:T(8,128)(2,1)S(1)} %get-tuple-element.90), channel_id=1, source_target_pairs={{0,4},{4,0},{8,12},{12,8},{16,20},{20,16},{24,28},{28,24},{1,5},{5... | collective-permute-start | bytes 884744 | tf_op jit(solution)/shard_map/ppermute | solution.py:610
  51.1 12.0 %collective-permute-start.3 = (s16[4,288,128]{2,1,0:T(8,128)(2,1)S(1)}, s16[4,288,128]{2,1,0:T(8,128)(2,1)S(1)}, u32[]{:S(2)}, u32[]{:S(2)}) collective-permute-start(s16[4,288,128]{2,1,0:T(8,128)(2,1)S(1)} %get-tuple-element.91), channel_id=1, source_target_pairs={{0,8},{4,12},{8,0},{12,4},{16,24},{20,28},{24,16},{28,20},{1,9},{5... | collective-permute-start | bytes 884744 | tf_op jit(solution)/shard_map/ppermute | solution.py:610
  51.1 17.0 %collective-permute-start.7 = (s16[4,288,128]{2,1,0:T(8,128)(2,1)S(1)}, s16[4,288,128]{2,1,0:T(8,128)(2,1)S(1)}, u32[]{:S(2)}, u32[]{:S(2)}) collective-permute-start(s16[4,288,128]{2,1,0:T(8,128)(2,1)S(1)} %get-tuple-element.109), channel_id=1, source_target_pairs={{0,12},{4,8},{8,4},{12,0},{16,28},{20,24},{24,20},{28,16},{1,13},{... | collective-permute-start | bytes 884744 | tf_op jit(solution)/shard_map/ppermute | solution.py:610
  60.7 2.3 %copy-start.5 = (f32[24,16,128]{2,1,0:T(8,128)}, f32[24,16,128]{2,1,0:T(8,128)S(1)}, u32[]{:S(2)}) copy-start(f32[24,16,128]{2,1,0:T(8,128)S(1)} %view_sums.2.refs_0_) | copy-start | bytes 589828
  63.0 1.2 %copy-start.11 = (s16[4,288,128]{2,1,0:T(8,128)(2,1)}, s16[4,288,128]{2,1,0:T(8,128)(2,1)S(1)}, u32[]{:S(2)}) copy-start(s16[4,288,128]{2,1,0:T(8,128)(2,1)S(1)} %get-tuple-element.132) | copy-start | bytes 884740
  64.3 9.9 %collective-permute-start.9 = (s16[4,288,128]{2,1,0:T(8,128)(2,1)S(1)}, s16[4,288,128]{2,1,0:T(8,128)(2,1)S(1)}, u32[]{:S(2)}, u32[]{:S(2)}) collective-permute-start(s16[4,288,128]{2,1,0:T(8,128)(2,1)S(1)} %get-tuple-element.114), channel_id=1, source_target_pairs={{0,4},{4,0},{8,12},{12,8},{16,20},{20,16},{24,28},{28,24},{1,5},{5... | collective-permute-start | bytes 884744 | tf_op jit(solution)/shard_map/ppermute | solution.py:610
  65.0 9.1 %collective-permute-start.10 = (s16[4,288,128]{2,1,0:T(8,128)(2,1)S(1)}, s16[4,288,128]{2,1,0:T(8,128)(2,1)S(1)}, u32[]{:S(2)}, u32[]{:S(2)}) collective-permute-start(s16[4,288,128]{2,1,0:T(8,128)(2,1)S(1)} %get-tuple-element.115), channel_id=1, source_target_pairs={{0,8},{4,12},{8,0},{12,4},{16,24},{20,28},{24,16},{28,20},{1,9},{5... | collective-permute-start | bytes 884744 | tf_op jit(solution)/shard_map/ppermute | solution.py:610
  68.8 9.1 %collective-permute-start.8 = (s16[4,288,128]{2,1,0:T(8,128)(2,1)S(1)}, s16[4,288,128]{2,1,0:T(8,128)(2,1)S(1)}, u32[]{:S(2)}, u32[]{:S(2)}) collective-permute-start(s16[4,288,128]{2,1,0:T(8,128)(2,1)S(1)} %depth_grads.5), channel_id=1, source_target_pairs={{0,12},{4,8},{8,4},{12,0},{16,28},{20,24},{24,20},{28,16},{1,13},{... | collective-permute-start | bytes 884744 | tf_op jit(solution)/shard_map/ppermute | solution.py:610
  73.5 0.7 copy-start.6
  77.9 28.0 %copy-start.4 = (f32[8,36864]{1,0:T(8,128)S(1)}, f32[8,36864]{1,0:T(8,128)}, u32[]{:S(2)}) copy-start(f32[8,36864]{1,0:T(8,128)} %s_ref.1) | copy-start | bytes 3538948
  79.2 26.6 %collective-permute-start.16 = (s16[8,288,128]{2,1,0:T(8,128)(2,1)S(1)}, s16[8,288,128]{2,1,0:T(8,128)(2,1)S(1)}, u32[]{:S(2)}, u32[]{:S(2)}) collective-permute-start(s16[8,288,128]{2,1,0:T(8,128)(2,1)S(1)} %fold_codes.1), channel_id=1, source_target_pairs={{0,16},{4,20},{8,24},{12,28},{16,0},{20,4},{24,8},{28,12},{1,17},{... | collective-permute-start | bytes 1769480 | tf_op jit(solution)/shard_map/ppermute | solution.py:610
  82.0 14.7 %collective-permute-start.13 = (s16[4,288,128]{2,1,0:T(8,128)(2,1)}, s16[4,288,128]{2,1,0:T(8,128)(2,1)S(1)}, u32[]{:S(2)}, u32[]{:S(2)}) collective-permute-start(s16[4,288,128]{2,1,0:T(8,128)(2,1)} %get-tuple-element.130), channel_id=1, source_target_pairs={{0,4},{4,0},{8,12},{12,8},{16,20},{20,16},{24,28},{28,24},{1,5},{5... | collective-permute-start | bytes 884744 | tf_op jit(solution)/shard_map/ppermute | solution.py:610
  83.1 19.7 %collective-permute-start.14 = (s16[4,288,128]{2,1,0:T(8,128)(2,1)}, s16[4,288,128]{2,1,0:T(8,128)(2,1)S(1)}, u32[]{:S(2)}, u32[]{:S(2)}) collective-permute-start(s16[4,288,128]{2,1,0:T(8,128)(2,1)} %get-tuple-element.131), channel_id=1, source_target_pairs={{0,8},{4,12},{8,0},{12,4},{16,24},{20,28},{24,16},{28,20},{1,9},{5... | collective-permute-start | bytes 884744 | tf_op jit(solution)/shard_map/ppermute | solution.py:610
  83.7 21.0 %collective-permute-start.15 = (s16[4,288,128]{2,1,0:T(8,128)(2,1)}, s16[4,288,128]{2,1,0:T(8,128)(2,1)S(1)}, u32[]{:S(2)}, u32[]{:S(2)}) collective-permute-start(s16[4,288,128]{2,1,0:T(8,128)(2,1)} %copy-done.11), channel_id=1, source_target_pairs={{0,12},{4,8},{8,4},{12,0},{16,28},{20,24},{24,20},{28,16},{1,13},{... | collective-permute-start | bytes 884744 | tf_op jit(solution)/shard_map/ppermute | solution.py:610
  86.4 1.2 %collective-permute-start.11 = (f32[76,7]{0,1:T(8,128)S(1)}, f32[76,7]{0,1:T(8,128)S(1)}, u32[]{:S(2)}, u32[]{:S(2)}) collective-permute-start(f32[76,7]{0,1:T(8,128)S(1)} %copy.25), channel_id=1, source_target_pairs={{0,1},{1,0},{2,3},{3,2},{4,5},{5,4},{6,7},{7,6},{8,9},{9,8},{10,11... | collective-permute-start | bytes 6392 | tf_op jit(solution)/shard_map/ppermute | solution.py:668
  87.6 3.6 %collective-permute-start.12 = (f32[76,7]{0,1:T(8,128)S(1)}, f32[76,7]{0,1:T(8,128)S(1)}, u32[]{:S(2)}, u32[]{:S(2)}) collective-permute-start(f32[76,7]{0,1:T(8,128)S(1)} %add.11), channel_id=1, source_target_pairs={{0,2},{1,3},{2,0},{3,1},{4,6},{5,7},{6,4},{7,5},{8,10},{9,11},{10,... | collective-permute-start | bytes 6392 | tf_op jit(solution)/shard_map/ppermute | solution.py:668
  91.9 17.5 %all-to-all-start.1 = ((f32[8,8,7]{2,1,0:T(8,128)}), f32[8,8,7]{2,1,0:T(8,128)}, u32[]{:S(2)}, u32[]{:S(2)}) async-start(f32[8,8,7]{2,1,0:T(8,128)} %bitcast.35), calls=%async_computation.1 | async-start | bytes 65536 | tf_op jit(solution)/shard_map/all_to_all | solution.py:672
  96.7 9.2 %copy-start.1 = (f32[8,36864]{1,0:T(8,128)S(1)}, f32[8,36864]{1,0:T(8,128)}, u32[]{:S(2)}) copy-start(f32[8,36864]{1,0:T(8,128)} %x_ref.1) | copy-start | bytes 3538948
  96.7 9.2 %copy-start.3 = (f32[8,36864]{1,0:T(8,128)S(1)}, f32[8,36864]{1,0:T(8,128)}, u32[]{:S(2)}) copy-start(f32[8,36864]{1,0:T(8,128)} %m_ref.1) | copy-start | bytes 3538948
  (1 other events, 0.6 us)

commit v6 on v5

--- a/solution.py
+++ b/solution.py
@@ -415,7 +415,7 @@
 
 def update_depths(local, far, values, moment, second, bound, chunk, done):
     images, rows, _ = far.shape
-    block = 48
+    block = 96
     steps = rows // block
     first = chunk * steps
     wide = pl.BlockSpec((images, block * LANES), lambda t: (0, first + t))
@@ -655,7 +655,7 @@
     folded, far_sums = tie((folded, far_sums))
     far_codes = [swap(part, half) for part in folded]
     small = view_terms(names, cams, poses, [near_sums, far_sums], shards * images)
-    near_grads, small = tie((near_grads, small))
+    near_grads, _ = tie((near_grads, totals))
     near_total = fold_totals(table, exchange(near_grads), 0, every, images, cap)
     done = []
     for c in range(1):

time: 111 us -> 111 us (level)
  local copies, waits for them, and re-layouts: 8.39 us -> 9.84 us
    unnamed x30 -> x32, local copies, waits for them, and re-layouts: 5.33 us -> 6.77 us
  transfers between devices with their start and end apart: 19 -> 19, of which waited for: 8 -> 8; matrix products, arithmetic and copies ran while one was open for 3% -> 3% of each run, Pallas kernels for 31% -> 30%
where the time goes in v6:
time: 111 us
  Pallas kernels  37.7 us (34%)
  waiting for transfers between devices  32.8 us (30%)
  starting transfers between devices  27.6 us (25%)
  local copies, waits for them, and re-layouts  9.84 us (9%)
  other arithmetic  2.14 us (2%)
    ppermute x15, waiting for transfers between devices, swap(): return lax.ppermute(value, 'img', [(i, i ^ k) for i in range(shards)])  15 us
    ppermute x15, starting transfers between devices, swap(): return lax.ppermute(value, 'img', [(i, i ^ k) for i in range(shards)])  14.7 us
    all_to_all x1, waiting for transfers between devices, body(): mail = lax.all_to_all(letters, 'img', 0, 0, tiled=True)  14.6 us
    pallas_call x2, Pallas kernels, view_sums(): pl.pallas_call(functools.partial(sum_kernel, first, half, cap), out_shape...  9.89 us
    all_to_all x1, starting transfers between devices, body(): mail = lax.all_to_all(letters, 'img', 0, 0, tiled=True)  7.25 us
    unnamed x32, local copies, waits for them, and re-layouts  6.77 us
    pallas_call x1, Pallas kernels, prepare_views(): pl.pallas_call(prepare_kernel, out_shape=[jax.ShapeDtypeStruct((2 * pairs...  4.67 us
    pallas_call x3, Pallas kernels, depth_grads(): pl.pallas_call(functools.partial(grad_kernel, first, ks, cap), out_shape=...  4.28 us
  transfers between devices with their start and end apart: 19, of which 8 were waited for; matrix products, arithmetic and copies ran while one was open for 3% of the time, Pallas kernels for 30%

profile of v6, /device:TPU:0, one launch (start us, length us, event | category | flops | bytes accessed | tf_op | source)
XLA Modules:
  0.0 110.9 jit_solution(9346582139073226094)
XLA Ops:
  0.6 1.5 %fusion = s16[1,8,288,128]{3,1,2,0:T(8,128)(2,1)S(1)} fusion(f32[8,36864]{1,0:T(8,128)} %x_ref.1), kind=kLoop, calls=%fused_computation.1 | loop fusion | flops 1179648 | bytes 1769472
  3.1 1.3 %letters_of.1 = f32[8,9,128]{2,1,0:T(8,128)} custom-call(s32[2,12]{1,0:T(2,128)} %bitcast.39, f32[8,7]{1,0:T(8,128)} %refs_0_.1), custom_call_target="tpu_custom_call" | custom-call | flops 1 | bytes 1 | tf_op jit(solution)/shard_map/letters_of/pallas_call | solution.py:80
  4.5 7.3 %all-to-all-start = ((f32[8,9,128]{2,1,0:T(8,128)}), f32[8,9,128]{2,1,0:T(8,128)S(1)}, u32[]{:S(2)}, u32[]{:S(2)}) async-start(f32[8,9,128]{2,1,0:T(8,128)} %letters_of.1), calls=%async_computation | async-start | bytes 131072 | tf_op jit(solution)/shard_map/all_to_all | solution.py:626
  11.7 2.9 %collective-permute-start.1 = (s16[8,144,128]{2,1,0:T(8,128)(2,1)}, s16[8,144,128]{2,1,0:T(8,128)(2,1)S(1)}, u32[]{:S(2)}, u32[]{:S(2)}) collective-permute-start(s16[8,144,128]{2,1,0:T(8,128)(2,1)} %get-tuple-element.85), channel_id=1, source_target_pairs={{0,16},{4,20},{8,24},{12,28},{16,0},{20,4},{24,8},{28,12},{1,17},{... | collective-permute-start | bytes 884744 | tf_op jit(solution)/shard_map/ppermute | solution.py:610
  14.7 14.6 %all-to-all-done.all_ref = f32[8,9,128]{2,1,0:T(8,128)S(1)} async-done(((f32[8,9,128]{2,1,0:T(8,128)}), f32[8,9,128]{2,1,0:T(8,128)S(1)}, u32[]{:S(2)}, u32[]{:S(2)}) %all-to-all-start) | async-done | bytes 36896 | tf_op jit(solution)/shard_map/all_to_all | solution.py:626
  29.9 2.3 %slot_tables.1.tab_ref = s32[68]{0:T(128)} custom-call(s32[1]{0:T(128)} %bitcast.1.me_ref, s32[8,24]{1,0:T(8,128)} %bitcast.37), custom_call_target="tpu_custom_call" | custom-call | flops 1 | bytes 1 | tf_op jit(solution)/shard_map/slot_tables/pallas_call | solution.py:127
  32.8 1.4 %pack_slots.2 = (s16[4,288,128]{2,1,0:T(8,128)(2,1)S(1)}, s16[4,288,128]{2,1,0:T(8,128)(2,1)}, s16[4,288,128]{2,1,0:T(8,128)(2,1)S(1)}, s16[4,288,128]{2,1,0:T(8,128)(2,1)S(1)}) custom-call(s32[68]{0:T(128)S(1)} %copy-done.9, s16[8,288,128]{2,1,0:T(8,128)(2,1)S(1)} %bitcast.33), custom_call_target="tpu_custom_call" | custom-call | flops 1 | bytes 1 | tf_op jit(solution)/shard_map/pack_slots/pallas_call | solution.py:154
  35.7 1.4 %collective-permute-start.4 = (s16[4,288,128]{2,1,0:T(8,128)(2,1)}, s16[4,288,128]{2,1,0:T(8,128)(2,1)S(1)}, u32[]{:S(2)}, u32[]{:S(2)}) collective-permute-start(s16[4,288,128]{2,1,0:T(8,128)(2,1)} %get-tuple-element.95), channel_id=1, source_target_pairs={{0,4},{4,0},{8,12},{12,8},{16,20},{20,16},{24,28},{28,24},{1,5},{5... | collective-permute-start | bytes 884744 | tf_op jit(solution)/shard_map/ppermute | solution.py:610
  37.8 2.0 %collective-permute-start.6 = (s16[4,288,128]{2,1,0:T(8,128)(2,1)}, s16[4,288,128]{2,1,0:T(8,128)(2,1)S(1)}, u32[]{:S(2)}, u32[]{:S(2)}) collective-permute-start(s16[4,288,128]{2,1,0:T(8,128)(2,1)} %copy-done.11), channel_id=1, source_target_pairs={{0,12},{4,8},{8,4},{12,0},{16,28},{20,24},{24,20},{28,16},{1,13},{... | collective-permute-start | bytes 884744 | tf_op jit(solution)/shard_map/ppermute | solution.py:610
  39.9 1.9 %view_coefs.1 = (f32[24,16]{1,0:T(8,128)}, f32[24,7]{1,0:T(8,128)}, f32[24,7]{1,0:T(8,128)}) custom-call(s32[2,12]{1,0:T(2,128)} %bitcast.40, f32[8,9,128]{2,1,0:T(8,128)} %copy-done.13, f32[12,7]{1,0:T(8,128)} %copy.21.pair_ref), custom_call_target="tpu_custom_call" | custom-call | flops 1 | bytes 1 | tf_op jit(solution)/shard_map/view_coefs/pallas_call | solution.py:504
  41.8 2.5 %copy-done = bf16[12,2,3,36864]{3,1,2,0:T(2,128)(2,1)S(1)} copy-done((bf16[12,2,3,36864]{3,1,2,0:T(2,128)(2,1)S(1)}, bf16[12,2,3,36864]{3,1,2,0:T(2,128)(2,1)}, u32[]{:S(2)}) %copy-start) | copy-done | bytes 5308440
  45.0 4.7 %prepare_views.1 = (bf16[24,4,288,128]{3,2,1,0:T(8,128)(2,1)S(1)}, f32[24,2,288,128]{3,2,1,0:T(8,128)S(1)}) custom-call(f32[1]{0:T(128)} %bitcast.3.row_ref, f32[24,16]{1,0:T(8,128)S(1)} %copy-done.7, bf16[12,3,576,128]{3,2,1,0:T(8,128)(2,1)S(1)} %bitcast.31, bf16[12,576,128]{2,1,0:T(8,128)(2,1)S(1)} %bitcast.34), custom_call_target="tpu_custom_call" | custom-call | flops 1 | bytes 1 | tf_op jit(solution)/shard_map/prepare_views/pallas_call | solution.py:224
  49.7 1.2 %pack_slots.3 = (s16[4,288,128]{2,1,0:T(8,128)(2,1)S(1)}, s16[4,288,128]{2,1,0:T(8,128)(2,1)S(1)}, s16[4,288,128]{2,1,0:T(8,128)(2,1)S(1)}, s16[4,288,128]{2,1,0:T(8,128)(2,1)S(1)}) custom-call(s32[68]{0:T(128)S(1)} %copy-done.10, s16[8,144,128]{2,1,0:T(8,128)(2,1)} %collective-permute-done.refs_0_, s16[8,144,128]{2,1,0:T(8,128)(2,1)S(1)} %collective-permute-done.1.refs_1_), custom_call_target="tpu_custom_call" | custom-call | flops 1 | bytes 1 | tf_op jit(solution)/shard_map/pack_slots/pallas_call | solution.py:154
  50.9 1.5 %collective-permute-start.2 = (s16[4,288,128]{2,1,0:T(8,128)(2,1)S(1)}, s16[4,288,128]{2,1,0:T(8,128)(2,1)S(1)}, u32[]{:S(2)}, u32[]{:S(2)}) collective-permute-start(s16[4,288,128]{2,1,0:T(8,128)(2,1)S(1)} %get-tuple-element.91), channel_id=1, source_target_pairs={{0,4},{4,0},{8,12},{12,8},{16,20},{20,16},{24,28},{28,24},{1,5},{5... | collective-permute-start | bytes 884744 | tf_op jit(solution)/shard_map/ppermute | solution.py:610
  52.4 2.0 %collective-permute-start.7 = (s16[4,288,128]{2,1,0:T(8,128)(2,1)S(1)}, s16[4,288,128]{2,1,0:T(8,128)(2,1)S(1)}, u32[]{:S(2)}, u32[]{:S(2)}) collective-permute-start(s16[4,288,128]{2,1,0:T(8,128)(2,1)S(1)} %get-tuple-element.104), channel_id=1, source_target_pairs={{0,12},{4,8},{8,4},{12,0},{16,28},{20,24},{24,20},{28,16},{1,13},{... | collective-permute-start | bytes 884744 | tf_op jit(solution)/shard_map/ppermute | solution.py:610
  55.4 4.9 %view_sums.2.refs_0_ = f32[24,16,128]{2,1,0:T(8,128)S(1)} custom-call(s32[68]{0:T(128)S(1)} %copy-done.10, f32[24,16]{1,0:T(8,128)S(1)} %copy-done.8, f32[1]{0:T(128)} %bitcast.3.row_ref, bf16[24,4,288,128]{3,2,1,0:T(8,128)(2,1)S(1)} %get-tuple-element.93.view_ref, s16[4,288,128]{2,1,0:T(8,128)(2,1)S(1)} %get-tuple-element.94.refs_0_, ...), custom_call_target="tpu_custom_call" | custom-call | flops 1 | bytes 1 | tf_op jit(solution)/shard_map/view_sums/pallas_call | solution.py:325
  60.4 2.3 %depth_grads.3 = (s16[4,288,128]{2,1,0:T(8,128)(2,1)S(1)}, s16[4,288,128]{2,1,0:T(8,128)(2,1)}, s16[4,288,128]{2,1,0:T(8,128)(2,1)}, s16[4,288,128]{2,1,0:T(8,128)(2,1)}) custom-call(s32[68]{0:T(128)S(1)} %copy-done.10, f32[24,2,288,128]{3,2,1,0:T(8,128)S(1)} %get-tuple-element.98.slope_ref, s16[4,288,128]{2,1,0:T(8,128)(2,1)S(1)} %get-tuple-element.94.refs_0_, ...), custom_call_target="tpu_custom_call" | custom-call | flops 1 | bytes 1 | tf_op jit(solution)/shard_map/depth_grads/pallas_call | solution.py:263
  62.7 1.2 %depth_grads.4 = (s16[4,288,128]{2,1,0:T(8,128)(2,1)S(1)}, s16[4,288,128]{2,1,0:T(8,128)(2,1)S(1)}, s16[4,288,128]{2,1,0:T(8,128)(2,1)S(1)}) custom-call(s32[68]{0:T(128)S(1)} %copy-done.10, f32[24,2,288,128]{3,2,1,0:T(8,128)S(1)} %get-tuple-element.98.slope_ref, s16[4,288,128]{2,1,0:T(8,128)(2,1)S(1)} %get-tuple-element.112.refs_0_, ...), custom_call_target="tpu_custom_call" | custom-call | flops 1 | bytes 1 | tf_op jit(solution)/shard_map/depth_grads/pallas_call | solution.py:263
  64.9 3.2 %collective-permute-done.7.refs_0_.refs_3_ = s16[4,288,128]{2,1,0:T(8,128)(2,1)S(1)} collective-permute-done((s16[4,288,128]{2,1,0:T(8,128)(2,1)S(1)}, s16[4,288,128]{2,1,0:T(8,128)(2,1)S(1)}, u32[]{:S(2)}, u32[]{:S(2)}) %collective-permute-start.7) | collective-permute-done | bytes 294944 | tf_op jit(solution)/shard_map/ppermute | solution.py:610
  68.9 4.9 %view_sums.3.refs_1_ = f32[24,16,128]{2,1,0:T(8,128)S(1)} custom-call(s32[68]{0:T(128)S(1)} %copy-done.10, f32[24,16]{1,0:T(8,128)S(1)} %copy-done.8, f32[1]{0:T(128)} %bitcast.3.row_ref, bf16[24,4,288,128]{3,2,1,0:T(8,128)(2,1)S(1)} %get-tuple-element.93.view_ref, s16[4,288,128]{2,1,0:T(8,128)(2,1)S(1)} %get-tuple-element.112.refs_0_, ...), custom_call_target="tpu_custom_call" | custom-call | flops 1 | bytes 1 | tf_op jit(solution)/shard_map/view_sums/pallas_call | solution.py:325
  75.6 2.4 %collective-permute-done.8.refs_0_ = s16[4,288,128]{2,1,0:T(8,128)(2,1)S(1)} collective-permute-done((s16[4,288,128]{2,1,0:T(8,128)(2,1)S(1)}, s16[4,288,128]{2,1,0:T(8,128)(2,1)S(1)}, u32[]{:S(2)}, u32[]{:S(2)}) %collective-permute-start.8) | collective-permute-done | bytes 294944 | tf_op jit(solution)/shard_map/ppermute | solution.py:610
  78.0 1.3 %fold_codes.1 = s16[8,288,128]{2,1,0:T(8,128)(2,1)S(1)} custom-call(s32[68]{0:T(128)S(1)} %copy-done.10, f32[8,288,128]{2,1,0:T(8,128)S(1)} %fold_totals.2.total_ref, s16[4,288,128]{2,1,0:T(8,128)(2,1)S(1)} %collective-permute-done.8.refs_0_), custom_call_target="tpu_custom_call" | custom-call | flops 1 | bytes 1 | tf_op jit(solution)/shard_map/fold_codes/pallas_call | solution.py:379
  79.4 2.1 %collective-permute-start.13 = (s16[4,288,128]{2,1,0:T(8,128)(2,1)}, s16[4,288,128]{2,1,0:T(8,128)(2,1)S(1)}, u32[]{:S(2)}, u32[]{:S(2)}) collective-permute-start(s16[4,288,128]{2,1,0:T(8,128)(2,1)} %get-tuple-element.128), channel_id=1, source_target_pairs={{0,4},{4,0},{8,12},{12,8},{16,20},{20,16},{24,28},{28,24},{1,5},{5... | collective-permute-start | bytes 884744 | tf_op jit(solution)/shard_map/ppermute | solution.py:610
  83.0 2.7 %view_terms.1 = f32[76,7]{1,0:T(8,128)} custom-call(s32[2,12]{1,0:T(2,128)} %bitcast.41, f32[24,7]{1,0:T(8,128)} %get-tuple-element.83.cam_ref, f32[24,7]{1,0:T(8,128)} %get-tuple-element.84.pose_ref, f32[24,16,128]{2,1,0:T(8,128)} %copy-done.5, f32[24,16,128]{2,1,0:T(8,128)} %copy-done.6), custom_call_target="tpu_custom_call" | custom-call | flops 1 | bytes 1 | tf_op jit(solution)/shard_map/view_terms/pallas_call | solution.py:552
  86.6 1.2 %collective-permute-done.11 = f32[76,7]{0,1:T(8,128)S(1)} collective-permute-done((f32[76,7]{0,1:T(8,128)S(1)}, f32[76,7]{0,1:T(8,128)S(1)}, u32[]{:S(2)}, u32[]{:S(2)}) %collective-permute-start.11) | collective-permute-done | bytes 2160 | tf_op jit(solution)/shard_map/ppermute | solution.py:668
  87.8 1.5 %collective-permute-start.12 = (f32[76,7]{0,1:T(8,128)S(1)}, f32[76,7]{0,1:T(8,128)S(1)}, u32[]{:S(2)}, u32[]{:S(2)}) collective-permute-start(f32[76,7]{0,1:T(8,128)S(1)} %add.11), channel_id=1, source_target_pairs={{0,2},{1,3},{2,0},{3,1},{4,6},{5,7},{6,4},{7,5},{8,10},{9,11},{10,... | collective-permute-start | bytes 6392 | tf_op jit(solution)/shard_map/ppermute | solution.py:668
  89.3 2.1 %collective-permute-done.12 = f32[76,7]{0,1:T(8,128)S(1)} collective-permute-done((f32[76,7]{0,1:T(8,128)S(1)}, f32[76,7]{0,1:T(8,128)S(1)}, u32[]{:S(2)}, u32[]{:S(2)}) %collective-permute-start.12) | collective-permute-done | bytes 2160 | tf_op jit(solution)/shard_map/ppermute | solution.py:668
  92.1 4.1 %all-to-all-start.1 = ((f32[8,8,7]{2,1,0:T(8,128)}), f32[8,8,7]{2,1,0:T(8,128)}, u32[]{:S(2)}, u32[]{:S(2)}) async-start(f32[8,8,7]{2,1,0:T(8,128)} %bitcast.35), calls=%async_computation.1 | async-start | bytes 65536 | tf_op jit(solution)/shard_map/all_to_all | solution.py:672
  96.8 1.6 %collective-permute-done.14.refs_2_ = s16[4,288,128]{2,1,0:T(8,128)(2,1)S(1)} collective-permute-done((s16[4,288,128]{2,1,0:T(8,128)(2,1)}, s16[4,288,128]{2,1,0:T(8,128)(2,1)S(1)}, u32[]{:S(2)}, u32[]{:S(2)}) %collective-permute-start.14) | collective-permute-done | bytes 294944 | tf_op jit(solution)/shard_map/ppermute | solution.py:610
  98.4 6.8 %collective-permute-done.15.refs_3_ = s16[4,288,128]{2,1,0:T(8,128)(2,1)S(1)} collective-permute-done((s16[4,288,128]{2,1,0:T(8,128)(2,1)}, s16[4,288,128]{2,1,0:T(8,128)(2,1)S(1)}, u32[]{:S(2)}, u32[]{:S(2)}) %collective-permute-start.15) | collective-permute-done | bytes 294944 | tf_op jit(solution)/shard_map/ppermute | solution.py:610
  106.4 3.1 %update_depths.1 = (f32[8,36864]{1,0:T(8,128)}, f32[8,36864]{1,0:T(8,128)}, f32[8,36864]{1,0:T(8,128)}) custom-call(f32[8,288,128]{2,1,0:T(8,128)S(1)} %fold_totals.3.local_ref, s16[8,288,128]{2,1,0:T(8,128)(2,1)S(1)} %collective-permute-done.16.far_ref, f32[8,36864]{1,0:T(8,128)S(1)} %copy-done.1, f32[8,36864]{1,0:T(8,128)S(1)} %copy-done.3, ...), custom_call_target="tpu_custom_call" | custom-call | flops 1 | bytes 1 | tf_op jit(solution)/shard_map/update_depths/pallas_call | solution.py:422
  109.5 1.4 %update_small.1 = (f32[8,7]{1,0:T(8,128)}, f32[8,7]{1,0:T(8,128)}, f32[8,7]{1,0:T(8,128)}, f32[7,12]{1,0:T(8,128)}, f32[7,12]{1,0:T(8,128)}, /*index=5*/f32[7,12]{1,0:T(8,128)}) custom-call(f32[8,8,7]{2,1,0:T(8,128)} %all-to-all-done.1.mail_ref, f32[7,12]{1,0:T(8,128)} %slice_bitcast_fusion.pose_ref, f32[8,7]{1,0:T(8,128)} %refs_0_.1, f32[8,7]{1,0:T(8,128)} %refs_1_.1, ...), custom_call_target="tpu_custom_call" | custom-call | flops 1 | bytes 1 | tf_op jit(solution)/shard_map/update_small/pallas_call | solution.py:574
  (63 shorter events, 14.4 us)
Async XLA Ops:
  2.2 35.0 %copy-start.14 = (f32[12,7]{0,1:T(8,128)S(1)}, f32[12,7]{0,1:T(8,128)}, u32[]{:S(2)}) copy-start(f32[12,7]{0,1:T(8,128)} %param.19) | copy-start | bytes 1012
  2.3 39.5 %copy-start.2 = (bf16[12,2,36864]{2,1,0:T(2,128)(2,1)S(1)}, bf16[12,2,36864]{2,1,0:T(2,128)(2,1)}, u32[]{:S(2)}) copy-start(bf16[12,2,36864]{2,1,0:T(2,128)(2,1)} %param.23) | copy-start | bytes 5308420
  4.5 24.8 %all-to-all-start = ((f32[8,9,128]{2,1,0:T(8,128)}), f32[8,9,128]{2,1,0:T(8,128)S(1)}, u32[]{:S(2)}, u32[]{:S(2)}) async-start(f32[8,9,128]{2,1,0:T(8,128)} %letters_of.1), calls=%async_computation | async-start | bytes 131072 | tf_op jit(solution)/shard_map/all_to_all | solution.py:626
  11.7 38.0 %collective-permute-start.1 = (s16[8,144,128]{2,1,0:T(8,128)(2,1)}, s16[8,144,128]{2,1,0:T(8,128)(2,1)S(1)}, u32[]{:S(2)}, u32[]{:S(2)}) collective-permute-start(s16[8,144,128]{2,1,0:T(8,128)(2,1)} %get-tuple-element.85), channel_id=1, source_target_pairs={{0,16},{4,20},{8,24},{12,28},{16,0},{20,4},{24,8},{28,12},{1,17},{... | collective-permute-start | bytes 884744 | tf_op jit(solution)/shard_map/ppermute | solution.py:610
  14.7 35.0 %collective-permute-start = (s16[8,144,128]{2,1,0:T(8,128)(2,1)}, s16[8,144,128]{2,1,0:T(8,128)(2,1)}, u32[]{:S(2)}, u32[]{:S(2)}) collective-permute-start(s16[8,144,128]{2,1,0:T(8,128)(2,1)} %get-tuple-element.145), channel_id=1, source_target_pairs={{0,16},{4,20},{8,24},{12,28},{16,0},{20,4},{24,8},{28,12},{1,17},{... | collective-permute-start | bytes 884744 | tf_op jit(solution)/shard_map/ppermute | solution.py:610
  34.3 0.7 copy-start.11
  35.0 0.7 copy-start.12
  35.7 16.7 %collective-permute-start.4 = (s16[4,288,128]{2,1,0:T(8,128)(2,1)}, s16[4,288,128]{2,1,0:T(8,128)(2,1)S(1)}, u32[]{:S(2)}, u32[]{:S(2)}) collective-permute-start(s16[4,288,128]{2,1,0:T(8,128)(2,1)} %get-tuple-element.95), channel_id=1, source_target_pairs={{0,4},{4,0},{8,12},{12,8},{16,20},{20,16},{24,28},{28,24},{1,5},{5... | collective-permute-start | bytes 884744 | tf_op jit(solution)/shard_map/ppermute | solution.py:610
  37.8 16.6 %collective-permute-start.5 = (s16[4,288,128]{2,1,0:T(8,128)(2,1)}, s16[4,288,128]{2,1,0:T(8,128)(2,1)S(1)}, u32[]{:S(2)}, u32[]{:S(2)}) collective-permute-start(s16[4,288,128]{2,1,0:T(8,128)(2,1)} %copy-done.12), channel_id=1, source_target_pairs={{0,8},{4,12},{8,0},{12,4},{16,24},{20,28},{24,16},{28,20},{1,9},{5... | collective-permute-start | bytes 884744 | tf_op jit(solution)/shard_map/ppermute | solution.py:610
  37.8 17.6 %collective-permute-start.6 = (s16[4,288,128]{2,1,0:T(8,128)(2,1)}, s16[4,288,128]{2,1,0:T(8,128)(2,1)S(1)}, u32[]{:S(2)}, u32[]{:S(2)}) collective-permute-start(s16[4,288,128]{2,1,0:T(8,128)(2,1)} %copy-done.11), channel_id=1, source_target_pairs={{0,12},{4,8},{8,4},{12,0},{16,28},{20,24},{24,20},{28,16},{1,13},{... | collective-permute-start | bytes 884744 | tf_op jit(solution)/shard_map/ppermute | solution.py:610
  41.8 2.5 %copy-start = (bf16[12,2,3,36864]{3,1,2,0:T(2,128)(2,1)S(1)}, bf16[12,2,3,36864]{3,1,2,0:T(2,128)(2,1)}, u32[]{:S(2)}) copy-start(bf16[12,2,3,36864]{3,1,2,0:T(2,128)(2,1)} %param.22) | copy-start | bytes 15925252
  44.3 0.7 copy-start.7
  45.0 4.7 %copy-start.10 = (s32[68]{0:T(128)S(1)}, s32[68]{0:T(128)}, u32[]{:S(2)}) copy-start(s32[68]{0:T(128)} %slot_tables.1.tab_ref) | copy-start | bytes 820
  45.0 10.4 %copy-start.8 = (f32[24,16]{1,0:T(8,128)S(1)}, f32[24,16]{1,0:T(8,128)}, u32[]{:S(2)}) copy-start(f32[24,16]{1,0:T(8,128)} %get-tuple-element.86.coef_ref) | copy-start | bytes 4612
  50.9 11.8 %collective-permute-start.2 = (s16[4,288,128]{2,1,0:T(8,128)(2,1)S(1)}, s16[4,288,128]{2,1,0:T(8,128)(2,1)S(1)}, u32[]{:S(2)}, u32[]{:S(2)}) collective-permute-start(s16[4,288,128]{2,1,0:T(8,128)(2,1)S(1)} %get-tuple-element.91), channel_id=1, source_target_pairs={{0,4},{4,0},{8,12},{12,8},{16,20},{20,16},{24,28},{28,24},{1,5},{5... | collective-permute-start | bytes 884744 | tf_op jit(solution)/shard_map/ppermute | solution.py:610
  52.4 10.3 %collective-permute-start.3 = (s16[4,288,128]{2,1,0:T(8,128)(2,1)S(1)}, s16[4,288,128]{2,1,0:T(8,128)(2,1)S(1)}, u32[]{:S(2)}, u32[]{:S(2)}) collective-permute-start(s16[4,288,128]{2,1,0:T(8,128)(2,1)S(1)} %get-tuple-element.92), channel_id=1, source_target_pairs={{0,8},{4,12},{8,0},{12,4},{16,24},{20,28},{24,16},{28,20},{1,9},{5... | collective-permute-start | bytes 884744 | tf_op jit(solution)/shard_map/ppermute | solution.py:610
  52.4 15.7 %collective-permute-start.7 = (s16[4,288,128]{2,1,0:T(8,128)(2,1)S(1)}, s16[4,288,128]{2,1,0:T(8,128)(2,1)S(1)}, u32[]{:S(2)}, u32[]{:S(2)}) collective-permute-start(s16[4,288,128]{2,1,0:T(8,128)(2,1)S(1)} %get-tuple-element.104), channel_id=1, source_target_pairs={{0,12},{4,8},{8,4},{12,0},{16,28},{20,24},{24,20},{28,16},{1,13},{... | collective-permute-start | bytes 884744 | tf_op jit(solution)/shard_map/ppermute | solution.py:610
  60.4 2.3 %copy-start.5 = (f32[24,16,128]{2,1,0:T(8,128)}, f32[24,16,128]{2,1,0:T(8,128)S(1)}, u32[]{:S(2)}) copy-start(f32[24,16,128]{2,1,0:T(8,128)S(1)} %view_sums.2.refs_0_) | copy-start | bytes 589828
  64.0 10.6 %collective-permute-start.9 = (s16[4,288,128]{2,1,0:T(8,128)(2,1)S(1)}, s16[4,288,128]{2,1,0:T(8,128)(2,1)S(1)}, u32[]{:S(2)}, u32[]{:S(2)}) collective-permute-start(s16[4,288,128]{2,1,0:T(8,128)(2,1)S(1)} %get-tuple-element.109), channel_id=1, source_target_pairs={{0,4},{4,0},{8,12},{12,8},{16,20},{20,16},{24,28},{28,24},{1,5},{5... | collective-permute-start | bytes 884744 | tf_op jit(solution)/shard_map/ppermute | solution.py:610
  64.6 10.0 %collective-permute-start.10 = (s16[4,288,128]{2,1,0:T(8,128)(2,1)S(1)}, s16[4,288,128]{2,1,0:T(8,128)(2,1)S(1)}, u32[]{:S(2)}, u32[]{:S(2)}) collective-permute-start(s16[4,288,128]{2,1,0:T(8,128)(2,1)S(1)} %get-tuple-element.110), channel_id=1, source_target_pairs={{0,8},{4,12},{8,0},{12,4},{16,24},{20,28},{24,16},{28,20},{1,9},{5... | collective-permute-start | bytes 884744 | tf_op jit(solution)/shard_map/ppermute | solution.py:610
  68.8 9.2 %collective-permute-start.8 = (s16[4,288,128]{2,1,0:T(8,128)(2,1)S(1)}, s16[4,288,128]{2,1,0:T(8,128)(2,1)S(1)}, u32[]{:S(2)}, u32[]{:S(2)}) collective-permute-start(s16[4,288,128]{2,1,0:T(8,128)(2,1)S(1)} %depth_grads.5), channel_id=1, source_target_pairs={{0,12},{4,8},{8,4},{12,0},{16,28},{20,24},{24,20},{28,16},{1,13},{... | collective-permute-start | bytes 884744 | tf_op jit(solution)/shard_map/ppermute | solution.py:610
  73.9 0.7 copy-start.6
  78.0 28.3 %copy-start.4 = (f32[8,36864]{1,0:T(8,128)S(1)}, f32[8,36864]{1,0:T(8,128)}, u32[]{:S(2)}) copy-start(f32[8,36864]{1,0:T(8,128)} %s_ref.1) | copy-start | bytes 3538948
  79.3 27.0 %collective-permute-start.16 = (s16[8,288,128]{2,1,0:T(8,128)(2,1)S(1)}, s16[8,288,128]{2,1,0:T(8,128)(2,1)S(1)}, u32[]{:S(2)}, u32[]{:S(2)}) collective-permute-start(s16[8,288,128]{2,1,0:T(8,128)(2,1)S(1)} %fold_codes.1), channel_id=1, source_target_pairs={{0,16},{4,20},{8,24},{12,28},{16,0},{20,4},{24,8},{28,12},{1,17},{... | collective-permute-start | bytes 1769480 | tf_op jit(solution)/shard_map/ppermute | solution.py:610
  79.4 17.4 %collective-permute-start.13 = (s16[4,288,128]{2,1,0:T(8,128)(2,1)}, s16[4,288,128]{2,1,0:T(8,128)(2,1)S(1)}, u32[]{:S(2)}, u32[]{:S(2)}) collective-permute-start(s16[4,288,128]{2,1,0:T(8,128)(2,1)} %get-tuple-element.128), channel_id=1, source_target_pairs={{0,4},{4,0},{8,12},{12,8},{16,20},{20,16},{24,28},{28,24},{1,5},{5... | collective-permute-start | bytes 884744 | tf_op jit(solution)/shard_map/ppermute | solution.py:610
  81.5 16.9 %collective-permute-start.14 = (s16[4,288,128]{2,1,0:T(8,128)(2,1)}, s16[4,288,128]{2,1,0:T(8,128)(2,1)S(1)}, u32[]{:S(2)}, u32[]{:S(2)}) collective-permute-start(s16[4,288,128]{2,1,0:T(8,128)(2,1)} %get-tuple-element.129), channel_id=1, source_target_pairs={{0,8},{4,12},{8,0},{12,4},{16,24},{20,28},{24,16},{28,20},{1,9},{5... | collective-permute-start | bytes 884744 | tf_op jit(solution)/shard_map/ppermute | solution.py:610
  82.3 22.9 %collective-permute-start.15 = (s16[4,288,128]{2,1,0:T(8,128)(2,1)}, s16[4,288,128]{2,1,0:T(8,128)(2,1)S(1)}, u32[]{:S(2)}, u32[]{:S(2)}) collective-permute-start(s16[4,288,128]{2,1,0:T(8,128)(2,1)} %get-tuple-element.130), channel_id=1, source_target_pairs={{0,12},{4,8},{8,4},{12,0},{16,28},{20,24},{24,20},{28,16},{1,13},{... | collective-permute-start | bytes 884744 | tf_op jit(solution)/shard_map/ppermute | solution.py:610
  86.6 1.2 %collective-permute-start.11 = (f32[76,7]{0,1:T(8,128)S(1)}, f32[76,7]{0,1:T(8,128)S(1)}, u32[]{:S(2)}, u32[]{:S(2)}) collective-permute-start(f32[76,7]{0,1:T(8,128)S(1)} %copy.25), channel_id=1, source_target_pairs={{0,1},{1,0},{2,3},{3,2},{4,5},{5,4},{6,7},{7,6},{8,9},{9,8},{10,11... | collective-permute-start | bytes 6392 | tf_op jit(solution)/shard_map/ppermute | solution.py:668
  87.8 3.6 %collective-permute-start.12 = (f32[76,7]{0,1:T(8,128)S(1)}, f32[76,7]{0,1:T(8,128)S(1)}, u32[]{:S(2)}, u32[]{:S(2)}) collective-permute-start(f32[76,7]{0,1:T(8,128)S(1)} %add.11), channel_id=1, source_target_pairs={{0,2},{1,3},{2,0},{3,1},{4,6},{5,7},{6,4},{7,5},{8,10},{9,11},{10,... | collective-permute-start | bytes 6392 | tf_op jit(solution)/shard_map/ppermute | solution.py:668
  92.1 17.4 %all-to-all-start.1 = ((f32[8,8,7]{2,1,0:T(8,128)}), f32[8,8,7]{2,1,0:T(8,128)}, u32[]{:S(2)}, u32[]{:S(2)}) async-start(f32[8,8,7]{2,1,0:T(8,128)} %bitcast.35), calls=%async_computation.1 | async-start | bytes 65536 | tf_op jit(solution)/shard_map/all_to_all | solution.py:672
  96.8 9.5 %copy-start.1 = (f32[8,36864]{1,0:T(8,128)S(1)}, f32[8,36864]{1,0:T(8,128)}, u32[]{:S(2)}) copy-start(f32[8,36864]{1,0:T(8,128)} %x_ref.1) | copy-start | bytes 3538948
  96.8 9.5 %copy-start.3 = (f32[8,36864]{1,0:T(8,128)S(1)}, f32[8,36864]{1,0:T(8,128)}, u32[]{:S(2)}) copy-start(f32[8,36864]{1,0:T(8,128)} %m_ref.1) | copy-start | bytes 3538948
  (2 other events, 1.3 us)

commit v7 on v6

--- a/solution.py
+++ b/solution.py
@@ -98,6 +98,7 @@
     me = me_ref[0]
     shards = 2 * half
     spare = 2 * shards
+    mirror = half + half // 2
     requests = list_ref.shape[1]
 
     @pl.loop(0, (spare + 1) * cap, unroll=8)
@@ -118,9 +119,10 @@
         for k in range(half):
             image = list_ref[me ^ k, r]
             owner = over(image, images)
-            cell = jnp.where(owner == me, k, jnp.where(owner == (me ^ half), half + k, spare))
+            cell = jnp.where(owner == me, k, jnp.where(owner == (me ^ mirror), half + k, spare))
             put(cell, image - owner * images)
-        put(shards + (over(list_ref[me, r], images) ^ me), r)
+        away = over(list_ref[me, r], images) ^ me
+        put(shards + jnp.where(away < half, away, half + (away ^ mirror)), r)
 
 
 def slot_tables(me, lists, half, cap, images):
@@ -622,9 +624,10 @@
     codes = codes.reshape(images, rows, LANES)
     first = rows // 2
     parts = [codes[:, :first], codes[:, first:]]
-    letters, parts[1:] = tie((letters, parts[1:]))
     mail = lax.all_to_all(letters, "img", 0, 0, tiled=True)
-    far = [swap(part, half) for part in parts]
+    mail, parts = tie((mail, parts))
+    mirror = half + half // 2
+    far = [swap(part, mirror) for part in parts]
 
     lists = mail[:, images, :requests].astype(jnp.int32)
     table = slot_tables(me.reshape(1), lists, half, cap, images)
@@ -653,7 +656,7 @@
     last_back, totals = tie((back[-1:], totals))
     folded = [fold_codes(table, totals, last_back, slots, late, cap, far_bound)]
     folded, far_sums = tie((folded, far_sums))
-    far_codes = [swap(part, half) for part in folded]
+    far_codes = [swap(part, mirror) for part in folded]
     small = view_terms(names, cams, poses, [near_sums, far_sums], shards * images)
     near_grads, _ = tie((near_grads, totals))
     near_total = fold_totals(table, exchange(near_grads), 0, every, images, cap)

time: 111 us -> 108 us (0.973)
  waiting for transfers between devices: 32.8 us -> 20.8 us
  starting transfers between devices: 27.6 us -> 36.3 us
    all_to_all x1, waiting for transfers between devices: 14.6 us -> 4.41 us  [body(): mail = lax.all_to_all(letters, 'img', 0, 0, tiled=True)]
    ppermute x15, starting transfers between devices: 14.7 us -> 23.6 us  [swap(): return lax.ppermute(value, 'img', [(i, i ^ k) for i in range(shards)])]
    ppermute x15, waiting for transfers between devices: 15 us -> 13.1 us  [swap(): return lax.ppermute(value, 'img', [(i, i ^ k) for i in range(shards)])]
  transfers between devices with their start and end apart: 19 -> 19, of which waited for: 8 -> 6; matrix products, arithmetic and copies ran while one was open for 3% -> 6% of each run, Pallas kernels for 30% -> 31%
where the time goes in v7:
time: 108 us
  Pallas kernels  37.6 us (35%)
  starting transfers between devices  36.3 us (34%)
  waiting for transfers between devices  20.8 us (19%)
  local copies, waits for them, and re-layouts  9.83 us (9%)
  other arithmetic  2.12 us (2%)
    ppermute x15, starting transfers between devices, swap(): return lax.ppermute(value, 'img', [(i, i ^ k) for i in range(shards)])  23.6 us
    ppermute x15, waiting for transfers between devices, swap(): return lax.ppermute(value, 'img', [(i, i ^ k) for i in range(shards)])  13.1 us
    pallas_call x2, Pallas kernels, view_sums(): pl.pallas_call(functools.partial(sum_kernel, first, half, cap), out_shape...  9.89 us
    all_to_all x1, starting transfers between devices, body(): mail = lax.all_to_all(letters, 'img', 0, 0, tiled=True)  7.25 us
    unnamed x32, local copies, waits for them, and re-layouts  6.76 us
    pallas_call x1, Pallas kernels, prepare_views(): pl.pallas_call(prepare_kernel, out_shape=[jax.ShapeDtypeStruct((2 * pairs...  4.67 us
    all_to_all x1, waiting for transfers between devices, body(): mail = lax.all_to_all(letters, 'img', 0, 0, tiled=True)  4.41 us
    pallas_call x3, Pallas kernels, depth_grads(): pl.pallas_call(functools.partial(grad_kernel, first, ks, cap), out_shape=...  4.27 us
  transfers between devices with their start and end apart: 19, of which 6 were waited for; matrix products, arithmetic and copies ran while one was open for 6% of the time, Pallas kernels for 31%

profile of v7, /device:TPU:0, one launch (start us, length us, event | category | flops | bytes accessed | tf_op | source)
XLA Modules:
  0.0 107.5 jit_solution(17300975377548703706)
XLA Ops:
  0.6 1.3 %letters_of.1 = f32[8,9,128]{2,1,0:T(8,128)} custom-call(s32[2,12]{1,0:T(2,128)} %bitcast.39, f32[8,7]{1,0:T(8,128)} %refs_0_.1), custom_call_target="tpu_custom_call" | custom-call | flops 1 | bytes 1 | tf_op jit(solution)/shard_map/letters_of/pallas_call | solution.py:80
  2.0 7.3 %all-to-all-start = ((f32[8,9,128]{2,1,0:T(8,128)}), f32[8,9,128]{2,1,0:T(8,128)S(1)}, u32[]{:S(2)}, u32[]{:S(2)}) async-start(f32[8,9,128]{2,1,0:T(8,128)} %letters_of.1), calls=%async_computation | async-start | bytes 131072 | tf_op jit(solution)/shard_map/all_to_all | solution.py:627
  9.2 1.5 %fusion = s16[1,8,288,128]{3,1,2,0:T(8,128)(2,1)S(1)} fusion(f32[8,36864]{1,0:T(8,128)} %x_ref.1), kind=kLoop, calls=%fused_computation.1 | loop fusion | flops 1179648 | bytes 1769472
  11.7 4.4 %all-to-all-done.all_ref = f32[8,9,128]{2,1,0:T(8,128)S(1)} async-done(((f32[8,9,128]{2,1,0:T(8,128)}), f32[8,9,128]{2,1,0:T(8,128)S(1)}, u32[]{:S(2)}, u32[]{:S(2)}) %all-to-all-start) | async-done | bytes 36896 | tf_op jit(solution)/shard_map/all_to_all | solution.py:627
  16.7 3.3 %collective-permute-start.1 = (s16[8,144,128]{2,1,0:T(8,128)(2,1)}, s16[8,144,128]{2,1,0:T(8,128)(2,1)}, u32[]{:S(2)}, u32[]{:S(2)}) collective-permute-start(s16[8,144,128]{2,1,0:T(8,128)(2,1)} %get-tuple-element.87), channel_id=1, source_target_pairs={{0,24},{4,28},{8,16},{12,20},{16,8},{20,12},{24,0},{28,4},{1,25},{... | collective-permute-start | bytes 884744 | tf_op jit(solution)/shard_map/ppermute | solution.py:612
  20.6 2.3 %slot_tables.1.tab_ref = s32[68]{0:T(128)} custom-call(s32[1]{0:T(128)} %bitcast.1.me_ref, s32[8,24]{1,0:T(8,128)} %bitcast.37), custom_call_target="tpu_custom_call" | custom-call | flops 1 | bytes 1 | tf_op jit(solution)/shard_map/slot_tables/pallas_call | solution.py:129
  23.5 1.4 %pack_slots.2 = (s16[4,288,128]{2,1,0:T(8,128)(2,1)S(1)}, s16[4,288,128]{2,1,0:T(8,128)(2,1)}, s16[4,288,128]{2,1,0:T(8,128)(2,1)S(1)}, s16[4,288,128]{2,1,0:T(8,128)(2,1)S(1)}) custom-call(s32[68]{0:T(128)S(1)} %copy-done.9, s16[8,288,128]{2,1,0:T(8,128)(2,1)S(1)} %bitcast.33), custom_call_target="tpu_custom_call" | custom-call | flops 1 | bytes 1 | tf_op jit(solution)/shard_map/pack_slots/pallas_call | solution.py:156
  27.4 3.1 %collective-permute-start.6 = (s16[4,288,128]{2,1,0:T(8,128)(2,1)}, s16[4,288,128]{2,1,0:T(8,128)(2,1)S(1)}, u32[]{:S(2)}, u32[]{:S(2)}) collective-permute-start(s16[4,288,128]{2,1,0:T(8,128)(2,1)} %copy-done.11), channel_id=1, source_target_pairs={{0,12},{4,8},{8,4},{12,0},{16,28},{20,24},{24,20},{28,16},{1,13},{... | collective-permute-start | bytes 884744 | tf_op jit(solution)/shard_map/ppermute | solution.py:612
  30.5 1.9 %view_coefs.1 = (f32[24,16]{1,0:T(8,128)}, f32[24,7]{1,0:T(8,128)}, f32[24,7]{1,0:T(8,128)}) custom-call(s32[2,12]{1,0:T(2,128)} %bitcast.40, f32[8,9,128]{2,1,0:T(8,128)} %copy-done.13, f32[12,7]{1,0:T(8,128)} %copy.21.pair_ref), custom_call_target="tpu_custom_call" | custom-call | flops 1 | bytes 1 | tf_op jit(solution)/shard_map/view_coefs/pallas_call | solution.py:506
  32.4 2.5 %copy-done = bf16[12,2,3,36864]{3,1,2,0:T(2,128)(2,1)S(1)} copy-done((bf16[12,2,3,36864]{3,1,2,0:T(2,128)(2,1)S(1)}, bf16[12,2,3,36864]{3,1,2,0:T(2,128)(2,1)}, u32[]{:S(2)}) %copy-start) | copy-done | bytes 5308440
  35.7 4.7 %prepare_views.1 = (bf16[24,4,288,128]{3,2,1,0:T(8,128)(2,1)S(1)}, f32[24,2,288,128]{3,2,1,0:T(8,128)S(1)}) custom-call(f32[1]{0:T(128)} %bitcast.3.row_ref, f32[24,16]{1,0:T(8,128)S(1)} %copy-done.7, bf16[12,3,576,128]{3,2,1,0:T(8,128)(2,1)S(1)} %bitcast.31, bf16[12,576,128]{2,1,0:T(8,128)(2,1)S(1)} %bitcast.34), custom_call_target="tpu_custom_call" | custom-call | flops 1 | bytes 1 | tf_op jit(solution)/shard_map/prepare_views/pallas_call | solution.py:226
  40.4 1.2 %pack_slots.3 = (s16[4,288,128]{2,1,0:T(8,128)(2,1)S(1)}, s16[4,288,128]{2,1,0:T(8,128)(2,1)S(1)}, s16[4,288,128]{2,1,0:T(8,128)(2,1)S(1)}, s16[4,288,128]{2,1,0:T(8,128)(2,1)S(1)}) custom-call(s32[68]{0:T(128)S(1)} %copy-done.10, s16[8,144,128]{2,1,0:T(8,128)(2,1)S(1)} %collective-permute-done.refs_0_, s16[8,144,128]{2,1,0:T(8,128)(2,1)} %collective-permute-done.1.refs_1_), custom_call_target="tpu_custom_call" | custom-call | flops 1 | bytes 1 | tf_op jit(solution)/shard_map/pack_slots/pallas_call | solution.py:156
  42.0 3.5 %collective-permute-start.3 = (s16[4,288,128]{2,1,0:T(8,128)(2,1)S(1)}, s16[4,288,128]{2,1,0:T(8,128)(2,1)S(1)}, u32[]{:S(2)}, u32[]{:S(2)}) collective-permute-start(s16[4,288,128]{2,1,0:T(8,128)(2,1)S(1)} %get-tuple-element.94), channel_id=1, source_target_pairs={{0,8},{4,12},{8,0},{12,4},{16,24},{20,28},{24,16},{28,20},{1,9},{5... | collective-permute-start | bytes 884744 | tf_op jit(solution)/shard_map/ppermute | solution.py:612
  45.7 5.3 %view_sums.2.refs_0_ = f32[24,16,128]{2,1,0:T(8,128)S(1)} custom-call(s32[68]{0:T(128)S(1)} %copy-done.10, f32[24,16]{1,0:T(8,128)S(1)} %copy-done.8, f32[1]{0:T(128)} %bitcast.3.row_ref, bf16[24,4,288,128]{3,2,1,0:T(8,128)(2,1)S(1)} %get-tuple-element.95.view_ref, s16[4,288,128]{2,1,0:T(8,128)(2,1)S(1)} %get-tuple-element.96.refs_0_, ...), custom_call_target="tpu_custom_call" | custom-call | flops 1 | bytes 1 | tf_op jit(solution)/shard_map/view_sums/pallas_call | solution.py:327
  51.0 2.4 %depth_grads.3 = (s16[4,288,128]{2,1,0:T(8,128)(2,1)S(1)}, s16[4,288,128]{2,1,0:T(8,128)(2,1)}, s16[4,288,128]{2,1,0:T(8,128)(2,1)}, s16[4,288,128]{2,1,0:T(8,128)(2,1)}) custom-call(s32[68]{0:T(128)S(1)} %copy-done.10, f32[24,2,288,128]{3,2,1,0:T(8,128)S(1)} %get-tuple-element.100.slope_ref, s16[4,288,128]{2,1,0:T(8,128)(2,1)S(1)} %get-tuple-element.96.refs_0_, ...), custom_call_target="tpu_custom_call" | custom-call | flops 1 | bytes 1 | tf_op jit(solution)/shard_map/depth_grads/pallas_call | solution.py:265
  54.6 1.3 %collective-permute-start.9 = (s16[4,288,128]{2,1,0:T(8,128)(2,1)S(1)}, s16[4,288,128]{2,1,0:T(8,128)(2,1)S(1)}, u32[]{:S(2)}, u32[]{:S(2)}) collective-permute-start(s16[4,288,128]{2,1,0:T(8,128)(2,1)S(1)} %get-tuple-element.111), channel_id=1, source_target_pairs={{0,4},{4,0},{8,12},{12,8},{16,20},{20,16},{24,28},{28,24},{1,5},{5... | collective-permute-start | bytes 884744 | tf_op jit(solution)/shard_map/ppermute | solution.py:612
  55.8 1.8 %collective-permute-start.10 = (s16[4,288,128]{2,1,0:T(8,128)(2,1)S(1)}, s16[4,288,128]{2,1,0:T(8,128)(2,1)S(1)}, u32[]{:S(2)}, u32[]{:S(2)}) collective-permute-start(s16[4,288,128]{2,1,0:T(8,128)(2,1)S(1)} %get-tuple-element.112), channel_id=1, source_target_pairs={{0,8},{4,12},{8,0},{12,4},{16,24},{20,28},{24,16},{28,20},{1,9},{5... | collective-permute-start | bytes 884744 | tf_op jit(solution)/shard_map/ppermute | solution.py:612
  58.4 3.2 %collective-permute-start.8 = (s16[4,288,128]{2,1,0:T(8,128)(2,1)S(1)}, s16[4,288,128]{2,1,0:T(8,128)(2,1)S(1)}, u32[]{:S(2)}, u32[]{:S(2)}) collective-permute-start(s16[4,288,128]{2,1,0:T(8,128)(2,1)S(1)} %depth_grads.5), channel_id=1, source_target_pairs={{0,12},{4,8},{8,4},{12,0},{16,28},{20,24},{24,20},{28,16},{1,13},{... | collective-permute-start | bytes 884744 | tf_op jit(solution)/shard_map/ppermute | solution.py:612
  61.6 4.6 %view_sums.3.refs_1_ = f32[24,16,128]{2,1,0:T(8,128)S(1)} custom-call(s32[68]{0:T(128)S(1)} %copy-done.10, f32[24,16]{1,0:T(8,128)S(1)} %copy-done.8, f32[1]{0:T(128)} %bitcast.3.row_ref, bf16[24,4,288,128]{3,2,1,0:T(8,128)(2,1)S(1)} %get-tuple-element.95.view_ref, s16[4,288,128]{2,1,0:T(8,128)(2,1)S(1)} %get-tuple-element.114.refs_0_, ...), custom_call_target="tpu_custom_call" | custom-call | flops 1 | bytes 1 | tf_op jit(solution)/shard_map/view_sums/pallas_call | solution.py:327
  68.0 2.5 %collective-permute-done.8.refs_0_ = s16[4,288,128]{2,1,0:T(8,128)(2,1)S(1)} collective-permute-done((s16[4,288,128]{2,1,0:T(8,128)(2,1)S(1)}, s16[4,288,128]{2,1,0:T(8,128)(2,1)S(1)}, u32[]{:S(2)}, u32[]{:S(2)}) %collective-permute-start.8) | collective-permute-done | bytes 294944 | tf_op jit(solution)/shard_map/ppermute | solution.py:612
  70.5 1.3 %fold_codes.1 = s16[8,288,128]{2,1,0:T(8,128)(2,1)S(1)} custom-call(s32[68]{0:T(128)S(1)} %copy-done.10, f32[8,288,128]{2,1,0:T(8,128)S(1)} %fold_totals.2.total_ref, s16[4,288,128]{2,1,0:T(8,128)(2,1)S(1)} %collective-permute-done.8.refs_0_), custom_call_target="tpu_custom_call" | custom-call | flops 1 | bytes 1 | tf_op jit(solution)/shard_map/fold_codes/pallas_call | solution.py:381
  71.9 2.3 %collective-permute-start.16 = (s16[8,288,128]{2,1,0:T(8,128)(2,1)S(1)}, s16[8,288,128]{2,1,0:T(8,128)(2,1)S(1)}, u32[]{:S(2)}, u32[]{:S(2)}) collective-permute-start(s16[8,288,128]{2,1,0:T(8,128)(2,1)S(1)} %fold_codes.1), channel_id=1, source_target_pairs={{0,24},{4,28},{8,16},{12,20},{16,8},{20,12},{24,0},{28,4},{1,25},{... | collective-permute-start | bytes 1769480 | tf_op jit(solution)/shard_map/ppermute | solution.py:612
  75.4 2.3 %collective-permute-start.15 = (s16[4,288,128]{2,1,0:T(8,128)(2,1)}, s16[4,288,128]{2,1,0:T(8,128)(2,1)S(1)}, u32[]{:S(2)}, u32[]{:S(2)}) collective-permute-start(s16[4,288,128]{2,1,0:T(8,128)(2,1)} %get-tuple-element.132), channel_id=1, source_target_pairs={{0,12},{4,8},{8,4},{12,0},{16,28},{20,24},{24,20},{28,16},{1,13},{... | collective-permute-start | bytes 884744 | tf_op jit(solution)/shard_map/ppermute | solution.py:612
  77.7 2.7 %view_terms.1 = f32[76,7]{1,0:T(8,128)} custom-call(s32[2,12]{1,0:T(2,128)} %bitcast.41, f32[24,7]{1,0:T(8,128)} %get-tuple-element.84.cam_ref, f32[24,7]{1,0:T(8,128)} %get-tuple-element.85.pose_ref, f32[24,16,128]{2,1,0:T(8,128)} %copy-done.5, f32[24,16,128]{2,1,0:T(8,128)} %copy-done.6), custom_call_target="tpu_custom_call" | custom-call | flops 1 | bytes 1 | tf_op jit(solution)/shard_map/view_terms/pallas_call | solution.py:554
  81.2 1.2 %collective-permute-done.11 = f32[76,7]{0,1:T(8,128)S(1)} collective-permute-done((f32[76,7]{0,1:T(8,128)S(1)}, f32[76,7]{0,1:T(8,128)S(1)}, u32[]{:S(2)}, u32[]{:S(2)}) %collective-permute-start.11) | collective-permute-done | bytes 2160 | tf_op jit(solution)/shard_map/ppermute | solution.py:671
  82.4 1.5 %collective-permute-start.12 = (f32[76,7]{0,1:T(8,128)S(1)}, f32[76,7]{0,1:T(8,128)S(1)}, u32[]{:S(2)}, u32[]{:S(2)}) collective-permute-start(f32[76,7]{0,1:T(8,128)S(1)} %add.11), channel_id=1, source_target_pairs={{0,2},{1,3},{2,0},{3,1},{4,6},{5,7},{6,4},{7,5},{8,10},{9,11},{10,... | collective-permute-start | bytes 6392 | tf_op jit(solution)/shard_map/ppermute | solution.py:671
  83.9 2.1 %collective-permute-done.12 = f32[76,7]{0,1:T(8,128)S(1)} collective-permute-done((f32[76,7]{0,1:T(8,128)S(1)}, f32[76,7]{0,1:T(8,128)S(1)}, u32[]{:S(2)}, u32[]{:S(2)}) %collective-permute-start.12) | collective-permute-done | bytes 2160 | tf_op jit(solution)/shard_map/ppermute | solution.py:671
  86.7 4.0 %all-to-all-start.1 = ((f32[8,8,7]{2,1,0:T(8,128)}), f32[8,8,7]{2,1,0:T(8,128)}, u32[]{:S(2)}, u32[]{:S(2)}) async-start(f32[8,8,7]{2,1,0:T(8,128)} %bitcast.35), calls=%async_computation.1 | async-start | bytes 65536 | tf_op jit(solution)/shard_map/all_to_all | solution.py:675
  91.3 3.1 %collective-permute-done.14.refs_2_ = s16[4,288,128]{2,1,0:T(8,128)(2,1)S(1)} collective-permute-done((s16[4,288,128]{2,1,0:T(8,128)(2,1)}, s16[4,288,128]{2,1,0:T(8,128)(2,1)S(1)}, u32[]{:S(2)}, u32[]{:S(2)}) %collective-permute-start.14) | collective-permute-done | bytes 294944 | tf_op jit(solution)/shard_map/ppermute | solution.py:612
  94.4 7.5 %collective-permute-done.15.refs_3_ = s16[4,288,128]{2,1,0:T(8,128)(2,1)S(1)} collective-permute-done((s16[4,288,128]{2,1,0:T(8,128)(2,1)}, s16[4,288,128]{2,1,0:T(8,128)(2,1)S(1)}, u32[]{:S(2)}, u32[]{:S(2)}) %collective-permute-start.15) | collective-permute-done | bytes 294944 | tf_op jit(solution)/shard_map/ppermute | solution.py:612
  103.0 3.1 %update_depths.1 = (f32[8,36864]{1,0:T(8,128)}, f32[8,36864]{1,0:T(8,128)}, f32[8,36864]{1,0:T(8,128)}) custom-call(f32[8,288,128]{2,1,0:T(8,128)S(1)} %fold_totals.3.local_ref, s16[8,288,128]{2,1,0:T(8,128)(2,1)S(1)} %collective-permute-done.16.far_ref, f32[8,36864]{1,0:T(8,128)S(1)} %copy-done.1, f32[8,36864]{1,0:T(8,128)S(1)} %copy-done.3, ...), custom_call_target="tpu_custom_call" | custom-call | flops 1 | bytes 1 | tf_op jit(solution)/shard_map/update_depths/pallas_call | solution.py:424
  106.1 1.4 %update_small.1 = (f32[8,7]{1,0:T(8,128)}, f32[8,7]{1,0:T(8,128)}, f32[8,7]{1,0:T(8,128)}, f32[7,12]{1,0:T(8,128)}, f32[7,12]{1,0:T(8,128)}, /*index=5*/f32[7,12]{1,0:T(8,128)}) custom-call(f32[8,8,7]{2,1,0:T(8,128)} %all-to-all-done.1.mail_ref, f32[7,12]{1,0:T(8,128)} %slice_bitcast_fusion.pose_ref, f32[8,7]{1,0:T(8,128)} %refs_0_.1, f32[8,7]{1,0:T(8,128)} %refs_1_.1, ...), custom_call_target="tpu_custom_call" | custom-call | flops 1 | bytes 1 | tf_op jit(solution)/shard_map/update_small/pallas_call | solution.py:576
  (63 shorter events, 14.8 us)
Async XLA Ops:
  2.0 14.2 %all-to-all-start = ((f32[8,9,128]{2,1,0:T(8,128)}), f32[8,9,128]{2,1,0:T(8,128)S(1)}, u32[]{:S(2)}, u32[]{:S(2)}) async-start(f32[8,9,128]{2,1,0:T(8,128)} %letters_of.1), calls=%async_computation | async-start | bytes 131072 | tf_op jit(solution)/shard_map/all_to_all | solution.py:627
  10.8 16.0 %copy-start.14 = (f32[12,7]{0,1:T(8,128)S(1)}, f32[12,7]{0,1:T(8,128)}, u32[]{:S(2)}) copy-start(f32[12,7]{0,1:T(8,128)} %param.19) | copy-start | bytes 1012
  10.9 21.6 %copy-start.2 = (bf16[12,2,36864]{2,1,0:T(2,128)(2,1)S(1)}, bf16[12,2,36864]{2,1,0:T(2,128)(2,1)}, u32[]{:S(2)}) copy-start(bf16[12,2,36864]{2,1,0:T(2,128)(2,1)} %param.23) | copy-start | bytes 5308420
  16.1 4.4 %copy-start.13 = (f32[8,9,128]{2,1,0:T(8,128)}, f32[8,9,128]{2,1,0:T(8,128)S(1)}, u32[]{:S(2)}) copy-start(f32[8,9,128]{2,1,0:T(8,128)S(1)} %all-to-all-done.all_ref) | copy-start | bytes 110596
  16.1 24.2 %collective-permute-start = (s16[8,144,128]{2,1,0:T(8,128)(2,1)}, s16[8,144,128]{2,1,0:T(8,128)(2,1)S(1)}, u32[]{:S(2)}, u32[]{:S(2)}) collective-permute-start(s16[8,144,128]{2,1,0:T(8,128)(2,1)} %get-tuple-element.86), channel_id=1, source_target_pairs={{0,24},{4,28},{8,16},{12,20},{16,8},{20,12},{24,0},{28,4},{1,25},{... | collective-permute-start | bytes 884744 | tf_op jit(solution)/shard_map/ppermute | solution.py:612
  16.7 23.6 %collective-permute-start.1 = (s16[8,144,128]{2,1,0:T(8,128)(2,1)}, s16[8,144,128]{2,1,0:T(8,128)(2,1)}, u32[]{:S(2)}, u32[]{:S(2)}) collective-permute-start(s16[8,144,128]{2,1,0:T(8,128)(2,1)} %get-tuple-element.87), channel_id=1, source_target_pairs={{0,24},{4,28},{8,16},{12,20},{16,8},{20,12},{24,0},{28,4},{1,25},{... | collective-permute-start | bytes 884744 | tf_op jit(solution)/shard_map/ppermute | solution.py:612
  24.9 0.7 copy-start.11
  25.7 0.7 copy-start.12
  26.4 19.1 %collective-permute-start.4 = (s16[4,288,128]{2,1,0:T(8,128)(2,1)}, s16[4,288,128]{2,1,0:T(8,128)(2,1)S(1)}, u32[]{:S(2)}, u32[]{:S(2)}) collective-permute-start(s16[4,288,128]{2,1,0:T(8,128)(2,1)} %get-tuple-element.97), channel_id=1, source_target_pairs={{0,4},{4,0},{8,12},{12,8},{16,20},{20,16},{24,28},{28,24},{1,5},{5... | collective-permute-start | bytes 884744 | tf_op jit(solution)/shard_map/ppermute | solution.py:612
  27.4 18.3 %collective-permute-start.5 = (s16[4,288,128]{2,1,0:T(8,128)(2,1)}, s16[4,288,128]{2,1,0:T(8,128)(2,1)S(1)}, u32[]{:S(2)}, u32[]{:S(2)}) collective-permute-start(s16[4,288,128]{2,1,0:T(8,128)(2,1)} %copy-done.12), channel_id=1, source_target_pairs={{0,8},{4,12},{8,0},{12,4},{16,24},{20,28},{24,16},{28,20},{1,9},{5... | collective-permute-start | bytes 884744 | tf_op jit(solution)/shard_map/ppermute | solution.py:612
  27.4 18.3 %collective-permute-start.6 = (s16[4,288,128]{2,1,0:T(8,128)(2,1)}, s16[4,288,128]{2,1,0:T(8,128)(2,1)S(1)}, u32[]{:S(2)}, u32[]{:S(2)}) collective-permute-start(s16[4,288,128]{2,1,0:T(8,128)(2,1)} %copy-done.11), channel_id=1, source_target_pairs={{0,12},{4,8},{8,4},{12,0},{16,28},{20,24},{24,20},{28,16},{1,13},{... | collective-permute-start | bytes 884744 | tf_op jit(solution)/shard_map/ppermute | solution.py:612
  32.4 2.5 %copy-start = (bf16[12,2,3,36864]{3,1,2,0:T(2,128)(2,1)S(1)}, bf16[12,2,3,36864]{3,1,2,0:T(2,128)(2,1)}, u32[]{:S(2)}) copy-start(bf16[12,2,3,36864]{3,1,2,0:T(2,128)(2,1)} %param.22) | copy-start | bytes 15925252
  35.0 0.7 copy-start.7
  35.7 4.7 %copy-start.10 = (s32[68]{0:T(128)S(1)}, s32[68]{0:T(128)}, u32[]{:S(2)}) copy-start(s32[68]{0:T(128)} %slot_tables.1.tab_ref) | copy-start | bytes 820
  35.7 10.1 %copy-start.8 = (f32[24,16]{1,0:T(8,128)S(1)}, f32[24,16]{1,0:T(8,128)}, u32[]{:S(2)}) copy-start(f32[24,16]{1,0:T(8,128)} %get-tuple-element.88.coef_ref) | copy-start | bytes 4612
  41.6 11.8 %collective-permute-start.2 = (s16[4,288,128]{2,1,0:T(8,128)(2,1)S(1)}, s16[4,288,128]{2,1,0:T(8,128)(2,1)S(1)}, u32[]{:S(2)}, u32[]{:S(2)}) collective-permute-start(s16[4,288,128]{2,1,0:T(8,128)(2,1)S(1)} %get-tuple-element.93), channel_id=1, source_target_pairs={{0,4},{4,0},{8,12},{12,8},{16,20},{20,16},{24,28},{28,24},{1,5},{5... | collective-permute-start | bytes 884744 | tf_op jit(solution)/shard_map/ppermute | solution.py:612
  42.0 11.4 %collective-permute-start.3 = (s16[4,288,128]{2,1,0:T(8,128)(2,1)S(1)}, s16[4,288,128]{2,1,0:T(8,128)(2,1)S(1)}, u32[]{:S(2)}, u32[]{:S(2)}) collective-permute-start(s16[4,288,128]{2,1,0:T(8,128)(2,1)S(1)} %get-tuple-element.94), channel_id=1, source_target_pairs={{0,8},{4,12},{8,0},{12,4},{16,24},{20,28},{24,16},{28,20},{1,9},{5... | collective-permute-start | bytes 884744 | tf_op jit(solution)/shard_map/ppermute | solution.py:612
  45.5 12.1 %collective-permute-start.7 = (s16[4,288,128]{2,1,0:T(8,128)(2,1)S(1)}, s16[4,288,128]{2,1,0:T(8,128)(2,1)S(1)}, u32[]{:S(2)}, u32[]{:S(2)}) collective-permute-start(s16[4,288,128]{2,1,0:T(8,128)(2,1)S(1)} %get-tuple-element.106), channel_id=1, source_target_pairs={{0,12},{4,8},{8,4},{12,0},{16,28},{20,24},{24,20},{28,16},{1,13},{... | collective-permute-start | bytes 884744 | tf_op jit(solution)/shard_map/ppermute | solution.py:612
  51.0 2.4 %copy-start.5 = (f32[24,16,128]{2,1,0:T(8,128)}, f32[24,16,128]{2,1,0:T(8,128)S(1)}, u32[]{:S(2)}) copy-start(f32[24,16,128]{2,1,0:T(8,128)S(1)} %view_sums.2.refs_0_) | copy-start | bytes 589828
  54.6 12.4 %collective-permute-start.9 = (s16[4,288,128]{2,1,0:T(8,128)(2,1)S(1)}, s16[4,288,128]{2,1,0:T(8,128)(2,1)S(1)}, u32[]{:S(2)}, u32[]{:S(2)}) collective-permute-start(s16[4,288,128]{2,1,0:T(8,128)(2,1)S(1)} %get-tuple-element.111), channel_id=1, source_target_pairs={{0,4},{4,0},{8,12},{12,8},{16,20},{20,16},{24,28},{28,24},{1,5},{5... | collective-permute-start | bytes 884744 | tf_op jit(solution)/shard_map/ppermute | solution.py:612
  55.8 11.1 %collective-permute-start.10 = (s16[4,288,128]{2,1,0:T(8,128)(2,1)S(1)}, s16[4,288,128]{2,1,0:T(8,128)(2,1)S(1)}, u32[]{:S(2)}, u32[]{:S(2)}) collective-permute-start(s16[4,288,128]{2,1,0:T(8,128)(2,1)S(1)} %get-tuple-element.112), channel_id=1, source_target_pairs={{0,8},{4,12},{8,0},{12,4},{16,24},{20,28},{24,16},{28,20},{1,9},{5... | collective-permute-start | bytes 884744 | tf_op jit(solution)/shard_map/ppermute | solution.py:612
  58.4 12.1 %collective-permute-start.8 = (s16[4,288,128]{2,1,0:T(8,128)(2,1)S(1)}, s16[4,288,128]{2,1,0:T(8,128)(2,1)S(1)}, u32[]{:S(2)}, u32[]{:S(2)}) collective-permute-start(s16[4,288,128]{2,1,0:T(8,128)(2,1)S(1)} %depth_grads.5), channel_id=1, source_target_pairs={{0,12},{4,8},{8,4},{12,0},{16,28},{20,24},{24,20},{28,16},{1,13},{... | collective-permute-start | bytes 884744 | tf_op jit(solution)/shard_map/ppermute | solution.py:612
  70.5 32.5 %copy-start.4 = (f32[8,36864]{1,0:T(8,128)S(1)}, f32[8,36864]{1,0:T(8,128)}, u32[]{:S(2)}) copy-start(f32[8,36864]{1,0:T(8,128)} %s_ref.1) | copy-start | bytes 3538948
  71.9 31.1 %collective-permute-start.16 = (s16[8,288,128]{2,1,0:T(8,128)(2,1)S(1)}, s16[8,288,128]{2,1,0:T(8,128)(2,1)S(1)}, u32[]{:S(2)}, u32[]{:S(2)}) collective-permute-start(s16[8,288,128]{2,1,0:T(8,128)(2,1)S(1)} %fold_codes.1), channel_id=1, source_target_pairs={{0,24},{4,28},{8,16},{12,20},{16,8},{20,12},{24,0},{28,4},{1,25},{... | collective-permute-start | bytes 1769480 | tf_op jit(solution)/shard_map/ppermute | solution.py:612
  74.2 17.2 %collective-permute-start.13 = (s16[4,288,128]{2,1,0:T(8,128)(2,1)}, s16[4,288,128]{2,1,0:T(8,128)(2,1)S(1)}, u32[]{:S(2)}, u32[]{:S(2)}) collective-permute-start(s16[4,288,128]{2,1,0:T(8,128)(2,1)} %get-tuple-element.130), channel_id=1, source_target_pairs={{0,4},{4,0},{8,12},{12,8},{16,20},{20,16},{24,28},{28,24},{1,5},{5... | collective-permute-start | bytes 884744 | tf_op jit(solution)/shard_map/ppermute | solution.py:612
  74.5 19.9 %collective-permute-start.14 = (s16[4,288,128]{2,1,0:T(8,128)(2,1)}, s16[4,288,128]{2,1,0:T(8,128)(2,1)S(1)}, u32[]{:S(2)}, u32[]{:S(2)}) collective-permute-start(s16[4,288,128]{2,1,0:T(8,128)(2,1)} %get-tuple-element.131), channel_id=1, source_target_pairs={{0,8},{4,12},{8,0},{12,4},{16,24},{20,28},{24,16},{28,20},{1,9},{5... | collective-permute-start | bytes 884744 | tf_op jit(solution)/shard_map/ppermute | solution.py:612
  75.4 26.5 %collective-permute-start.15 = (s16[4,288,128]{2,1,0:T(8,128)(2,1)}, s16[4,288,128]{2,1,0:T(8,128)(2,1)S(1)}, u32[]{:S(2)}, u32[]{:S(2)}) collective-permute-start(s16[4,288,128]{2,1,0:T(8,128)(2,1)} %get-tuple-element.132), channel_id=1, source_target_pairs={{0,12},{4,8},{8,4},{12,0},{16,28},{20,24},{24,20},{28,16},{1,13},{... | collective-permute-start | bytes 884744 | tf_op jit(solution)/shard_map/ppermute | solution.py:612
  81.2 1.2 %collective-permute-start.11 = (f32[76,7]{0,1:T(8,128)S(1)}, f32[76,7]{0,1:T(8,128)S(1)}, u32[]{:S(2)}, u32[]{:S(2)}) collective-permute-start(f32[76,7]{0,1:T(8,128)S(1)} %copy.25), channel_id=1, source_target_pairs={{0,1},{1,0},{2,3},{3,2},{4,5},{5,4},{6,7},{7,6},{8,9},{9,8},{10,11... | collective-permute-start | bytes 6392 | tf_op jit(solution)/shard_map/ppermute | solution.py:671
  82.4 3.6 %collective-permute-start.12 = (f32[76,7]{0,1:T(8,128)S(1)}, f32[76,7]{0,1:T(8,128)S(1)}, u32[]{:S(2)}, u32[]{:S(2)}) collective-permute-start(f32[76,7]{0,1:T(8,128)S(1)} %add.11), channel_id=1, source_target_pairs={{0,2},{1,3},{2,0},{3,1},{4,6},{5,7},{6,4},{7,5},{8,10},{9,11},{10,... | collective-permute-start | bytes 6392 | tf_op jit(solution)/shard_map/ppermute | solution.py:671
  86.7 19.4 %all-to-all-start.1 = ((f32[8,8,7]{2,1,0:T(8,128)}), f32[8,8,7]{2,1,0:T(8,128)}, u32[]{:S(2)}, u32[]{:S(2)}) async-start(f32[8,8,7]{2,1,0:T(8,128)} %bitcast.35), calls=%async_computation.1 | async-start | bytes 65536 | tf_op jit(solution)/shard_map/all_to_all | solution.py:675
  91.3 11.6 %copy-start.1 = (f32[8,36864]{1,0:T(8,128)S(1)}, f32[8,36864]{1,0:T(8,128)}, u32[]{:S(2)}) copy-start(f32[8,36864]{1,0:T(8,128)} %x_ref.1) | copy-start | bytes 3538948
  91.3 11.6 %copy-start.3 = (f32[8,36864]{1,0:T(8,128)S(1)}, f32[8,36864]{1,0:T(8,128)}, u32[]{:S(2)}) copy-start(f32[8,36864]{1,0:T(8,128)} %m_ref.1) | copy-start | bytes 3538948
  (2 other events, 1.3 us)
